TPU v7x, 128 devices: a whole 4x4x4 slice. The times are simulated.
128 devices in a mesh: gx: 8 (over z, core), gy: 16 (over y, x).
Axes of the slice: x: 4, y: 4, z: 4, core: 2. Of those that a mesh axis runs over, the one named last changes fastest.
Arguments:
- charges: float32 [128, 256, 1024], P('gx', 'gy'), may hold values from -6 to 6
- kernel_taps: float32 [4, 3, 9], replicated, may hold values from 0.05 to 0.6
Outputs:
- potential: float32 [128, 256, 1024], P('gx', 'gy')
All inputs are finite; a program needn't handle non-finite values.
Results may differ from a plain program's by a relative error of at most 0.00018.
Values sent between devices are 32-bit elements; how exact they have to be, the bound alone decides.
No kernel may reach another device: no remote copies, remote signals or barrier semaphores. Data moves between devices by JAX's collectives and lax.ppermute only.
A program may use at most 128 MiB of HBM per device.

v0:
```python
import jax
import jax.numpy as jnp
from jax import lax
from jax.sharding import PartitionSpec as P

stencil_weights = ((-3, -0.0625), (-1, 0.5625), (0, 1.0), (1, 0.5625), (3, -0.0625))


def with_halo(cells, sides, width):
    for axis, dim in sides:
        count = lax.axis_size(axis)
        head = lax.slice_in_dim(cells, 0, width, axis=dim)
        tail = lax.slice_in_dim(cells, cells.shape[dim] - width, cells.shape[dim], axis=dim)
        cells = jnp.concatenate(
            [
                lax.ppermute(tail, axis, [(i, (i + 1) % count) for i in range(count)]),
                cells,
                lax.ppermute(head, axis, [((i + 1) % count, i) for i in range(count)]),
            ],
            axis=dim,
        )
    return cells


def convolve_along(values, kernel, along):
    summed = kernel[0] * jnp.roll(values, 4, along)
    for tap_index in range(1, 9):
        summed = summed + kernel[tap_index] * jnp.roll(values, 4 - tap_index, along)
    return summed


def convolve_three(values, kernel_rows):
    values = convolve_along(values, kernel_rows[0], 0)
    values = convolve_along(values, kernel_rows[1], 1)
    return convolve_along(values, kernel_rows[2], 2)


def restrict_along(values, along):
    length = values.shape[along]
    summed = None
    for offset, weight in stencil_weights:
        shifted = lax.slice_in_dim(jnp.roll(values, -offset, along), 0, length, 2, along)
        summed = weight * shifted if summed is None else summed + weight * shifted
    return summed


def prolong_padded(padded, along):
    length = padded.shape[along] - 4
    centre = lax.slice_in_dim(padded, 2, 2 + length, 1, along)
    right = lax.slice_in_dim(padded, 3, 3 + length, 1, along)
    left = lax.slice_in_dim(padded, 1, 1 + length, 1, along)
    farther = lax.slice_in_dim(padded, 4, 4 + length, 1, along)
    odd_cells = 0.5625 * (centre + right) - 0.0625 * (left + farther)
    stacked = jnp.stack([centre, odd_cells], axis=along + 1)
    new_shape = list(centre.shape)
    new_shape[along] = 2 * length
    return stacked.reshape(new_shape)


def prolong_along(values, along):
    widths = [(2, 2) if dim_index == along else (0, 0) for dim_index in range(3)]
    return prolong_padded(jnp.pad(values, widths, mode="wrap"), along)


def prolong_brick(padded):
    return prolong_along(prolong_padded(prolong_padded(padded, 0), 1), 2)


def convolve_valid(padded, kernel, along, length):
    summed = kernel[0] * lax.slice_in_dim(padded, 0, length, 1, along)
    for tap_index in range(1, 9):
        summed = summed + kernel[tap_index] * lax.slice_in_dim(
            padded, tap_index, tap_index + length, 1, along
        )
    return summed


def restrict_valid(padded, along, margin, length):
    half_length = length // 2
    summed = None
    for offset, weight in stencil_weights:
        begin = margin + offset
        shifted = lax.slice_in_dim(padded, begin, begin + 2 * half_length - 1, 2, along)
        summed = weight * shifted if summed is None else summed + weight * shifted
    return summed


def level_step(charge_grid, kernel_rows, factor):
    rows_x, rows_y = (charge_grid.shape[0], charge_grid.shape[1])
    padded_x = with_halo(charge_grid, (("gx", 0),), 4)
    smoothed = convolve_valid(padded_x, kernel_rows[0], 0, rows_x)
    padded_y = with_halo(smoothed, (("gy", 1),), 4)
    smoothed = convolve_valid(padded_y, kernel_rows[1], 1, rows_y)
    rimmed = with_halo(charge_grid, (("gx", 0), ("gy", 1)), 3)
    coarser = restrict_valid(restrict_valid(rimmed, 0, 3, rows_x), 1, 3, rows_y)
    potential_part = factor * convolve_along(smoothed, kernel_rows[2], 2)
    return (potential_part, restrict_along(coarser, 2))


def arrange_whole(stacked, count_x, count_y):
    brick_rows_x, brick_rows_y, depth_cells = (stacked.shape[1], stacked.shape[2], stacked.shape[3])
    grid_blocks = stacked.reshape(count_x, count_y, brick_rows_x, brick_rows_y, depth_cells)
    grid_blocks = jnp.transpose(grid_blocks, (0, 2, 1, 3, 4))
    return grid_blocks.reshape(count_x * brick_rows_x, count_y * brick_rows_y, depth_cells)


def per_device(charges, kernel_taps):
    brick_x = lax.axis_index("gx")
    brick_y = lax.axis_index("gy")
    count_x = lax.axis_size("gx")
    count_y = lax.axis_size("gy")
    bricked_levels = 3
    potentials = []
    charge_grid = charges
    for section_index in range(bricked_levels):
        potential_part, charge_grid = level_step(
            charge_grid, kernel_taps[section_index], 0.5**section_index
        )
        potentials.append(potential_part)
    gathered = lax.all_gather(charge_grid[None], ("gx", "gy"), axis=0, tiled=True)
    entire = arrange_whole(gathered, count_x, count_y)
    coarsest = 0.5**3 * convolve_three(entire, kernel_taps[3])
    rows_x, rows_y = (charge_grid.shape[0], charge_grid.shape[1])
    wrapped = jnp.pad(coarsest, ((2, 2), (2, 2), (0, 0)), mode="wrap")
    window = lax.dynamic_slice(
        wrapped,
        (brick_x * rows_x, brick_y * rows_y, jnp.int32(0)),
        (rows_x + 4, rows_y + 4, coarsest.shape[2]),
    )
    running = potentials[-1] + prolong_brick(window)
    for section_index in reversed(range(bricked_levels - 1)):
        rimmed = with_halo(running, (("gx", 0), ("gy", 1)), 2)
        running = potentials[section_index] + prolong_brick(rimmed)
    return running


def solution(mesh):
    placed = (P("gx", "gy", None), P())
    return jax.shard_map(
        per_device, mesh=mesh, in_specs=placed, out_specs=P("gx", "gy", None), check_vma=False
    )
```

profile of v0, /device:TPU:30, one launch (start us, length us, event | category | flops | bytes accessed | tf_op | source)
XLA Modules:
  0.0 291.9 jit_solution(2112111977702537539)
XLA Ops:
  1.2 3.5 %collective-permute-start.1 = (f32[4,16,1024]{2,1,0:T(8,128)S(1)}, f32[4,16,1024]{2,1,0:T(8,128)S(1)}, u32[]{:S(2)}, u32[]{:S(2)}) collective-permute-start(f32[4,16,1024]{2,1,0:T(8,128)S(1)} %get-tuple-element.30), channel_id=1, source_target_pairs={{16,0},{32,16},{48,32},{64,48},{80,64},{96,80},{112,96},{0,112},{1... | collective-permute-start | bytes 786440 | tf_op jit(solution)/shard_map/ppermute | solution.py:18
  5.8 2.9 %collective-permute-start.5 = (f32[3,16,1024]{2,1,0:T(8,128)S(1)}, f32[3,16,1024]{2,1,0:T(8,128)S(1)}, u32[]{:S(2)}, u32[]{:S(2)}) collective-permute-start(f32[3,16,1024]{2,1,0:T(8,128)S(1)} %get-tuple-element.31), channel_id=1, source_target_pairs={{16,0},{32,16},{48,32},{64,48},{80,64},{96,80},{112,96},{0,112},{1... | collective-permute-start | bytes 589832 | tf_op jit(solution)/shard_map/ppermute | solution.py:18
  13.5 6.1 %fusion.22 = (f32[16,16,1024]{2,1,0:T(8,128)S(1)}, f32[22,16,1024]{2,1,0:T(8,128)S(1)}) fusion(f32[20,16,1024]{2,1,0:T(8,128)S(1)} %constant_dynamic-update-slice_fusion.2, f32[20,16,1024]{2,1,0:T(8,128)S(1)} %get-tuple-element.27, f32[16,16,1024]{2,1,0:T(8,128)S(1)} %copy-done, f32[]{:T(128)} %bitcast.10, f32[]{:T(128)} %bitcast.9, f32[]{:T(128)} %bitcast.8, ...), kind=kLoop, calls=%fused_computation.38 | loop fusion | flops 4456448 | bytes 11534372 | tf_op jit(solution)/shard_map/add | solution.py:72
  22.5 3.5 %collective-permute-start.6 = (f32[22,3,1024]{2,0,1:T(8,128)S(1)}, f32[22,3,1024]{2,0,1:T(8,128)S(1)}, u32[]{:S(2)}, u32[]{:S(2)}) collective-permute-start(f32[22,3,1024]{2,0,1:T(8,128)S(1)} %copy.768), channel_id=1, source_target_pairs={{0,1},{1,2},{2,3},{3,4},{4,5},{5,6},{6,7},{7,8},{8,9},{9,10},{10,1... | collective-permute-start | bytes 811016 | tf_op jit(solution)/shard_map/ppermute | solution.py:16
  30.7 7.4 %fusion.3 = f32[16,16,1024]{2,1,0:T(8,128)S(1)} fusion(f32[16,16,1024]{2,1,0:T(8,128)S(1)} %get-tuple-element.25, f32[16,4,1024]{2,1,0:T(4,128)S(1)} %copy.724, f32[16,4,1024]{2,1,0:T(4,128)S(1)} %copy.722, f32[]{:T(128)} %bitcast.18, f32[]{:T(128)} %bitcast.17, f32[]{:T(128)} %bitcast.16, f32[]{:T(128)} %bitcast.15, f32[]{:T(128)} %bitcast.14, f32[]{:T(128)} %bitcast.13, ...), kind=kLoop, calls=%fused_computation.16 | loop fusion | flops 6553600 | bytes 2621476 | tf_op jit(solution)/shard_map/add | solution.py:72
  48.2 4.5 %slice.1716 = f32[8,8,512]{2,1,0:T(8,128)S(1)} slice(f32[8,8,1024]{2,1,0:T(8,128)S(1)} %multiply_add_fusion.1), slice={[0:8:1], [0:8:1], [0:1024:2]} | slice | bytes 262144 | tf_op jit(solution)/shard_map/slice | solution.py:42
  52.8 4.5 %slice.1715 = f32[8,8,512]{2,1,0:T(8,128)S(1)} slice(f32[8,8,1024]{2,1,0:T(8,128)S(1)} %get-tuple-element.289), slice={[0:8:1], [0:8:1], [0:1024:2]} | slice | bytes 262144 | tf_op jit(solution)/shard_map/slice | solution.py:42
  57.3 4.5 %slice.1719 = f32[8,8,512]{2,1,0:T(8,128)S(1)} slice(f32[8,8,1024]{2,1,0:T(8,128)S(1)} %get-tuple-element.290), slice={[0:8:1], [0:8:1], [0:1024:2]} | slice | bytes 262144 | tf_op jit(solution)/shard_map/slice | solution.py:42
  61.9 4.5 %slice.1712 = f32[8,8,512]{2,1,0:T(8,128)S(1)} slice(f32[8,8,1024]{2,1,0:T(8,128)S(1)} %get-tuple-element.287), slice={[0:8:1], [0:8:1], [0:1024:2]} | slice | bytes 262144 | tf_op jit(solution)/shard_map/slice | solution.py:42
  66.4 5.0 %slice.1722 = f32[8,8,512]{2,1,0:T(8,128)S(1)} slice(f32[8,8,1024]{2,1,0:T(8,128)S(1)} %get-tuple-element.288), slice={[0:8:1], [0:8:1], [0:1024:2]} | slice | bytes 262144 | tf_op jit(solution)/shard_map/slice | solution.py:42
  71.6 2.9 %collective-permute-start.13 = (f32[3,8,512]{2,1,0:T(8,128)S(1)}, f32[3,8,512]{2,1,0:T(8,128)S(1)}, u32[]{:S(2)}, u32[]{:S(2)}) collective-permute-start(f32[3,8,512]{2,1,0:T(8,128)S(1)} %get-tuple-element.126), channel_id=1, source_target_pairs={{16,0},{32,16},{48,32},{64,48},{80,64},{96,80},{112,96},{0,112},{1... | collective-permute-start | bytes 147464 | tf_op jit(solution)/shard_map/ppermute | solution.py:18
  74.6 2.9 %collective-permute-start.9 = (f32[4,8,512]{2,1,0:T(8,128)S(1)}, f32[4,8,512]{2,1,0:T(8,128)S(1)}, u32[]{:S(2)}, u32[]{:S(2)}) collective-permute-start(f32[4,8,512]{2,1,0:T(8,128)S(1)} %get-tuple-element.124), channel_id=1, source_target_pairs={{16,0},{32,16},{48,32},{64,48},{80,64},{96,80},{112,96},{0,112},{1... | collective-permute-start | bytes 196616 | tf_op jit(solution)/shard_map/ppermute | solution.py:18
  79.4 5.5 %fusion.82 = f32[8,8,512]{2,1,0:T(8,128)S(1)} fusion(f32[8,8,512]{2,1,0:T(8,128)S(1)} %multiply_add_fusion.3, f32[4,8,512]{2,1,0:T(8,128)S(1)} %collective-permute-done.9, f32[4,8,512]{2,1,0:T(8,128)S(1)} %collective-permute-done.8, f32[]{:T(128)} %bitcast.37, f32[]{:T(128)} %bitcast.36, f32[]{:T(128)} %bitcast.35, f32[]{:T(128)} %bitcast.34, f32[]{:T(128)} %bitcast.33, ...), kind=kLoop, calls=%fused_computation.193 | loop fusion | flops 819200 | bytes 393252 | tf_op jit(solution)/shard_map/add | solution.py:72
  87.3 5.0 %collective-permute-start.14 = (f32[14,3,512]{2,0,1:T(8,128)S(1)}, f32[14,3,512]{2,0,1:T(8,128)S(1)}, u32[]{:S(2)}, u32[]{:S(2)}) collective-permute-start(f32[14,3,512]{2,0,1:T(8,128)S(1)} %copy.733), channel_id=1, source_target_pairs={{0,1},{1,2},{2,3},{3,4},{4,5},{5,6},{6,7},{7,8},{8,9},{9,10},{10,1... | collective-permute-start | bytes 258056 | tf_op jit(solution)/shard_map/ppermute | solution.py:16
  94.4 5.8 %fusion.102 = f32[8,8,512]{2,1,0:T(8,128)S(1)} fusion(f32[8,8,512]{2,1,0:T(8,128)S(1)} %fusion.82, f32[8,4,512]{2,1,0:T(4,128)S(1)} %copy.732, f32[8,4,512]{2,1,0:T(4,128)S(1)} %copy.730, f32[]{:T(128)} %bitcast.45, f32[]{:T(128)} %bitcast.44, f32[]{:T(128)} %bitcast.43, f32[]{:T(128)} %bitcast.42, f32[]{:T(128)} %bitcast.41, f32[]{:T(128)} %bitcast.40, ...), kind=kLoop, calls=%fused_computation.213 | loop fusion | flops 819200 | bytes 393252 | tf_op jit(solution)/shard_map/add | solution.py:72
  108.3 2.9 %collective-permute-start.21 = (f32[3,4,256]{2,1,0:T(4,128)S(1)}, f32[3,4,256]{2,1,0:T(4,128)S(1)}, u32[]{:S(2)}, u32[]{:S(2)}) collective-permute-start(f32[3,4,256]{2,1,0:T(4,128)S(1)} %get-tuple-element.166), channel_id=1, source_target_pairs={{16,0},{32,16},{48,32},{64,48},{80,64},{96,80},{112,96},{0,112},{1... | collective-permute-start | bytes 36872 | tf_op jit(solution)/shard_map/ppermute | solution.py:18
  111.9 3.0 %collective-permute-start.17 = (f32[4,4,256]{2,1,0:T(4,128)S(1)}, f32[4,4,256]{2,1,0:T(4,128)S(1)}, u32[]{:S(2)}, u32[]{:S(2)}) collective-permute-start(f32[4,4,256]{2,1,0:T(4,128)S(1)} %multiply_add_fusion.7), channel_id=1, source_target_pairs={{16,0},{32,16},{48,32},{64,48},{80,64},{96,80},{112,96},{0,112},{1... | collective-permute-start | bytes 49160 | tf_op jit(solution)/shard_map/ppermute | solution.py:18
  116.3 5.6 %fusion.160 = f32[4,4,256]{2,1,0:T(4,128)S(1)} fusion(f32[4,4,256]{2,1,0:T(4,128)S(1)} %multiply_add_fusion.7, f32[4,4,256]{2,1,0:T(4,128)S(1)} %collective-permute-done.17, f32[4,4,256]{2,1,0:T(4,128)S(1)} %collective-permute-done.16, f32[]{:T(128)} %bitcast.64, f32[]{:T(128)} %bitcast.63, f32[]{:T(128)} %bitcast.62, f32[]{:T(128)} %bitcast.61, ...), kind=kLoop, calls=%fused_computation.326 | loop fusion | flops 94208 | bytes 65572 | tf_op jit(solution)/shard_map/add | solution.py:72
  121.9 3.5 %collective-permute-start.18 = (f32[4,4,256]{2,1,0:T(4,128)S(1)}, f32[4,4,256]{2,1,0:T(4,128)S(1)}, u32[]{:S(2)}, u32[]{:S(2)}) collective-permute-start(f32[4,4,256]{2,1,0:T(4,128)S(1)} %fusion.160), channel_id=1, source_target_pairs={{0,1},{1,2},{2,3},{3,4},{4,5},{5,6},{6,7},{7,8},{8,9},{9,10},{10,1... | collective-permute-start | bytes 49160 | tf_op jit(solution)/shard_map/ppermute | solution.py:16
  125.5 5.4 %collective-permute-start.22 = (f32[10,3,256]{2,1,0:T(4,128)S(1)}, f32[10,3,256]{2,1,0:T(4,128)S(1)}, u32[]{:S(2)}, u32[]{:S(2)}) collective-permute-start(f32[10,3,256]{2,1,0:T(4,128)S(1)} %get-tuple-element.133), channel_id=1, source_target_pairs={{0,1},{1,2},{2,3},{3,4},{4,5},{5,6},{6,7},{7,8},{8,9},{9,10},{10,1... | collective-permute-start | bytes 92168 | tf_op jit(solution)/shard_map/ppermute | solution.py:16
  132.5 5.6 %fusion.176 = f32[4,4,256]{2,1,0:T(4,128)S(1)} fusion(f32[4,4,256]{2,1,0:T(4,128)S(1)} %fusion.160, f32[4,4,256]{2,1,0:T(4,128)S(1)} %collective-permute-done.19, f32[4,4,256]{2,1,0:T(4,128)S(1)} %collective-permute-done.18, f32[]{:T(128)} %bitcast.72, f32[]{:T(128)} %bitcast.71, f32[]{:T(128)} %bitcast.70, f32[]{:T(128)} %bitcast.69, f32[]{:T(128)} %bitcast.68, ...), kind=kLoop, calls=%fused_computation.342 | loop fusion | flops 94208 | bytes 65572 | tf_op jit(solution)/shard_map/add | solution.py:72
  140.7 60.3 %all-gather = f32[256,2,128]{2,1,0:T(2,128)S(1)} all-gather(f32[2,2,128]{2,1,0:T(2,128)S(1)} %multiply_add_fusion.9), channel_id=2, replica_groups=mesh['gx'=8,'gy'=16] {'gx','gy'}, dimensions={0}, use_global_device_ids=true | all-gather | bytes 264192 | tf_op jit(solution)/shard_map/all_gather | solution.py:120
  201.6 5.8 %fusion.61 = f32[16,32,128]{2,1,0:T(8,128)S(1)} fusion(f32[12,32,128]{2,1,0:T(8,128)S(1)} %bitcast.190, f32[4,32,128]{2,1,0:T(8,128)S(1)} %bitcast.193, f32[13,32,128]{2,1,0:T(8,128)S(1)} %get-tuple-element.78, f32[3,32,128]{2,1,0:T(8,128)S(1)} %get-tuple-element.80, f32[14,32,128]{2,1,0:T(8,128)S(1)} %bitcast.188, f32[2,32,128]{2,1,0:T(8,128)S(1)} %bitcast.198, ...), kind=kLoop, calls=%fused_computation.138 | loop fusion | flops 1638400 | bytes 2621476 | tf_op jit(solution)/shard_map/add | solution.py:28
  207.6 6.0 %fusion.69 = f32[16,32,128]{2,1,0:T(8,128)S(1)} fusion(f32[16,28,128]{2,1,0:T(8,128)S(1)} %get-tuple-element.58, f32[16,4,128]{2,1,0:T(4,128)S(1)} %get-tuple-element.60, f32[16,29,128]{2,1,0:T(8,128)S(1)} %get-tuple-element.62, f32[16,3,128]{2,1,0:T(4,128)S(1)} %get-tuple-element.64, f32[16,30,128]{2,1,0:T(8,128)S(1)} %get-tuple-element.66, ...), kind=kLoop, calls=%fused_computation.154 | loop fusion | flops 1638400 | bytes 2621476 | tf_op jit(solution)/shard_map/add | solution.py:28
  214.8 6.3 %fusion.78 = f32[16,32,128]{2,1,0:T(8,128)S(1)} fusion(f32[16,32,124]{2,1,0:T(8,128)S(1)} %get-tuple-element.42, f32[16,32,4]{2,1,0:T(8,128)S(1)} %get-tuple-element.44, f32[16,32,125]{2,1,0:T(8,128)S(1)} %get-tuple-element.46, f32[16,32,3]{2,1,0:T(8,128)S(1)} %get-tuple-element.48, f32[16,32,126]{2,1,0:T(8,128)S(1)} %get-tuple-element.50, ...), kind=kLoop, calls=%fused_computation.171 | loop fusion | flops 1703936 | bytes 2621476 | tf_op jit(solution)/shard_map/mul | solution.py:122
  221.9 5.7 %multiply_add_fusion.6 = f32[4,4,256]{2,1,0:T(4,128)S(1)} fusion(f32[4,4,256]{2,1,0:T(4,128)S(1)} %copy.746, f32[4,4,4]{2,1,0:T(4,128)S(1)} %get-tuple-element.150, f32[4,4,252]{2,1,0:T(4,128)S(1)} %get-tuple-element.152, f32[4,4,3]{2,1,0:T(4,128)S(1)} %get-tuple-element.154, f32[4,4,253]{2,1,0:T(4,128)S(1)} %get-tuple-element.156, ...), kind=kLoop, calls=%fused_computation.389 | loop fusion | flops 110592 | bytes 180260 | tf_op jit(solution)/shard_map/add | solution.py:130
  236.2 5.6 %collective-permute-done.27 = f32[8,2,256]{2,0,1:T(8,128)S(1)} collective-permute-done((f32[8,2,256]{2,0,1:T(8,128)S(1)}, f32[8,2,256]{2,0,1:T(8,128)S(1)}, u32[]{:S(2)}, u32[]{:S(2)}) %collective-permute-start.27) | collective-permute-done | bytes 16416 | tf_op jit(solution)/shard_map/ppermute | solution.py:18
  246.3 7.3 %fusion.132 = f32[8,8,512]{2,1,0:T(8,128)S(1)} fusion(f32[8,8,512]{2,1,0:T(8,128)} %copy.758, f32[8,8,508]{2,1,0:T(8,128)} %get-tuple-element.106, f32[8,8,4]{2,1,0:T(8,128)} %get-tuple-element.108, f32[8,8,509]{2,1,0:T(8,128)} %get-tuple-element.110, f32[8,8,3]{2,1,0:T(8,128)} %get-tuple-element.112, f32[8,8,510]{2,1,0:T(8,128)} %get-tuple-element.114, ...), kind=kLoop, calls=%fused_computation.248 | loop fusion | flops 884736 | bytes 1441828 | tf_op jit(solution)/shard_map/add | solution.py:133
  262.4 3.6 %collective-permute-done.31 = f32[12,2,512]{2,1,0:T(2,128)S(1)} collective-permute-done((f32[12,2,512]{2,1,0:T(2,128)S(1)}, f32[12,2,512]{2,1,0:T(2,128)S(1)}, u32[]{:S(2)}, u32[]{:S(2)}) %collective-permute-start.31) | collective-permute-done | bytes 49184 | tf_op jit(solution)/shard_map/ppermute | solution.py:18
  267.7 7.5 %copy.764 = f32[16,16,512,2]{1,0,3,2:T(8,128)} copy(f32[16,16,512,2]{2,0,1,3:T(8,128)S(1)} %pad_maximum_fusion.3) | data formatting | bytes 2097152 | tf_op jit(solution)/shard_map/stack | solution.py:54
  275.2 5.2 %copy.765 = f32[16,16,1024]{2,1,0:T(8,128)S(1)} copy(f32[16,16,1024]{1,0,2:T(8,128)} %bitcast.168) | data formatting | bytes 2097152 | tf_op jit(solution)/shard_map/reshape | solution.py:57
  280.5 11.2 %fusion.38 = f32[16,16,1024]{2,1,0:T(8,128)} fusion(f32[16,16,1024]{2,1,0:T(8,128)S(1)} %copy.765, f32[16,16,1020]{2,1,0:T(8,128)} %get-tuple-element.8, f32[16,16,4]{2,1,0:T(8,128)S(1)} %get-tuple-element.10, f32[16,16,1021]{2,1,0:T(8,128)} %get-tuple-element.12, f32[16,16,3]{2,1,0:T(8,128)} %get-tuple-element.14, f32[16,16,1022]{2,1,0:T(8,128)} %get-tuple-element.16, ...), kind=kLoop, calls=%fused_computation.62 | loop fusion | flops 6815744 | bytes 11534372 | tf_op jit(solution)/shard_map/add | solution.py:133
  (251 shorter events, 71.6 us)
Async XLA Ops:
  1.2 11.9 %collective-permute-start = (f32[4,16,1024]{2,1,0:T(8,128)S(1)}, f32[4,16,1024]{2,1,0:T(8,128)S(1)}, u32[]{:S(2)}, u32[]{:S(2)}) collective-permute-start(f32[4,16,1024]{2,1,0:T(8,128)S(1)} %get-tuple-element.29), channel_id=1, source_target_pairs={{0,16},{16,32},{32,48},{48,64},{64,80},{80,96},{96,112},{112,0},{1... | collective-permute-start | bytes 786440 | tf_op jit(solution)/shard_map/ppermute | solution.py:16
  1.2 12.2 %collective-permute-start.1 = (f32[4,16,1024]{2,1,0:T(8,128)S(1)}, f32[4,16,1024]{2,1,0:T(8,128)S(1)}, u32[]{:S(2)}, u32[]{:S(2)}) collective-permute-start(f32[4,16,1024]{2,1,0:T(8,128)S(1)} %get-tuple-element.30), channel_id=1, source_target_pairs={{16,0},{32,16},{48,32},{64,48},{80,64},{96,80},{112,96},{0,112},{1... | collective-permute-start | bytes 786440 | tf_op jit(solution)/shard_map/ppermute | solution.py:18
  5.7 7.3 %collective-permute-start.4 = (f32[3,16,1024]{2,1,0:T(8,128)S(1)}, f32[3,16,1024]{2,1,0:T(8,128)S(1)}, u32[]{:S(2)}, u32[]{:S(2)}) collective-permute-start(f32[3,16,1024]{2,1,0:T(8,128)S(1)} %get-tuple-element.32), channel_id=1, source_target_pairs={{0,16},{16,32},{32,48},{48,64},{64,80},{80,96},{96,112},{112,0},{1... | collective-permute-start | bytes 589832 | tf_op jit(solution)/shard_map/ppermute | solution.py:16
  5.8 16.4 %collective-permute-start.5 = (f32[3,16,1024]{2,1,0:T(8,128)S(1)}, f32[3,16,1024]{2,1,0:T(8,128)S(1)}, u32[]{:S(2)}, u32[]{:S(2)}) collective-permute-start(f32[3,16,1024]{2,1,0:T(8,128)S(1)} %get-tuple-element.31), channel_id=1, source_target_pairs={{16,0},{32,16},{48,32},{64,48},{80,64},{96,80},{112,96},{0,112},{1... | collective-permute-start | bytes 589832 | tf_op jit(solution)/shard_map/ppermute | solution.py:18
  19.8 9.0 %collective-permute-start.2 = (f32[16,4,1024]{2,0,1:T(8,128)S(1)}, f32[16,4,1024]{2,0,1:T(8,128)S(1)}, u32[]{:S(2)}, u32[]{:S(2)}) collective-permute-start(f32[16,4,1024]{2,0,1:T(8,128)S(1)} %copy.721), channel_id=1, source_target_pairs={{0,1},{1,2},{2,3},{3,4},{4,5},{5,6},{6,7},{7,8},{8,9},{9,10},{10,1... | collective-permute-start | bytes 786440 | tf_op jit(solution)/shard_map/ppermute | solution.py:16
  20.2 10.3 %collective-permute-start.3 = (f32[16,4,1024]{2,0,1:T(8,128)S(1)}, f32[16,4,1024]{2,0,1:T(8,128)S(1)}, u32[]{:S(2)}, u32[]{:S(2)}) collective-permute-start(f32[16,4,1024]{2,0,1:T(8,128)S(1)} %copy.723), channel_id=1, source_target_pairs={{1,0},{2,1},{3,2},{4,3},{5,4},{6,5},{7,6},{8,7},{9,8},{10,9},{11,1... | collective-permute-start | bytes 786440 | tf_op jit(solution)/shard_map/ppermute | solution.py:18
  22.5 23.2 %collective-permute-start.6 = (f32[22,3,1024]{2,0,1:T(8,128)S(1)}, f32[22,3,1024]{2,0,1:T(8,128)S(1)}, u32[]{:S(2)}, u32[]{:S(2)}) collective-permute-start(f32[22,3,1024]{2,0,1:T(8,128)S(1)} %copy.768), channel_id=1, source_target_pairs={{0,1},{1,2},{2,3},{3,4},{4,5},{5,6},{6,7},{7,8},{8,9},{9,10},{10,1... | collective-permute-start | bytes 811016 | tf_op jit(solution)/shard_map/ppermute | solution.py:16
  26.2 19.7 %collective-permute-start.7 = (f32[22,3,1024]{2,0,1:T(8,128)S(1)}, f32[22,3,1024]{2,0,1:T(8,128)S(1)}, u32[]{:S(2)}, u32[]{:S(2)}) collective-permute-start(f32[22,3,1024]{2,0,1:T(8,128)S(1)} %copy.769), channel_id=1, source_target_pairs={{1,0},{2,1},{3,2},{4,3},{5,4},{6,5},{7,6},{8,7},{9,8},{10,9},{11,1... | collective-permute-start | bytes 811016 | tf_op jit(solution)/shard_map/ppermute | solution.py:18
  71.5 6.0 %collective-permute-start.12 = (f32[3,8,512]{2,1,0:T(8,128)S(1)}, f32[3,8,512]{2,1,0:T(8,128)S(1)}, u32[]{:S(2)}, u32[]{:S(2)}) collective-permute-start(f32[3,8,512]{2,1,0:T(8,128)S(1)} %get-tuple-element.125), channel_id=1, source_target_pairs={{0,16},{16,32},{32,48},{48,64},{64,80},{80,96},{96,112},{112,0},{1... | collective-permute-start | bytes 147464 | tf_op jit(solution)/shard_map/ppermute | solution.py:16
  71.6 5.9 %collective-permute-start.13 = (f32[3,8,512]{2,1,0:T(8,128)S(1)}, f32[3,8,512]{2,1,0:T(8,128)S(1)}, u32[]{:S(2)}, u32[]{:S(2)}) collective-permute-start(f32[3,8,512]{2,1,0:T(8,128)S(1)} %get-tuple-element.126), channel_id=1, source_target_pairs={{16,0},{32,16},{48,32},{64,48},{80,64},{96,80},{112,96},{0,112},{1... | collective-permute-start | bytes 147464 | tf_op jit(solution)/shard_map/ppermute | solution.py:18
  74.5 4.9 %collective-permute-start.8 = (f32[4,8,512]{2,1,0:T(8,128)S(1)}, f32[4,8,512]{2,1,0:T(8,128)S(1)}, u32[]{:S(2)}, u32[]{:S(2)}) collective-permute-start(f32[4,8,512]{2,1,0:T(8,128)S(1)} %get-tuple-element.123), channel_id=1, source_target_pairs={{0,16},{16,32},{32,48},{48,64},{64,80},{80,96},{96,112},{112,0},{1... | collective-permute-start | bytes 196616 | tf_op jit(solution)/shard_map/ppermute | solution.py:16
  74.6 4.9 %collective-permute-start.9 = (f32[4,8,512]{2,1,0:T(8,128)S(1)}, f32[4,8,512]{2,1,0:T(8,128)S(1)}, u32[]{:S(2)}, u32[]{:S(2)}) collective-permute-start(f32[4,8,512]{2,1,0:T(8,128)S(1)} %get-tuple-element.124), channel_id=1, source_target_pairs={{16,0},{32,16},{48,32},{64,48},{80,64},{96,80},{112,96},{0,112},{1... | collective-permute-start | bytes 196616 | tf_op jit(solution)/shard_map/ppermute | solution.py:18
  85.0 7.4 %collective-permute-start.10 = (f32[8,4,512]{2,0,1:T(8,128)S(1)}, f32[8,4,512]{2,0,1:T(8,128)S(1)}, u32[]{:S(2)}, u32[]{:S(2)}) collective-permute-start(f32[8,4,512]{2,0,1:T(8,128)S(1)} %copy.729), channel_id=1, source_target_pairs={{0,1},{1,2},{2,3},{3,4},{4,5},{5,6},{6,7},{7,8},{8,9},{9,10},{10,1... | collective-permute-start | bytes 196616 | tf_op jit(solution)/shard_map/ppermute | solution.py:16
  86.7 7.7 %collective-permute-start.11 = (f32[8,4,512]{2,0,1:T(8,128)S(1)}, f32[8,4,512]{2,0,1:T(8,128)S(1)}, u32[]{:S(2)}, u32[]{:S(2)}) collective-permute-start(f32[8,4,512]{2,0,1:T(8,128)S(1)} %copy.731), channel_id=1, source_target_pairs={{1,0},{2,1},{3,2},{4,3},{5,4},{6,5},{7,6},{8,7},{9,8},{10,9},{11,1... | collective-permute-start | bytes 196616 | tf_op jit(solution)/shard_map/ppermute | solution.py:18
  87.3 16.7 %collective-permute-start.14 = (f32[14,3,512]{2,0,1:T(8,128)S(1)}, f32[14,3,512]{2,0,1:T(8,128)S(1)}, u32[]{:S(2)}, u32[]{:S(2)}) collective-permute-start(f32[14,3,512]{2,0,1:T(8,128)S(1)} %copy.733), channel_id=1, source_target_pairs={{0,1},{1,2},{2,3},{3,4},{4,5},{5,6},{6,7},{7,8},{8,9},{9,10},{10,1... | collective-permute-start | bytes 258056 | tf_op jit(solution)/shard_map/ppermute | solution.py:16
  92.3 11.7 %collective-permute-start.15 = (f32[14,3,512]{2,0,1:T(8,128)S(1)}, f32[14,3,512]{2,0,1:T(8,128)S(1)}, u32[]{:S(2)}, u32[]{:S(2)}) collective-permute-start(f32[14,3,512]{2,0,1:T(8,128)S(1)} %copy.734), channel_id=1, source_target_pairs={{1,0},{2,1},{3,2},{4,3},{5,4},{6,5},{7,6},{8,7},{9,8},{10,9},{11,1... | collective-permute-start | bytes 258056 | tf_op jit(solution)/shard_map/ppermute | solution.py:18
  108.3 6.6 %collective-permute-start.20 = (f32[3,4,256]{2,1,0:T(4,128)S(1)}, f32[3,4,256]{2,1,0:T(4,128)S(1)}, u32[]{:S(2)}, u32[]{:S(2)}) collective-permute-start(f32[3,4,256]{2,1,0:T(4,128)S(1)} %get-tuple-element.165), channel_id=1, source_target_pairs={{0,16},{16,32},{32,48},{48,64},{64,80},{80,96},{96,112},{112,0},{1... | collective-permute-start | bytes 36872 | tf_op jit(solution)/shard_map/ppermute | solution.py:16
  108.3 6.6 %collective-permute-start.21 = (f32[3,4,256]{2,1,0:T(4,128)S(1)}, f32[3,4,256]{2,1,0:T(4,128)S(1)}, u32[]{:S(2)}, u32[]{:S(2)}) collective-permute-start(f32[3,4,256]{2,1,0:T(4,128)S(1)} %get-tuple-element.166), channel_id=1, source_target_pairs={{16,0},{32,16},{48,32},{64,48},{80,64},{96,80},{112,96},{0,112},{1... | collective-permute-start | bytes 36872 | tf_op jit(solution)/shard_map/ppermute | solution.py:18
  111.9 4.4 %collective-permute-start.16 = (f32[4,4,256]{2,1,0:T(4,128)S(1)}, f32[4,4,256]{2,1,0:T(4,128)S(1)}, u32[]{:S(2)}, u32[]{:S(2)}) collective-permute-start(f32[4,4,256]{2,1,0:T(4,128)S(1)} %multiply_add_fusion.7), channel_id=1, source_target_pairs={{0,16},{16,32},{32,48},{48,64},{64,80},{80,96},{96,112},{112,0},{1... | collective-permute-start | bytes 49160 | tf_op jit(solution)/shard_map/ppermute | solution.py:16
  111.9 4.4 %collective-permute-start.17 = (f32[4,4,256]{2,1,0:T(4,128)S(1)}, f32[4,4,256]{2,1,0:T(4,128)S(1)}, u32[]{:S(2)}, u32[]{:S(2)}) collective-permute-start(f32[4,4,256]{2,1,0:T(4,128)S(1)} %multiply_add_fusion.7), channel_id=1, source_target_pairs={{16,0},{32,16},{48,32},{64,48},{80,64},{96,80},{112,96},{0,112},{1... | collective-permute-start | bytes 49160 | tf_op jit(solution)/shard_map/ppermute | solution.py:18
  121.9 8.9 %collective-permute-start.18 = (f32[4,4,256]{2,1,0:T(4,128)S(1)}, f32[4,4,256]{2,1,0:T(4,128)S(1)}, u32[]{:S(2)}, u32[]{:S(2)}) collective-permute-start(f32[4,4,256]{2,1,0:T(4,128)S(1)} %fusion.160), channel_id=1, source_target_pairs={{0,1},{1,2},{2,3},{3,4},{4,5},{5,6},{6,7},{7,8},{8,9},{9,10},{10,1... | collective-permute-start | bytes 49160 | tf_op jit(solution)/shard_map/ppermute | solution.py:16
  125.4 7.1 %collective-permute-start.19 = (f32[4,4,256]{2,1,0:T(4,128)S(1)}, f32[4,4,256]{2,1,0:T(4,128)S(1)}, u32[]{:S(2)}, u32[]{:S(2)}) collective-permute-start(f32[4,4,256]{2,1,0:T(4,128)S(1)} %fusion.160), channel_id=1, source_target_pairs={{1,0},{2,1},{3,2},{4,3},{5,4},{6,5},{7,6},{8,7},{9,8},{10,9},{11,1... | collective-permute-start | bytes 49160 | tf_op jit(solution)/shard_map/ppermute | solution.py:18
  125.5 13.2 %collective-permute-start.22 = (f32[10,3,256]{2,1,0:T(4,128)S(1)}, f32[10,3,256]{2,1,0:T(4,128)S(1)}, u32[]{:S(2)}, u32[]{:S(2)}) collective-permute-start(f32[10,3,256]{2,1,0:T(4,128)S(1)} %get-tuple-element.133), channel_id=1, source_target_pairs={{0,1},{1,2},{2,3},{3,4},{4,5},{5,6},{6,7},{7,8},{8,9},{9,10},{10,1... | collective-permute-start | bytes 92168 | tf_op jit(solution)/shard_map/ppermute | solution.py:16
  130.9 7.8 %collective-permute-start.23 = (f32[10,3,256]{2,1,0:T(4,128)S(1)}, f32[10,3,256]{2,1,0:T(4,128)S(1)}, u32[]{:S(2)}, u32[]{:S(2)}) collective-permute-start(f32[10,3,256]{2,1,0:T(4,128)S(1)} %get-tuple-element.134), channel_id=1, source_target_pairs={{1,0},{2,1},{3,2},{4,3},{5,4},{6,5},{7,6},{8,7},{9,8},{10,9},{11,1... | collective-permute-start | bytes 92168 | tf_op jit(solution)/shard_map/ppermute | solution.py:18
  227.6 4.3 %collective-permute-start.24 = (f32[2,4,256]{2,1,0:T(4,128)S(1)}, f32[2,4,256]{2,1,0:T(4,128)S(1)}, u32[]{:S(2)}, u32[]{:S(2)}) collective-permute-start(f32[2,4,256]{2,1,0:T(4,128)S(1)} %get-tuple-element.147), channel_id=1, source_target_pairs={{0,16},{16,32},{32,48},{48,64},{64,80},{80,96},{96,112},{112,0},{1... | collective-permute-start | bytes 24584 | tf_op jit(solution)/shard_map/ppermute | solution.py:16
  227.6 4.3 %collective-permute-start.25 = (f32[2,4,256]{2,1,0:T(4,128)S(1)}, f32[2,4,256]{2,1,0:T(4,128)S(1)}, u32[]{:S(2)}, u32[]{:S(2)}) collective-permute-start(f32[2,4,256]{2,1,0:T(4,128)S(1)} %get-tuple-element.148), channel_id=1, source_target_pairs={{16,0},{32,16},{48,32},{64,48},{80,64},{96,80},{112,96},{0,112},{1... | collective-permute-start | bytes 24584 | tf_op jit(solution)/shard_map/ppermute | solution.py:18
  232.0 4.2 %collective-permute-start.26 = (f32[8,2,256]{2,0,1:T(8,128)S(1)}, f32[8,2,256]{2,0,1:T(8,128)S(1)}, u32[]{:S(2)}, u32[]{:S(2)}) collective-permute-start(f32[8,2,256]{2,0,1:T(8,128)S(1)} %copy.747), channel_id=1, source_target_pairs={{0,1},{1,2},{2,3},{3,4},{4,5},{5,6},{6,7},{7,8},{8,9},{9,10},{10,1... | collective-permute-start | bytes 49160 | tf_op jit(solution)/shard_map/ppermute | solution.py:16
  234.7 7.1 %collective-permute-start.27 = (f32[8,2,256]{2,0,1:T(8,128)S(1)}, f32[8,2,256]{2,0,1:T(8,128)S(1)}, u32[]{:S(2)}, u32[]{:S(2)}) collective-permute-start(f32[8,2,256]{2,0,1:T(8,128)S(1)} %copy.748), channel_id=1, source_target_pairs={{1,0},{2,1},{3,2},{4,3},{5,4},{6,5},{7,6},{8,7},{9,8},{10,9},{11,1... | collective-permute-start | bytes 49160 | tf_op jit(solution)/shard_map/ppermute | solution.py:18
  253.6 4.6 %collective-permute-start.28 = (f32[2,8,512]{2,1,0:T(8,128)S(1)}, f32[2,8,512]{2,1,0:T(8,128)S(1)}, u32[]{:S(2)}, u32[]{:S(2)}) collective-permute-start(f32[2,8,512]{2,1,0:T(8,128)S(1)} %get-tuple-element.103), channel_id=1, source_target_pairs={{0,16},{16,32},{32,48},{48,64},{64,80},{80,96},{96,112},{112,0},{1... | collective-permute-start | bytes 98312 | tf_op jit(solution)/shard_map/ppermute | solution.py:16
  253.6 4.5 %collective-permute-start.29 = (f32[2,8,512]{2,1,0:T(8,128)S(1)}, f32[2,8,512]{2,1,0:T(8,128)S(1)}, u32[]{:S(2)}, u32[]{:S(2)}) collective-permute-start(f32[2,8,512]{2,1,0:T(8,128)S(1)} %get-tuple-element.104), channel_id=1, source_target_pairs={{16,0},{32,16},{48,32},{64,48},{80,64},{96,80},{112,96},{0,112},{1... | collective-permute-start | bytes 98312 | tf_op jit(solution)/shard_map/ppermute | solution.py:18
  258.2 4.2 %collective-permute-start.30 = (f32[12,2,512]{2,1,0:T(2,128)S(1)}, f32[12,2,512]{2,1,0:T(2,128)S(1)}, u32[]{:S(2)}, u32[]{:S(2)}) collective-permute-start(f32[12,2,512]{2,1,0:T(2,128)S(1)} %get-tuple-element.101), channel_id=1, source_target_pairs={{0,1},{1,2},{2,3},{3,4},{4,5},{5,6},{6,7},{7,8},{8,9},{9,10},{10,1... | collective-permute-start | bytes 147464 | tf_op jit(solution)/shard_map/ppermute | solution.py:16
  258.3 7.7 %collective-permute-start.31 = (f32[12,2,512]{2,1,0:T(2,128)S(1)}, f32[12,2,512]{2,1,0:T(2,128)S(1)}, u32[]{:S(2)}, u32[]{:S(2)}) collective-permute-start(f32[12,2,512]{2,1,0:T(2,128)S(1)} %get-tuple-element.102), channel_id=1, source_target_pairs={{1,0},{2,1},{3,2},{4,3},{5,4},{6,5},{7,6},{8,7},{9,8},{10,9},{11,1... | collective-permute-start | bytes 147464 | tf_op jit(solution)/shard_map/ppermute | solution.py:18
  (4 other events, 32.3 us)
where the time goes:
time: 296 us; the launch traced here: 292 us
  other arithmetic  82.1 us (28%)
  local copies, waits for them, and re-layouts  73.4 us (25%)
  blocking collectives  60.3 us (20%)
  starting transfers between devices  51.5 us (17%)
  waiting for transfers between devices  23.3 us (8%)
    all_gather x1, blocking collectives, per_device(): lax.all_gather(charge_grid[None], ('gx', 'gy'), axis=0, tiled=True)  60.3 us
    add x6, other arithmetic, convolve_valid(): summed + kernel[tap_index] * lax.slice_in_dim(padded, tap_index, tap_inde...  35.9 us
    ppermute x16, starting transfers between devices, with_halo(): lax.ppermute(head, axis, [((i + 1) % count, i) for i in range(count)])  29.2 us
    slice x15, local copies, waits for them, and re-layouts, restrict_along(): lax.slice_in_dim(jnp.roll(values, -offset, along), 0, length, 2, along)  27.3 us
    ppermute x16, starting transfers between devices, with_halo(): lax.ppermute(tail, axis, [(i, (i + 1) % count) for i in range(count)])  22.3 us
    slice x50, local copies, waits for them, and re-layouts, convolve_along(): summed = summed + kernel[tap_index] * jnp.roll(values, 4 - tap_index, along)  20 us
    add x2, other arithmetic, per_device(): running = potentials[section_index] + prolong_brick(rimmed)  18.5 us
    ppermute x16, waiting for transfers between devices, with_halo(): lax.ppermute(head, axis, [((i + 1) % count, i) for i in range(count)])  14.3 us
  transfers between devices with their start and end apart: 32, of which 12 were waited for; matrix products, arithmetic and copies ran while one was open for 16% of the time, Pallas kernels for 0%

commit v1 on v0

v1 whole, which is shorter than its diff:
```python
import jax
import jax.numpy as jnp
import numpy as np
from jax import lax
from jax.experimental import pallas as pl
from jax.experimental.pallas import tpu as pltpu
from jax.sharding import PartitionSpec as P

first_cell = (0, -1, -2, -2)
cell_count = (16, 11, 9, 7)
brick_cells = (16, 8, 4, 2)
restrict_taps = {-3: -0.0625, -1: 0.5625, 0: 1.0, 1: 0.5625, 3: -0.0625}
lanes = 128
block_rows = ((), (0, 1, 2, 3), (4, 5), (6,))
rows_per_block = 8


def restrict_1d(level):
    matrix = np.zeros((cell_count[level + 1], cell_count[level]), np.float32)
    for coarse in range(cell_count[level + 1]):
        for fine in range(cell_count[level]):
            offset = first_cell[level] + fine - 2 * (first_cell[level + 1] + coarse)
            matrix[coarse, fine] = restrict_taps.get(offset, 0.0)
    return matrix


def prolong_entries(fine):
    if fine % 2 == 0:
        return {fine // 2: 1.0}
    left = (fine - 1) // 2
    return {left - 1: -0.0625, left: 0.5625, left + 1: 0.5625, left + 2: -0.0625}


def prolong_1d(level):
    matrix = np.zeros((cell_count[level], cell_count[level + 1]), np.float32)
    for fine in range(cell_count[level]):
        for coarse, weight in prolong_entries(first_cell[level] + fine).items():
            matrix[fine, coarse - first_cell[level + 1]] = weight
    return matrix


def padded(matrix, rows, columns):
    result = np.zeros((rows, columns), np.float32)
    result[: matrix.shape[0], : matrix.shape[1]] = matrix
    return jnp.asarray(result, jnp.bfloat16)


def restrict_window(rows, width, margin):
    matrix = np.zeros((rows, width), np.float32)
    for coarse in range(rows):
        for offset, weight in restrict_taps.items():
            matrix[coarse, margin + 2 * coarse + offset] = weight
    return jnp.asarray(matrix, jnp.bfloat16)


def prolong_window(rows, width, margin):
    matrix = np.zeros((rows, width), np.float32)
    for fine in range(rows):
        for coarse, weight in prolong_entries(fine).items():
            matrix[fine, margin + coarse] = weight
    return jnp.asarray(matrix, jnp.bfloat16)


def tap_bases():
    bases = np.full((6, lanes, lanes), 256, np.int32)
    for level in (1, 2, 3):
        count = cell_count[level]
        for axis in (0, 1):
            for source in range(count * count):
                for wanted in range(count * count):
                    here, there = divmod(source, count), divmod(wanted, count)
                    if here[1 - axis] == there[1 - axis]:
                        bases[2 * (level - 1) + axis, source, wanted] = here[axis] - there[axis] + 4
    return jnp.asarray(bases)


def brick_offsets(level, axis, bricks):
    if level == 3 and axis == 0:
        return tuple(range(bricks))
    reach = {1: 1, 2: 3, 3: 5}[level]
    return tuple(range(-reach, reach + 1))


def weight_sections(count_x, count_y):
    sections, start = {}, 0
    for level in (1, 2, 3):
        for axis, bricks in ((0, count_x), (1, count_y)):
            offsets = brick_offsets(level, axis, bricks)
            sections[level, axis] = (start, offsets)
            start += len(offsets)
    return sections, start


def split(values):
    high = values.astype(jnp.bfloat16)
    return high, (values - high.astype(jnp.float32)).astype(jnp.bfloat16)


def dot(left, right):
    return lax.dot_general(left, right, (((1,), (0,)), ((), ())), preferred_element_type=jnp.float32)


def dot_lanes(left, right):
    return lax.dot_general(left, right, (((1,), (1,)), ((), ())), preferred_element_type=jnp.float32)


def wrapped(values, margin, axis):
    size = values.shape[axis]
    tail = lax.slice_in_dim(values, size - margin, size, axis=axis)
    head = lax.slice_in_dim(values, 0, margin, axis=axis)
    return jnp.concatenate([tail, values, head], axis=axis)


def restrict_kernel(taps, charges, down_1, down_2, down_3, lane_window, row_window, blocks, rim):
    rows_x, rows_y, depth = charges.shape
    high, low = split(charges[...].reshape(rows_x * rows_y, depth))
    patch = dot(down_1[...], high) + dot(down_1[...], low)
    high, low = split(wrapped(patch, lanes, 1))
    pieces = []
    for begin in range(0, depth, 256):
        pieces.append(
            dot_lanes(lane_window[...], high[:, begin : begin + 512])
            + dot_lanes(lane_window[...], low[:, begin : begin + 512])
        )
    grid = jnp.concatenate(pieces, axis=0)
    for level in (1, 2, 3):
        cells = grid.shape[0]
        rim[0:8, :] = grid[cells - 8 :, :]
        rim[8 : 8 + cells, :] = grid
        rim[8 + cells : 16 + cells, :] = grid[:8, :]
        for index, row in enumerate(block_rows[level]):
            summed = None
            for tap in range(9):
                begin = lanes * index + 4 + tap
                term = taps[3 * level + 2, tap] * rim[begin : begin + lanes, :]
                summed = term if summed is None else summed + term
            blocks[pl.ds(row, lanes, stride=rows_per_block), :] = summed
        if level == 3:
            break
        down = down_2 if level == 1 else down_3
        high, low = split(grid)
        high, low = split(wrapped(dot(high, down[...]) + dot(low, down[...]), 64, 0))
        pieces = []
        for begin in range(0, cells, 256):
            pieces.append(
                dot(row_window[...], high[begin : begin + 384])
                + dot(row_window[...], low[begin : begin + 384])
            )
        grid = jnp.concatenate(pieces, axis=0)
    blocks[pl.ds(7, lanes, stride=rows_per_block), :] = jnp.zeros((lanes, lanes), jnp.float32)


def weight_kernel(sections, taps, bases, weights):
    for (level, axis), (start, offsets) in sections.items():
        base = bases[2 * (level - 1) + axis]
        scale = 0.5**level if axis == 0 else 1.0
        values = [scale * taps[3 * level + axis, tap] for tap in range(9)]
        for index, offset in enumerate(offsets):
            number = base + brick_cells[level] * offset
            if level == 3 and axis == 0:
                number = number & 271
            chosen = jnp.zeros((lanes, lanes), jnp.float32)
            for tap in range(9):
                chosen = jnp.where(number == tap, values[tap], chosen)
            high, low = split(chosen)
            begin = (start + index) * lanes
            weights[begin : begin + lanes, 0:lanes] = high
            weights[begin : begin + lanes, lanes : 2 * lanes] = low


def weighted(pieces, weights, start):
    high = jnp.concatenate([piece[0] for piece in pieces], axis=1)
    low = jnp.concatenate([piece[1] for piece in pieces], axis=1)
    rows = pl.ds(start * lanes, len(pieces) * lanes)
    both = dot(high, weights[rows, :])
    return both[:, :lanes] + both[:, lanes:] + dot(low, weights[rows, 0:lanes])


def convolve_kernel(sections, count_x, count_y, received, weights, blocks):
    for level in (1, 2, 3):
        slices = len(block_rows[level])
        values = jnp.concatenate(
            [received[pl.ds(row, lanes, stride=rows_per_block), :] for row in block_rows[level]], axis=0
        )
        start, offsets = sections[level, 0]
        parts = [part.reshape(slices, count_x, count_y, lanes) for part in split(values)]
        pieces = []
        for offset in offsets:
            turn = offset % count_x
            pieces.append(
                [
                    jnp.concatenate([part[:, turn:], part[:, :turn]], axis=1).reshape(slices * lanes, lanes)
                    if turn
                    else part.reshape(slices * lanes, lanes)
                    for part in parts
                ]
            )
        values = weighted(pieces, weights, start)
        start, offsets = sections[level, 1]
        stack = values.reshape(slices * count_x, count_y, lanes)
        pieces = []
        for offset in offsets:
            turn = offset % count_y
            turned = jnp.concatenate([stack[:, turn:], stack[:, :turn]], axis=1) if turn else stack
            pieces.append(split(turned.reshape(slices * lanes, lanes)))
        values = weighted(pieces, weights, start)
        for index, row in enumerate(block_rows[level]):
            blocks[pl.ds(row, lanes, stride=rows_per_block), :] = values[lanes * index : lanes * (index + 1)]
    blocks[pl.ds(7, lanes, stride=rows_per_block), :] = jnp.zeros((lanes, lanes), jnp.float32)


def prolong_rows(values, row_window):
    high, low = split(wrapped(values, 64, 0))
    pieces = []
    for begin in range(0, values.shape[0], lanes):
        pieces.append(
            dot(row_window[...], high[begin : begin + 256]) + dot(row_window[...], low[begin : begin + 256])
        )
    return jnp.concatenate(pieces, axis=0)


def finish_kernel(received, up_3, up_2, up_1, row_window, finest, potential):
    running = received[pl.ds(block_rows[3][0], lanes, stride=rows_per_block), :]
    for level, up in ((2, up_3), (1, up_2)):
        own = jnp.concatenate(
            [received[pl.ds(row, lanes, stride=rows_per_block), :] for row in block_rows[level]], axis=0
        )
        high, low = split(running)
        running = own + prolong_rows(dot(high, up[...]) + dot(low, up[...]), row_window)
    high, low = split(prolong_rows(running, row_window))
    smooth = dot_lanes(up_1[...], high) + dot_lanes(up_1[...], low)
    potential[...] = finest[...] + smooth.reshape(potential.shape)


def convolve_x_kernel(taps, before, own, after, summed_ref, head, tail):
    rows_x, rows_y, depth = own.shape

    def layer(index):
        if index < 4:
            return before[index]
        return own[index - 4] if index < 4 + rows_x else after[index - 4 - rows_x]

    for row in range(rows_x):
        summed = taps[0, 0] * layer(row)
        for tap in range(1, 9):
            summed = summed + taps[0, tap] * layer(row + tap)
        summed_ref[row] = summed
        head[row] = summed[:4]
        tail[row] = summed[rows_y - 4 :]


def convolve_yz_kernel(taps, before, own, after, result, rim):
    rows_x, rows_y, depth = own.shape
    for row in range(rows_x):
        rim[row, 4:8, :] = before[row]
        rim[row, 8 : 8 + rows_y, :] = own[row]
        rim[row, 8 + rows_y : 12 + rows_y, :] = after[row]
    for row in range(rows_x):
        summed = taps[1, 0] * rim[row, 4 : 4 + rows_y, :]
        for tap in range(1, 9):
            summed = summed + taps[1, tap] * rim[row, 4 + tap : 4 + tap + rows_y, :]
        total = taps[2, 4] * summed
        for tap in (0, 1, 2, 3, 5, 6, 7, 8):
            total = total + taps[2, tap] * pltpu.roll(summed, (4 - tap) % depth, 1)
        result[row] = total


def in_vmem(count):
    return [pl.BlockSpec(memory_space=pltpu.VMEM)] * count


scalars = pl.BlockSpec(memory_space=pltpu.SMEM)


def shape_of(*shape, dtype=jnp.float32):
    return jax.ShapeDtypeStruct(shape, dtype)


def call(kernel, outs, in_specs, scratch=(), flops=0, moved=0):
    return pl.pallas_call(
        kernel,
        out_shape=outs,
        in_specs=in_specs,
        out_specs=jax.tree.map(lambda _: pl.BlockSpec(memory_space=pltpu.VMEM), outs),
        scratch_shapes=list(scratch),
        compiler_params=pltpu.CompilerParams(vmem_limit_bytes=40 * 2**20),
        cost_estimate=pl.CostEstimate(flops=flops, bytes_accessed=moved, transcendentals=0),
    )


def per_device(charges, kernel_taps):
    count_x, count_y = lax.axis_size("gx"), lax.axis_size("gy")
    rows_x, rows_y, depth = charges.shape
    taps = kernel_taps.reshape(12, 9)
    both = ("gx", "gy")
    downs = [restrict_1d(level) for level in range(3)]
    ups = [prolong_1d(level) for level in range(3)]
    down_1 = padded(np.kron(downs[0], downs[0]), lanes, rows_x * rows_y)
    down_2 = padded(np.kron(downs[1].T, downs[1].T), lanes, lanes)
    down_3 = padded(np.kron(downs[2].T, downs[2].T), lanes, lanes)
    up_1 = padded(np.kron(ups[0], ups[0]), rows_x * rows_y, lanes)
    up_2 = padded(np.kron(ups[1].T, ups[1].T), lanes, lanes)
    up_3 = padded(np.kron(ups[2].T, ups[2].T), lanes, lanes)
    sections, section_count = weight_sections(count_x, count_y)
    block_shape = (lanes * rows_per_block, lanes)
    exchange_shape = (lanes, rows_per_block, lanes)

    blocks = call(
        restrict_kernel,
        shape_of(*block_shape),
        [scalars] + in_vmem(6),
        [pltpu.VMEM((depth // 2 + 16, lanes), jnp.float32)],
        flops=10**9,
        moved=2 * 10**6,
    )(
        taps,
        charges,
        down_1,
        down_2,
        down_3,
        restrict_window(lanes, 512, 128),
        restrict_window(lanes, 384, 64),
    )
    received = lax.all_to_all(blocks.reshape(exchange_shape), both, 0, 0, tiled=True)

    weights = call(
        lambda *refs: weight_kernel(sections, *refs),
        shape_of(section_count * lanes, 2 * lanes, dtype=jnp.bfloat16),
        [scalars] + in_vmem(1),
        flops=2 * 10**7,
        moved=3 * 10**6,
    )(taps, tap_bases())

    def shifted(values, axis, step):
        count = lax.axis_size(axis)
        return lax.ppermute(values, axis, [(i, (i + step) % count) for i in range(count)])

    before = shifted(charges[rows_x - 4 :], "gx", 1)
    after = shifted(charges[:4], "gx", -1)
    summed, head, tail = call(
        convolve_x_kernel,
        (shape_of(rows_x, rows_y, depth), shape_of(rows_x, 4, depth), shape_of(rows_x, 4, depth)),
        [scalars] + in_vmem(3),
        flops=18 * rows_x * rows_y * depth,
        moved=3 * 10**6,
    )(taps, before, charges, after)
    finest = call(
        convolve_yz_kernel,
        shape_of(rows_x, rows_y, depth),
        [scalars] + in_vmem(3),
        [pltpu.VMEM((rows_x, rows_y + 16, depth), jnp.float32)],
        flops=36 * rows_x * rows_y * depth,
        moved=3 * 10**6,
    )(taps, shifted(tail, "gy", 1), summed, shifted(head, "gy", -1))

    blocks = call(
        lambda *refs: convolve_kernel(sections, count_x, count_y, *refs),
        shape_of(*block_shape),
        in_vmem(2),
        flops=10**9,
        moved=4 * 10**6,
    )(received.reshape(block_shape), weights)
    received = lax.all_to_all(blocks.reshape(exchange_shape), both, 0, 0, tiled=True)

    return call(
        finish_kernel,
        shape_of(rows_x, rows_y, depth),
        in_vmem(6),
        flops=10**9,
        moved=4 * 10**6,
    )(received.reshape(block_shape), up_3, up_2, up_1, prolong_window(256, 256, 64), finest)


def solution(mesh):
    placed = (P("gx", "gy", None), P())
    return jax.shard_map(
        per_device, mesh=mesh, in_specs=placed, out_specs=P("gx", "gy", None), check_vma=False
    )
```

time: 296 us -> 65.4 us (0.22)
  the two profiles are of different devices: /device:TPU:30 before, /device:TPU:1 now
where the time goes in v1:
time: 65.4 us; the launch traced here: 64.9 us
  starting transfers between devices  22.8 us (35%)
  Pallas kernels  17 us (26%)
  waiting for transfers between devices  16.8 us (26%)
  local copies, waits for them, and re-layouts  8.17 us (12%)
    all_to_all x2, starting transfers between devices, per_device(): lax.all_to_all(blocks.reshape(exchange_shape), both, 0, 0, tiled=True)  15.8 us
    all_to_all x2, waiting for transfers between devices, per_device(): lax.all_to_all(blocks.reshape(exchange_shape), both, 0, 0, tiled=True)  8.67 us
    ppermute x4, waiting for transfers between devices, shifted(): lax.ppermute(values, axis, [(i, (i + step) % count) for i in range(count)])  8.08 us
    unnamed x27, local copies, waits for them, and re-layouts  7.31 us
    ppermute x4, starting transfers between devices, shifted(): lax.ppermute(values, axis, [(i, (i + step) % count) for i in range(count)])  7.04 us
    pallas_call x1, Pallas kernels, per_device(): call(convolve_yz_kernel, shape_of(rows_x, rows_y, depth), [scalars] + in_...  4.15 us
    pallas_call x1, Pallas kernels, per_device(): call(restrict_kernel, shape_of(*block_shape), [scalars] + in_vmem(6), [pl...  3.31 us
    pallas_call x1, Pallas kernels, per_device(): call(lambda *refs: weight_kernel(sections, *refs), shape_of(section_count...  2.63 us
  transfers between devices with their start and end apart: 6, of which 2 were waited for; matrix products, arithmetic and copies ran while one was open for 1% of the time, Pallas kernels for 17%

profile of v1, /device:TPU:1, one launch (start us, length us, event | category | flops | bytes accessed | tf_op | source)
XLA Modules:
  0.0 64.9 jit_solution(5658450348528197293)
XLA Ops:
  0.0 0.7 %copy.14 = f32[4,3,9]{2,1,0:T(4,128)S(1)} copy(f32[4,3,9]{2,0,1:T(4,128)} %param.13) | data formatting | bytes 864 | tf_op args[1]
  0.7 1.2 %copy-done = f32[16,16,1024]{2,1,0:T(8,128)S(1)} copy-done((f32[16,16,1024]{2,1,0:T(8,128)S(1)}, f32[16,16,1024]{2,1,0:T(8,128)}, u32[]{:S(2)}) %copy-start) | copy-done | bytes 1048600
  1.9 0.9 %copy-done.5 = bf16[128,512]{1,0:T(8,128)(2,1)S(1)} copy-done((bf16[128,512]{1,0:T(8,128)(2,1)S(1)}, bf16[128,512]{1,0:T(8,128)(2,1)}, u32[]{:S(2)}) %copy-start.5) | copy-done | bytes 131096
  2.8 0.9 %copy-done.6 = bf16[128,384]{1,0:T(8,128)(2,1)S(1)} copy-done((bf16[128,384]{1,0:T(8,128)(2,1)S(1)}, bf16[128,384]{1,0:T(8,128)(2,1)}, u32[]{:S(2)}) %copy-start.6) | copy-done | bytes 98328
  3.7 0.8 %copy-done.8 = bf16[128,256]{1,0:T(8,128)(2,1)S(1)} copy-done((bf16[128,256]{1,0:T(8,128)(2,1)S(1)}, bf16[128,256]{1,0:T(8,128)(2,1)}, u32[]{:S(2)}) %copy-start.8) | copy-done | bytes 65560
  4.6 0.8 %copy-done.11 = bf16[128,128]{1,0:T(8,128)(2,1)S(1)} copy-done((bf16[128,128]{1,0:T(8,128)(2,1)S(1)}, bf16[128,128]{1,0:T(8,128)(2,1)}, u32[]{:S(2)}) %copy-start.11) | copy-done | bytes 32792
  5.3 0.8 %copy-done.12 = bf16[128,128]{1,0:T(8,128)(2,1)S(1)} copy-done((bf16[128,128]{1,0:T(8,128)(2,1)S(1)}, bf16[128,128]{1,0:T(8,128)(2,1)}, u32[]{:S(2)}) %copy-start.12) | copy-done | bytes 32792
  6.1 3.3 %shard_map.118 = f32[1024,128]{1,0:T(8,128)} custom-call(f32[12,9]{1,0:T(8,128)S(1)} %reshape.15.taps.refs_0_, f32[16,16,1024]{2,1,0:T(8,128)S(1)} %copy-done, bf16[128,256]{1,0:T(8,128)(2,1)S(1)} %copy-done.8, bf16[128,128]{1,0:T(8,128)(2,1)S(1)} %copy-done.11, bf16[128,128]{1,0:T(8,128)(2,1)S(1)} %copy-done.12, bf16[128,512]{1,0:T(8,128)(2,1)S(1)} %copy-done.5, ...), custom_call_target="tpu_custom_call" | custom-call | flops 1000000000 | bytes 2000000 | tf_op jit(solution)/shard_map/pallas_call | solution.py:308
  9.4 11.5 %all-to-all-start = ((f32[128,8,128]{2,1,0:T(8,128)}), f32[128,8,128]{2,1,0:T(8,128)S(1)}, u32[]{:S(2)}, u32[]{:S(2)}) async-start(f32[128,8,128]{2,1,0:T(8,128)} %bitcast), calls=%async_computation | async-start | bytes 1048576 | tf_op jit(solution)/shard_map/all_to_all | solution.py:324
  20.9 0.0 copy-done.1
  20.9 0.8 %fusion = (f32[4,16,1024]{2,1,0:T(8,128)}, f32[4,16,1024]{2,1,0:T(8,128)}) fusion(f32[16,16,1024]{2,1,0:T(8,128)S(1)} %copy-done.1), kind=kLoop, calls=%fused_computation | loop fusion | bytes 1048576 | tf_op jit(solution)/shard_map/slice | solution.py:339
  21.8 1.8 %collective-permute-start = (f32[4,16,1024]{2,1,0:T(8,128)}, f32[4,16,1024]{2,1,0:T(8,128)}, u32[]{:S(2)}, u32[]{:S(2)}) collective-permute-start(f32[4,16,1024]{2,1,0:T(8,128)} %get-tuple-element.12), channel_id=1, source_target_pairs={{0,16},{16,32},{32,48},{48,64},{64,80},{80,96},{96,112},{112,0},{1... | collective-permute-start | bytes 786440 | tf_op jit(solution)/shard_map/ppermute | solution.py:336
  23.5 0.0 collective-permute-start.1
  23.5 0.0 copy-done.3
  23.5 2.6 %shard_map.119.refs_1_ = bf16[4992,256]{1,0:T(8,128)(2,1)S(1)} custom-call(f32[12,9]{1,0:T(8,128)S(1)} %reshape.15.taps.refs_0_, s32[6,128,128]{2,1,0:T(8,128)S(1)} %copy-done.3), custom_call_target="tpu_custom_call" | custom-call | flops 20000000 | bytes 3000000 | tf_op jit(solution)/shard_map/pallas_call | solution.py:326
  26.2 8.7 %all-to-all-done = f32[128,8,128]{2,1,0:T(8,128)S(1)} async-done(((f32[128,8,128]{2,1,0:T(8,128)}), f32[128,8,128]{2,1,0:T(8,128)S(1)}, u32[]{:S(2)}, u32[]{:S(2)}) %all-to-all-start) | async-done | bytes 524320 | tf_op jit(solution)/shard_map/all_to_all | solution.py:324
  34.8 2.6 %shard_map.120 = f32[1024,128]{1,0:T(8,128)} custom-call(f32[1024,128]{1,0:T(8,128)S(1)} %bitcast.5, bf16[4992,256]{1,0:T(8,128)(2,1)S(1)} %shard_map.119.refs_1_), custom_call_target="tpu_custom_call" | custom-call | flops 1000000000 | bytes 4000000 | tf_op jit(solution)/shard_map/pallas_call | solution.py:356
  37.4 4.3 %all-to-all-start.1 = ((f32[128,8,128]{2,1,0:T(8,128)}), f32[128,8,128]{2,1,0:T(8,128)S(1)}, u32[]{:S(2)}, u32[]{:S(2)}) async-start(f32[128,8,128]{2,1,0:T(8,128)} %bitcast.2), calls=%async_computation.1 | async-start | bytes 1048576 | tf_op jit(solution)/shard_map/all_to_all | solution.py:363
  41.7 0.0 collective-permute-done.before
  41.8 0.0 collective-permute-done.1.after
  41.8 0.0 copy-start.2
  41.8 1.2 %copy-done.2 = f32[16,16,1024]{2,1,0:T(8,128)S(1)} copy-done((f32[16,16,1024]{2,1,0:T(8,128)S(1)}, f32[16,16,1024]{2,1,0:T(8,128)}, u32[]{:S(2)}) %copy-start.2) | copy-done | bytes 1048600
  43.0 1.8 %shard_map.121 = (f32[16,16,1024]{2,1,0:T(8,128)S(1)}, f32[16,4,1024]{2,1,0:T(4,128)S(1)}, f32[16,4,1024]{2,1,0:T(4,128)S(1)}) custom-call(f32[12,9]{1,0:T(8,128)S(1)} %reshape.15.taps.refs_0_, f32[4,16,1024]{2,1,0:T(8,128)} %collective-permute-done.before, f32[16,16,1024]{2,1,0:T(8,128)S(1)} %copy-done.2, f32[4,16,1024]{2,1,0:T(8,128)} %collective-permute-done.1.after), custom_call_target="tpu_custom_call" | custom-call | flops 4718592 | bytes 3000000 | tf_op jit(solution)/shard_map/pallas_call | solution.py:340
  44.8 1.5 %collective-permute-start.2 = (f32[16,4,1024]{2,1,0:T(4,128)S(1)}, f32[16,4,1024]{2,1,0:T(4,128)S(1)}, u32[]{:S(2)}, u32[]{:S(2)}) collective-permute-start(f32[16,4,1024]{2,1,0:T(4,128)S(1)} %get-tuple-element.8), channel_id=1, source_target_pairs={{0,1},{1,2},{2,3},{3,4},{4,5},{5,6},{6,7},{7,8},{8,9},{9,10},{10,1... | collective-permute-start | bytes 786440 | tf_op jit(solution)/shard_map/ppermute | solution.py:336
  46.2 3.8 %collective-permute-start.3 = (f32[16,4,1024]{2,1,0:T(4,128)S(1)}, f32[16,4,1024]{2,1,0:T(4,128)S(1)}, u32[]{:S(2)}, u32[]{:S(2)}) collective-permute-start(f32[16,4,1024]{2,1,0:T(4,128)S(1)} %get-tuple-element.10), channel_id=1, source_target_pairs={{0,15},{1,0},{2,1},{3,2},{4,3},{5,4},{6,5},{7,6},{8,7},{9,8},{10,9... | collective-permute-start | bytes 786440 | tf_op jit(solution)/shard_map/ppermute | solution.py:336
  50.0 8.1 %collective-permute-done.2.before = f32[16,4,1024]{2,1,0:T(4,128)S(1)} collective-permute-done((f32[16,4,1024]{2,1,0:T(4,128)S(1)}, f32[16,4,1024]{2,1,0:T(4,128)S(1)}, u32[]{:S(2)}, u32[]{:S(2)}) %collective-permute-start.2) | collective-permute-done | bytes 262176 | tf_op jit(solution)/shard_map/ppermute | solution.py:336
  58.1 0.0 collective-permute-done.3.after
  58.1 4.2 %shard_map.122.finest = f32[16,16,1024]{2,1,0:T(8,128)S(1)} custom-call(f32[12,9]{1,0:T(8,128)S(1)} %reshape.15.taps.refs_0_, f32[16,4,1024]{2,1,0:T(4,128)S(1)} %collective-permute-done.2.before, f32[16,16,1024]{2,1,0:T(8,128)S(1)} %get-tuple-element.9.own, f32[16,4,1024]{2,1,0:T(4,128)S(1)} %collective-permute-done.3.after), custom_call_target="tpu_custom_call" | custom-call | flops 9437184 | bytes 3000000 | tf_op jit(solution)/shard_map/pallas_call | solution.py:347
  62.3 0.0 all-to-all-done.1
  62.3 0.0 copy-done.4
  62.3 0.0 copy-done.7
  62.3 2.6 %shard_map.123 = f32[16,16,1024]{2,1,0:T(8,128)} custom-call(f32[1024,128]{1,0:T(8,128)S(1)} %bitcast.4, bf16[128,128]{1,0:T(8,128)(2,1)S(1)} %copy-done.9, bf16[128,128]{1,0:T(8,128)(2,1)S(1)} %copy-done.10, bf16[256,128]{1,0:T(8,128)(2,1)S(1)} %copy-done.7, bf16[256,256]{1,0:T(8,128)(2,1)S(1)} %copy-done.4, f32[16,16,1024]{2,1,0:T(8,128)S(1)} %shard_map.122.finest), custom_call_target="tpu_custom_call" | custom-call | flops 1000000000 | bytes 4000000 | tf_op jit(solution)/shard_map/pallas_call | solution.py:365
  (15 shorter events, 0.0 us)
Async XLA Ops:
  0.7 1.2 %copy-start = (f32[16,16,1024]{2,1,0:T(8,128)S(1)}, f32[16,16,1024]{2,1,0:T(8,128)}, u32[]{:S(2)}) copy-start(f32[16,16,1024]{2,1,0:T(8,128)} %own.1) | copy-start | bytes 3145732
  1.9 0.9 %copy-start.5 = (bf16[128,512]{1,0:T(8,128)(2,1)S(1)}, bf16[128,512]{1,0:T(8,128)(2,1)}, u32[]{:S(2)}) copy-start(bf16[128,512]{1,0:T(8,128)(2,1)} %constant.26.clone.lane_window) | copy-start | bytes 393220
  2.8 0.9 %copy-start.6 = (bf16[128,384]{1,0:T(8,128)(2,1)S(1)}, bf16[128,384]{1,0:T(8,128)(2,1)}, u32[]{:S(2)}) copy-start(bf16[128,384]{1,0:T(8,128)(2,1)} %constant.27.clone.row_window) | copy-start | bytes 294916
  3.7 0.8 %copy-start.8 = (bf16[128,256]{1,0:T(8,128)(2,1)S(1)}, bf16[128,256]{1,0:T(8,128)(2,1)}, u32[]{:S(2)}) copy-start(bf16[128,256]{1,0:T(8,128)(2,1)} %constant.20.clone.down_1) | copy-start | bytes 196612
  4.6 0.8 %copy-start.11 = (bf16[128,128]{1,0:T(8,128)(2,1)S(1)}, bf16[128,128]{1,0:T(8,128)(2,1)}, u32[]{:S(2)}) copy-start(bf16[128,128]{1,0:T(8,128)(2,1)} %constant.21.clone.down_2) | copy-start | bytes 98308
  5.3 0.8 %copy-start.12 = (bf16[128,128]{1,0:T(8,128)(2,1)S(1)}, bf16[128,128]{1,0:T(8,128)(2,1)}, u32[]{:S(2)}) copy-start(bf16[128,128]{1,0:T(8,128)(2,1)} %constant.22.clone.down_3) | copy-start | bytes 98308
  6.1 14.8 %copy-start.1 = (f32[16,16,1024]{2,1,0:T(8,128)S(1)}, f32[16,16,1024]{2,1,0:T(8,128)}, u32[]{:S(2)}) copy-start(f32[16,16,1024]{2,1,0:T(8,128)} %own.1) | copy-start | bytes 3145732
  6.1 17.4 %copy-start.3 = (s32[6,128,128]{2,1,0:T(8,128)S(1)}, s32[6,128,128]{2,1,0:T(8,128)}, u32[]{:S(2)}) copy-start(s32[6,128,128]{2,1,0:T(8,128)} %constant.28.clone.refs_1_) | copy-start | bytes 1179652
  9.4 25.4 %all-to-all-start = ((f32[128,8,128]{2,1,0:T(8,128)}), f32[128,8,128]{2,1,0:T(8,128)S(1)}, u32[]{:S(2)}, u32[]{:S(2)}) async-start(f32[128,8,128]{2,1,0:T(8,128)} %bitcast), calls=%async_computation | async-start | bytes 1048576 | tf_op jit(solution)/shard_map/all_to_all | solution.py:324
  21.8 20.0 %collective-permute-start = (f32[4,16,1024]{2,1,0:T(8,128)}, f32[4,16,1024]{2,1,0:T(8,128)}, u32[]{:S(2)}, u32[]{:S(2)}) collective-permute-start(f32[4,16,1024]{2,1,0:T(8,128)} %get-tuple-element.12), channel_id=1, source_target_pairs={{0,16},{16,32},{32,48},{48,64},{64,80},{80,96},{96,112},{112,0},{1... | collective-permute-start | bytes 786440 | tf_op jit(solution)/shard_map/ppermute | solution.py:336
  23.5 18.2 %collective-permute-start.1 = (f32[4,16,1024]{2,1,0:T(8,128)}, f32[4,16,1024]{2,1,0:T(8,128)}, u32[]{:S(2)}, u32[]{:S(2)}) collective-permute-start(f32[4,16,1024]{2,1,0:T(8,128)} %get-tuple-element.11), channel_id=1, source_target_pairs={{0,112},{16,0},{32,16},{48,32},{64,48},{80,64},{96,80},{112,96},{1... | collective-permute-start | bytes 786440 | tf_op jit(solution)/shard_map/ppermute | solution.py:336
  37.4 24.9 %copy-start.4 = (bf16[256,256]{1,0:T(8,128)(2,1)S(1)}, bf16[256,256]{1,0:T(8,128)(2,1)}, u32[]{:S(2)}) copy-start(bf16[256,256]{1,0:T(8,128)(2,1)} %constant.29.clone.row_window) | copy-start | bytes 393220
  37.4 24.9 %copy-start.7 = (bf16[256,128]{1,0:T(8,128)(2,1)S(1)}, bf16[256,128]{1,0:T(8,128)(2,1)}, u32[]{:S(2)}) copy-start(bf16[256,128]{1,0:T(8,128)(2,1)} %constant.23.clone.up_1) | copy-start | bytes 196612
  37.4 24.9 %copy-start.9 = (bf16[128,128]{1,0:T(8,128)(2,1)S(1)}, bf16[128,128]{1,0:T(8,128)(2,1)}, u32[]{:S(2)}) copy-start(bf16[128,128]{1,0:T(8,128)(2,1)} %constant.25.clone.up_3) | copy-start | bytes 98308
  37.4 24.9 %copy-start.10 = (bf16[128,128]{1,0:T(8,128)(2,1)S(1)}, bf16[128,128]{1,0:T(8,128)(2,1)}, u32[]{:S(2)}) copy-start(bf16[128,128]{1,0:T(8,128)(2,1)} %constant.24.clone.up_2) | copy-start | bytes 98308
  37.4 24.9 %all-to-all-start.1 = ((f32[128,8,128]{2,1,0:T(8,128)}), f32[128,8,128]{2,1,0:T(8,128)S(1)}, u32[]{:S(2)}, u32[]{:S(2)}) async-start(f32[128,8,128]{2,1,0:T(8,128)} %bitcast.2), calls=%async_computation.1 | async-start | bytes 1048576 | tf_op jit(solution)/shard_map/all_to_all | solution.py:363
  41.8 1.2 %copy-start.2 = (f32[16,16,1024]{2,1,0:T(8,128)S(1)}, f32[16,16,1024]{2,1,0:T(8,128)}, u32[]{:S(2)}) copy-start(f32[16,16,1024]{2,1,0:T(8,128)} %own.1) | copy-start | bytes 3145732
  44.8 13.4 %collective-permute-start.2 = (f32[16,4,1024]{2,1,0:T(4,128)S(1)}, f32[16,4,1024]{2,1,0:T(4,128)S(1)}, u32[]{:S(2)}, u32[]{:S(2)}) collective-permute-start(f32[16,4,1024]{2,1,0:T(4,128)S(1)} %get-tuple-element.8), channel_id=1, source_target_pairs={{0,1},{1,2},{2,3},{3,4},{4,5},{5,6},{6,7},{7,8},{8,9},{9,10},{10,1... | collective-permute-start | bytes 786440 | tf_op jit(solution)/shard_map/ppermute | solution.py:336
  46.2 11.9 %collective-permute-start.3 = (f32[16,4,1024]{2,1,0:T(4,128)S(1)}, f32[16,4,1024]{2,1,0:T(4,128)S(1)}, u32[]{:S(2)}, u32[]{:S(2)}) collective-permute-start(f32[16,4,1024]{2,1,0:T(4,128)S(1)} %get-tuple-element.10), channel_id=1, source_target_pairs={{0,15},{1,0},{2,1},{3,2},{4,3},{5,4},{6,5},{7,6},{8,7},{9,8},{10,9... | collective-permute-start | bytes 786440 | tf_op jit(solution)/shard_map/ppermute | solution.py:336

commit v2 on v1

v2 whole, which is shorter than its diff:
```python
import jax
import jax.numpy as jnp
import numpy as np
from jax import lax
from jax.experimental import pallas as pl
from jax.experimental.pallas import tpu as pltpu
from jax.sharding import PartitionSpec as P

first_cell = (0, -1, -2, -2)
cell_count = (16, 11, 9, 7)
brick_cells = (16, 8, 4, 2)
restrict_taps = {-3: -0.0625, -1: 0.5625, 0: 1.0, 1: 0.5625, 3: -0.0625}
lanes = 128
block_rows = ((), (0, 1, 2, 3), (4, 5), (6,))
rows_per_block = 8


def restrict_1d(level):
    matrix = np.zeros((cell_count[level + 1], cell_count[level]), np.float32)
    for coarse in range(cell_count[level + 1]):
        for fine in range(cell_count[level]):
            offset = first_cell[level] + fine - 2 * (first_cell[level + 1] + coarse)
            matrix[coarse, fine] = restrict_taps.get(offset, 0.0)
    return matrix


def prolong_entries(fine):
    if fine % 2 == 0:
        return {fine // 2: 1.0}
    left = (fine - 1) // 2
    return {left - 1: -0.0625, left: 0.5625, left + 1: 0.5625, left + 2: -0.0625}


def prolong_1d(level):
    matrix = np.zeros((cell_count[level], cell_count[level + 1]), np.float32)
    for fine in range(cell_count[level]):
        for coarse, weight in prolong_entries(first_cell[level] + fine).items():
            matrix[fine, coarse - first_cell[level + 1]] = weight
    return matrix


def padded(matrix, rows, columns):
    result = np.zeros((rows, columns), np.float32)
    result[: matrix.shape[0], : matrix.shape[1]] = matrix
    return result


def restrict_window(rows, width, margin):
    matrix = np.zeros((rows, width), np.float32)
    for coarse in range(rows):
        for offset, weight in restrict_taps.items():
            matrix[coarse, margin + 2 * coarse + offset] = weight
    return matrix


def prolong_window(rows, width, margin):
    matrix = np.zeros((rows, width), np.float32)
    for fine in range(rows):
        for coarse, weight in prolong_entries(fine).items():
            matrix[fine, margin + coarse] = weight
    return matrix


def tap_tables():
    tables = []
    for level in (1, 2, 3):
        count = cell_count[level]
        for axis in (0, 1):
            chooser, same, number = (np.zeros((rows, lanes), np.float32) for rows in (lanes, lanes, 16))
            number[:] = 256.0
            for cell in range(count * count):
                place = divmod(cell, count)
                chooser[cell, place[axis]] = 1.0
                for other in range(count * count):
                    same[cell, other] = divmod(other, count)[1 - axis] == place[1 - axis]
                for source in range(count):
                    number[source, cell] = source - place[axis] + 4
            tables += [chooser, same, number]
    return jnp.asarray(np.concatenate(tables), jnp.bfloat16)


def brick_offsets(level, axis, bricks):
    if level == 3 and axis == 0:
        return tuple(range(bricks))
    reach = {1: 1, 2: 3, 3: 5}[level]
    return tuple(range(-reach, reach + 1))


def weight_sections(count_x, count_y):
    sections, start = {}, 0
    for level in (1, 2, 3):
        for axis, bricks in ((0, count_x), (1, count_y)):
            offsets = brick_offsets(level, axis, bricks)
            sections[level, axis] = (start, offsets)
            start += len(offsets)
    return sections, start


def split(values):
    high = values.astype(jnp.bfloat16)
    return high, (values - high.astype(jnp.float32)).astype(jnp.bfloat16)


def dot(left, right):
    return lax.dot_general(left, right, (((1,), (0,)), ((), ())), preferred_element_type=jnp.float32)


def dot_lanes(left, right):
    return lax.dot_general(left, right, (((1,), (1,)), ((), ())), preferred_element_type=jnp.float32)


def wrapped(values, margin, axis):
    size = values.shape[axis]
    tail = lax.slice_in_dim(values, size - margin, size, axis=axis)
    head = lax.slice_in_dim(values, 0, margin, axis=axis)
    return jnp.concatenate([tail, values, head], axis=axis)


def both_ways(product):
    half = product.shape[1] // 2
    return product[:, :half] + product[:, half:]


def side_by_side(values):
    return jnp.concatenate(split(values), axis=1)


def restrict_kernel(
    taps_far, charges_far, constants_far, blocks_far, head, tail, taps, charges, constants, patch, rim, blocks, arrived
):
    rows_x, rows_y, depth = charges.shape
    columns = rows_x * rows_y
    copies = [
        pltpu.make_async_copy(constants_far, constants, arrived.at[0]),
        pltpu.make_async_copy(taps_far, taps, arrived.at[1]),
    ]
    leaving = [
        pltpu.make_async_copy(charges.at[pl.ds(0, 4)], head, arrived.at[2]),
        pltpu.make_async_copy(charges.at[pl.ds(rows_x - 4, 4)], tail, arrived.at[3]),
    ]
    chunks = []
    for index in range(depth // 256):
        section = pl.ds(256 * index, 256)
        chunks.append(
            pltpu.make_async_copy(
                charges_far.at[:, :, section], charges.at[:, :, section], arrived.at[4 + index]
            )
        )
    copies[0].start()
    for chunk in chunks:
        chunk.start()
    copies[1].start()
    copies[0].wait()
    for index, chunk in enumerate(chunks):
        chunk.wait()
        high, low = split(charges[:, :, 256 * index : 256 * (index + 1)].reshape(columns, 256))
        down = constants[:, 0:columns]
        high, low = split(dot(down, high) + dot(down, low))
        begin = lanes + 256 * index
        patch[0:lanes, begin : begin + 256] = high
        patch[lanes : 2 * lanes, begin : begin + 256] = low
    for copy in leaving:
        copy.start()
    patch[:, 0:lanes] = patch[:, depth : depth + lanes]
    patch[:, depth + lanes : depth + 2 * lanes] = patch[:, lanes : 2 * lanes]
    lane_window = constants[:, 256:768]
    row_window = constants[:, 768:1152]
    grid = jnp.concatenate(
        [
            both_ways(dot_lanes(lane_window, patch[:, begin : begin + 512]))
            for begin in range(0, depth, 256)
        ],
        axis=0,
    )
    copies[1].wait()
    for level in (1, 2, 3):
        cells = grid.shape[0]
        rim[0:8, :] = grid[cells - 8 :, :]
        rim[8 : 8 + cells, :] = grid
        rim[8 + cells : 16 + cells, :] = grid[:8, :]
        for index, row in enumerate(block_rows[level]):
            summed = None
            for tap in range(9):
                begin = lanes * index + 4 + tap
                term = taps[2, level, tap] * rim[begin : begin + lanes, :]
                summed = term if summed is None else summed + term
            blocks[pl.ds(row, lanes, stride=rows_per_block), :] = summed
        if level == 3:
            break
        down = constants[:, 1024 + 128 * level : 1152 + 128 * level]
        grid = dot(side_by_side(grid), jnp.concatenate([down, down], axis=0))
        ready = wrapped(side_by_side(grid), 64, 0)
        grid = jnp.concatenate(
            [both_ways(dot(row_window, ready[begin : begin + 384])) for begin in range(0, cells, 256)], axis=0
        )
    blocks[pl.ds(7, lanes, stride=rows_per_block), :] = jnp.zeros((lanes, lanes), jnp.float32)
    for index in range(4):
        section = pl.ds(256 * index, 256)
        leaving.append(
            pltpu.make_async_copy(blocks.at[section], blocks_far.at[section], arrived.at[4 + depth // 256 + index])
        )
        leaving[-1].start()
    for copy in leaving:
        copy.wait()


def weight_kernel(sections, taps, tables, weights):
    for (level, axis), (start, offsets) in sections.items():
        begin = (2 * (level - 1) + axis) * (2 * lanes + 16)
        chooser = tables[begin : begin + lanes, 0:16]
        same = tables[begin + lanes : begin + 2 * lanes, :]
        base = tables[begin + 2 * lanes : begin + 2 * lanes + 16, :].astype(jnp.float32).astype(jnp.int32)
        scale = 0.5**level if axis == 0 else 1.0
        values = [scale * taps[axis, level, tap] for tap in range(9)]
        for index, offset in enumerate(offsets):
            number = base + brick_cells[level] * offset
            if level == 3 and axis == 0:
                number = number & 271
            chosen = jnp.zeros(number.shape, jnp.float32)
            for tap in range(9):
                chosen = jnp.where(number == tap, values[tap], chosen)
            spread = dot(chooser, side_by_side(chosen)).astype(jnp.bfloat16)
            rows = pl.ds((start + index) * lanes, lanes)
            weights[rows, 0:lanes] = spread[:, :lanes] * same
            weights[rows, lanes : 2 * lanes] = spread[:, lanes:] * same


def weighted(pieces, weights, start):
    rows = pl.ds(start * lanes, len(pieces) * lanes)
    product = both_ways(dot(jnp.concatenate(pieces, axis=1), weights[rows, :]))
    half = product.shape[0] // 2
    return product[:half] + product[half:]


def convolve_kernel(sections, count_x, count_y, received, weights, blocks):
    for level in (1, 2, 3):
        slices = len(block_rows[level])
        values = jnp.concatenate(
            [received[pl.ds(row, lanes, stride=rows_per_block), :] for row in block_rows[level]], axis=0
        )
        start, offsets = sections[level, 0]
        stack = jnp.concatenate(split(values), axis=0).reshape(2 * slices, count_x, count_y, lanes)
        pieces = []
        for offset in offsets:
            turn = offset % count_x
            turned = jnp.concatenate([stack[:, turn:], stack[:, :turn]], axis=1) if turn else stack
            pieces.append(turned.reshape(2 * slices * lanes, lanes))
        values = weighted(pieces, weights, start)
        start, offsets = sections[level, 1]
        stack = values.reshape(slices * count_x, count_y, lanes)
        pieces = []
        for offset in offsets:
            turn = offset % count_y
            turned = jnp.concatenate([stack[:, turn:], stack[:, :turn]], axis=1) if turn else stack
            pieces.append(jnp.concatenate(split(turned.reshape(slices * lanes, lanes)), axis=0))
        values = weighted(pieces, weights, start)
        for index, row in enumerate(block_rows[level]):
            blocks[pl.ds(row, lanes, stride=rows_per_block), :] = values[lanes * index : lanes * (index + 1)]
    blocks[pl.ds(7, lanes, stride=rows_per_block), :] = jnp.zeros((lanes, lanes), jnp.float32)


def finish_kernel(received, constants, finest, potential, ready, left):
    rows_x, rows_y, depth = finest.shape
    row_window = constants[:, 512:768]
    running = received[pl.ds(block_rows[3][0], lanes, stride=rows_per_block), :]
    for level in (2, 1):
        own = jnp.concatenate(
            [received[pl.ds(row, lanes, stride=rows_per_block), :] for row in block_rows[level]], axis=0
        )
        up = constants[:, 128 * (2 - level) : 128 * (3 - level)]
        pairs = wrapped(side_by_side(dot(side_by_side(running), up)), 64, 0)
        running = own + jnp.concatenate(
            [
                both_ways(dot(row_window, pairs[begin : begin + 256]))
                for begin in range(0, running.shape[0], lanes)
            ],
            axis=0,
        )
    pairs = wrapped(side_by_side(running), 64, 0)
    copies = []
    for index in range(depth // 256):
        fine = both_ways(dot(row_window, pairs[lanes * index : lanes * index + 256]))
        smooth = dot_lanes(constants[:, 256:512], side_by_side(fine))
        section = slice(256 * index, 256 * (index + 1))
        ready[:, :, section] = finest[:, :, section] + smooth.reshape(rows_x, rows_y, 256)
        places = pl.ds(256 * index, 256)
        copies.append(
            pltpu.make_async_copy(ready.at[:, :, places], potential.at[:, :, places], left.at[index])
        )
        copies[-1].start()
    for copy in copies:
        copy.wait()


def convolve_x_kernel(taps, before, own, after, summed_ref, head, tail):
    rows_x, rows_y, depth = own.shape

    def layer(index):
        if index < 4:
            return before[index]
        return own[index - 4] if index < 4 + rows_x else after[index - 4 - rows_x]

    for row in range(rows_x):
        summed = taps[0, 0, 0] * layer(row)
        for tap in range(1, 9):
            summed = summed + taps[0, 0, tap] * layer(row + tap)
        summed_ref[row] = summed
        head[row] = summed[:4]
        tail[row] = summed[rows_y - 4 :]


def convolve_yz_kernel(taps, before, own, after, result, rim):
    rows_x, rows_y, depth = own.shape
    for row in range(rows_x):
        rim[row, 4:8, :] = before[row]
        rim[row, 8 : 8 + rows_y, :] = own[row]
        rim[row, 8 + rows_y : 12 + rows_y, :] = after[row]
    for row in range(rows_x):
        summed = taps[1, 0, 0] * rim[row, 4 : 4 + rows_y, :]
        for tap in range(1, 9):
            summed = summed + taps[1, 0, tap] * rim[row, 4 + tap : 4 + tap + rows_y, :]
        total = taps[2, 0, 4] * summed
        for tap in (0, 1, 2, 3, 5, 6, 7, 8):
            total = total + taps[2, 0, tap] * pltpu.roll(summed, (4 - tap) % depth, 1)
        result[row] = total


def in_vmem(count):
    return [pl.BlockSpec(memory_space=pltpu.VMEM)] * count


scalars = pl.BlockSpec(memory_space=pltpu.SMEM)
far = pl.BlockSpec(memory_space=pltpu.HBM)


def shape_of(*shape, dtype=jnp.float32):
    return jax.ShapeDtypeStruct(shape, dtype)


def call(kernel, outs, in_specs, scratch=(), out_specs=None, limit=16, flops=0, moved=0):
    if out_specs is None:
        out_specs = jax.tree.map(lambda _: pl.BlockSpec(memory_space=pltpu.VMEM), outs)
    return pl.pallas_call(
        kernel,
        out_shape=outs,
        in_specs=in_specs,
        out_specs=out_specs,
        scratch_shapes=list(scratch),
        compiler_params=pltpu.CompilerParams(vmem_limit_bytes=limit * 2**20),
        cost_estimate=pl.CostEstimate(flops=flops, bytes_accessed=moved, transcendentals=0),
    )


def per_device(charges, kernel_taps):
    count_x, count_y = lax.axis_size("gx"), lax.axis_size("gy")
    rows_x, rows_y, depth = charges.shape
    taps = jnp.transpose(kernel_taps, (1, 0, 2))
    both = ("gx", "gy")
    downs = [restrict_1d(level) for level in range(3)]
    ups = [prolong_1d(level) for level in range(3)]
    down_constants = np.concatenate(
        [
            padded(np.kron(downs[0], downs[0]), lanes, rows_x * rows_y),
            restrict_window(lanes, 512, 128),
            restrict_window(lanes, 384, 64),
            padded(np.kron(downs[1].T, downs[1].T), lanes, lanes),
            padded(np.kron(downs[2].T, downs[2].T), lanes, lanes),
        ],
        axis=1,
    )
    down_constants = jnp.asarray(down_constants, jnp.bfloat16)

    def twice(matrix, axis):
        return np.concatenate([matrix, matrix], axis=axis)

    up_1, up_2, up_3 = (
        padded(matrix, rows, lanes)
        for matrix, rows in (
            (np.kron(ups[0], ups[0]), 256),
            (np.kron(ups[1].T, ups[1].T), lanes),
            (np.kron(ups[2].T, ups[2].T), lanes),
        )
    )
    up_constants = jnp.asarray(
        np.concatenate(
            [twice(up_3, 0), twice(up_2, 0), twice(up_1, 1), prolong_window(256, 256, 64)], axis=1
        ),
        jnp.bfloat16,
    )
    sections, section_count = weight_sections(count_x, count_y)
    block_shape = (lanes * rows_per_block, lanes)
    exchange_shape = (lanes, rows_per_block, lanes)

    blocks, head, tail = call(
        restrict_kernel,
        (
            shape_of(*block_shape),
            shape_of(4, rows_y, depth),
            shape_of(4, rows_y, depth),
        ),
        [far] * 3,
        [
            pltpu.SMEM(taps.shape, jnp.float32),
            pltpu.VMEM((rows_x, rows_y, depth), jnp.float32),
            pltpu.VMEM(down_constants.shape, jnp.bfloat16),
            pltpu.VMEM((2 * lanes, depth + 2 * lanes), jnp.bfloat16),
            pltpu.VMEM((depth // 2 + 16, lanes), jnp.float32),
            pltpu.VMEM(block_shape, jnp.float32),
            pltpu.SemaphoreType.DMA((8 + depth // 256,)),
        ],
        (far,) * 3,
        limit=60,
        flops=10**9,
        moved=2 * 10**6,
    )(taps, charges, down_constants)
    received = lax.all_to_all(blocks.reshape(exchange_shape), both, 0, 0, tiled=True)

    weights = call(
        lambda *refs: weight_kernel(sections, *refs),
        shape_of(section_count * lanes, 2 * lanes, dtype=jnp.bfloat16),
        [scalars] + in_vmem(1),
        flops=2 * 10**7,
        moved=3 * 10**6,
    )(taps, tap_tables())

    def shifted(values, axis, step):
        count = lax.axis_size(axis)
        return lax.ppermute(values, axis, [(i, (i + step) % count) for i in range(count)])

    before = shifted(tail, "gx", 1)
    after = shifted(head, "gx", -1)
    summed, head, tail = call(
        convolve_x_kernel,
        (shape_of(rows_x, rows_y, depth), shape_of(rows_x, 4, depth), shape_of(rows_x, 4, depth)),
        [scalars] + in_vmem(3),
        flops=10**11,
        moved=3 * 10**6,
    )(taps, before, charges, after)
    received, _ = lax.optimization_barrier((received, tail))
    finest = call(
        convolve_yz_kernel,
        shape_of(rows_x, rows_y, depth),
        [scalars] + in_vmem(3),
        [pltpu.VMEM((rows_x, rows_y + 16, depth), jnp.float32)],
        flops=10**11,
        moved=3 * 10**6,
    )(taps, shifted(tail, "gy", 1), summed, shifted(head, "gy", -1))

    blocks = call(
        lambda *refs: convolve_kernel(sections, count_x, count_y, *refs),
        shape_of(*block_shape),
        in_vmem(2),
        flops=10**9,
        moved=4 * 10**6,
    )(received.reshape(block_shape), weights)
    received = lax.all_to_all(blocks.reshape(exchange_shape), both, 0, 0, tiled=True)

    return call(
        finish_kernel,
        shape_of(rows_x, rows_y, depth),
        in_vmem(3),
        [pltpu.VMEM((rows_x, rows_y, depth), jnp.float32), pltpu.SemaphoreType.DMA((depth // 256,))],
        far,
        flops=10**9,
        moved=4 * 10**6,
    )(received.reshape(block_shape), up_constants, finest)


def solution(mesh):
    placed = (P("gx", "gy", None), P())
    return jax.shard_map(
        per_device, mesh=mesh, in_specs=placed, out_specs=P("gx", "gy", None), check_vma=False
    )
```

time: 65.4 us -> 56.1 us (0.86)
  local copies, waits for them, and re-layouts: 8.17 us -> 2.99 us
  waiting for transfers between devices: 16.8 us -> 12.9 us
    ppermute x4, waiting for transfers between devices: 8.08 us -> 0.01 us  [shifted(): lax.ppermute(values, axis, [(i, (i + step) % count) for i in range(count)])]
    unnamed x27 -> x14, local copies, waits for them, and re-layouts: 7.31 us -> 2.99 us
    all_to_all x2, waiting for transfers between devices: 8.67 us -> 12.9 us  [per_device(): lax.all_to_all(blocks.reshape(exchange_shape), both, 0, 0, tiled=True)]
    pallas_call x1, Pallas kernels: 2.63 us -> 1.46 us  [per_device(): call(lambda *refs: weight_kernel(sections, *refs), shape_of(section_count...]
    slice x1 -> x0, local copies, waits for them, and re-layouts: 0.85 us -> none  [per_device(): after = shifted(charges[:4], 'gx', -1)]
    ppermute x4, starting transfers between devices: 7.04 us -> 7.85 us  [shifted(): lax.ppermute(values, axis, [(i, (i + step) % count) for i in range(count)])]
    pallas_call x2, Pallas kernels: 5.86 us -> 6.62 us  [the longest x1 4.51 us: per_device(): call(restrict_kernel, (shape_of(*block_shape), shape_of(4, rows_y, depth)...]
  transfers between devices with their start and end apart: 6 -> 6, of which waited for: 2 -> 2; matrix products, arithmetic and copies ran while one was open for 1% -> 0% of each run, Pallas kernels for 17% -> 18%
where the time goes in v2:
time: 56.1 us; the launch traced here: 55.8 us
  starting transfers between devices  23.1 us (41%)
  Pallas kernels  16.7 us (30%)
  waiting for transfers between devices  12.9 us (23%)
  local copies, waits for them, and re-layouts  2.99 us (5%)
    all_to_all x2, starting transfers between devices, per_device(): lax.all_to_all(blocks.reshape(exchange_shape), both, 0, 0, tiled=True)  15.3 us
    all_to_all x2, waiting for transfers between devices, per_device(): lax.all_to_all(blocks.reshape(exchange_shape), both, 0, 0, tiled=True)  12.9 us
    ppermute x4, starting transfers between devices, shifted(): lax.ppermute(values, axis, [(i, (i + step) % count) for i in range(count)])  7.85 us
    pallas_call x1, Pallas kernels, per_device(): call(convolve_yz_kernel, shape_of(rows_x, rows_y, depth), [scalars] + in_...  4.55 us
    pallas_call x1, Pallas kernels, per_device(): call(restrict_kernel, (shape_of(*block_shape), shape_of(4, rows_y, depth)...  4.51 us
    unnamed x14, local copies, waits for them, and re-layouts  2.99 us
    pallas_call x1, Pallas kernels, per_device(): call(lambda *refs: convolve_kernel(sections, count_x, count_y, *refs), sh...  2.32 us
    pallas_call x1, Pallas kernels, per_device(): call(finish_kernel, shape_of(rows_x, rows_y, depth), in_vmem(3), [pltpu.V...  2.11 us
  transfers between devices with their start and end apart: 6, of which 2 were waited for; matrix products, arithmetic and copies ran while one was open for 0% of the time, Pallas kernels for 18%

profile of v2, /device:TPU:1, one launch (start us, length us, event | category | flops | bytes accessed | tf_op | source)
XLA Modules:
  0.0 55.8 jit_solution(13059196276624476950)
XLA Ops:
  0.0 0.0 copy-start.3
  0.0 0.0 copy-start.2
  0.0 4.5 %shard_map.55 = (f32[1024,128]{1,0:T(8,128)}, f32[4,16,1024]{2,1,0:T(8,128)}, f32[4,16,1024]{2,1,0:T(8,128)}) custom-call(f32[3,4,9]{2,1,0:T(4,128)} %bitcast.8, f32[16,16,1024]{2,1,0:T(8,128)} %own.1, bf16[128,1408]{1,0:T(8,128)(2,1)} %constant.6.clone.constants_far), custom_call_target="tpu_custom_call" | custom-call | flops 1000000000 | bytes 2000000 | tf_op jit(solution)/shard_map/pallas_call | solution.py:394
  4.5 3.0 %collective-permute-start = (f32[4,16,1024]{2,1,0:T(8,128)}, f32[4,16,1024]{2,1,0:T(8,128)S(1)}, u32[]{:S(2)}, u32[]{:S(2)}) collective-permute-start(f32[4,16,1024]{2,1,0:T(8,128)} %get-tuple-element.13), channel_id=1, source_target_pairs={{0,16},{16,32},{32,48},{48,64},{64,80},{80,96},{96,112},{112,0},{1... | collective-permute-start | bytes 786440 | tf_op jit(solution)/shard_map/ppermute | solution.py:428
  7.6 0.0 collective-permute-start.1
  7.6 10.2 %all-to-all-start = ((f32[128,8,128]{2,1,0:T(8,128)}), f32[128,8,128]{2,1,0:T(8,128)S(1)}, u32[]{:S(2)}, u32[]{:S(2)}) async-start(f32[128,8,128]{2,1,0:T(8,128)} %bitcast.12), calls=%async_computation | async-start | bytes 1048576 | tf_op jit(solution)/shard_map/all_to_all | solution.py:416
  17.8 0.0 copy-start.1
  17.8 0.0 collective-permute-done.before
  17.8 0.0 collective-permute-done.1.after
  17.8 0.0 copy-done.3
  17.8 0.0 copy-done.2
  17.8 1.7 %shard_map.56 = (f32[16,16,1024]{2,1,0:T(8,128)S(1)}, f32[16,4,1024]{2,1,0:T(4,128)}, f32[16,4,1024]{2,1,0:T(4,128)S(1)}) custom-call(f32[3,4,9]{2,1,0:T(4,128)S(1)} %bitcast.9, f32[4,16,1024]{2,1,0:T(8,128)S(1)} %collective-permute-done.before, f32[16,16,1024]{2,1,0:T(8,128)S(1)} %copy-done.3, f32[4,16,1024]{2,1,0:T(8,128)S(1)} %collective-permute-done.1.after), custom_call_target="tpu_custom_call" | custom-call | flops 99999997952 | bytes 3000000 | tf_op jit(solution)/shard_map/pallas_call | solution.py:432
  19.6 0.0 copy-start.5
  19.6 1.0 %copy-done.5 = f32[16,16,1024]{2,1,0:T(8,128)} copy-done((f32[16,16,1024]{2,1,0:T(8,128)}, f32[16,16,1024]{2,1,0:T(8,128)S(1)}, u32[]{:S(2)}) %copy-start.5) | copy-done | bytes 1048600
  20.5 4.8 %collective-permute-start.3 = (f32[16,4,1024]{2,1,0:T(4,128)}, f32[16,4,1024]{2,1,0:T(4,128)}, u32[]{:S(2)}, u32[]{:S(2)}) collective-permute-start(f32[16,4,1024]{2,1,0:T(4,128)} %get-tuple-element.18), channel_id=1, source_target_pairs={{0,15},{1,0},{2,1},{3,2},{4,3},{5,4},{6,5},{7,6},{8,7},{9,8},{10,9... | collective-permute-start | bytes 786440 | tf_op jit(solution)/shard_map/ppermute | solution.py:428
  25.4 0.0 collective-permute-start.2
  25.4 0.0 copy-done.1
  25.4 1.5 %shard_map.57.refs_1_ = bf16[4992,256]{1,0:T(8,128)(2,1)S(1)} custom-call(f32[3,4,9]{2,1,0:T(4,128)S(1)} %bitcast.10, bf16[1632,128]{1,0:T(8,128)(2,1)S(1)} %copy-done.1), custom_call_target="tpu_custom_call" | custom-call | flops 20000000 | bytes 3000000 | tf_op jit(solution)/shard_map/pallas_call | solution.py:418
  26.8 4.8 %all-to-all-done = f32[128,8,128]{2,1,0:T(8,128)S(1)} async-done(((f32[128,8,128]{2,1,0:T(8,128)}), f32[128,8,128]{2,1,0:T(8,128)S(1)}, u32[]{:S(2)}, u32[]{:S(2)}) %all-to-all-start) | async-done | bytes 524320 | tf_op jit(solution)/shard_map/all_to_all | solution.py:416
  31.6 2.3 %shard_map.58 = f32[1024,128]{1,0:T(8,128)S(1)} custom-call(f32[1024,128]{1,0:T(8,128)S(1)} %bitcast.5, bf16[4992,256]{1,0:T(8,128)(2,1)S(1)} %shard_map.57.refs_1_), custom_call_target="tpu_custom_call" | custom-call | flops 1000000000 | bytes 4000000 | tf_op jit(solution)/shard_map/pallas_call | solution.py:449
  33.9 0.0 copy-start
  33.9 0.8 %copy-done = f32[1024,128]{1,0:T(8,128)} copy-done((f32[1024,128]{1,0:T(8,128)}, f32[1024,128]{1,0:T(8,128)S(1)}, u32[]{:S(2)}) %copy-start) | copy-done | bytes 524312
  34.7 5.0 %all-to-all-start.1 = ((f32[128,8,128]{2,1,0:T(8,128)}), f32[128,8,128]{2,1,0:T(8,128)S(1)}, u32[]{:S(2)}, u32[]{:S(2)}) async-start(f32[128,8,128]{2,1,0:T(8,128)} %bitcast.7), calls=%async_computation.1 | async-start | bytes 1048576 | tf_op jit(solution)/shard_map/all_to_all | solution.py:456
  39.8 0.0 collective-permute-done.3.after
  39.8 0.0 collective-permute-done.2.before
  39.8 0.0 copy-start.6
  39.8 1.2 %copy-done.6 = f32[16,16,1024]{2,1,0:T(8,128)S(1)} copy-done((f32[16,16,1024]{2,1,0:T(8,128)S(1)}, f32[16,16,1024]{2,1,0:T(8,128)}, u32[]{:S(2)}) %copy-start.6) | copy-done | bytes 1048600
  41.0 0.0 copy-start.4
  41.0 4.6 %shard_map.59.finest = f32[16,16,1024]{2,1,0:T(8,128)S(1)} custom-call(f32[3,4,9]{2,1,0:T(4,128)S(1)} %bitcast.11, f32[16,4,1024]{2,1,0:T(4,128)} %collective-permute-done.2.before, f32[16,16,1024]{2,1,0:T(8,128)S(1)} %copy-done.6, f32[16,4,1024]{2,1,0:T(4,128)} %collective-permute-done.3.after), custom_call_target="tpu_custom_call" | custom-call | flops 99999997952 | bytes 3000000 | tf_op jit(solution)/shard_map/pallas_call | solution.py:440
  45.6 8.1 %all-to-all-done.1 = f32[128,8,128]{2,1,0:T(8,128)S(1)} async-done(((f32[128,8,128]{2,1,0:T(8,128)}), f32[128,8,128]{2,1,0:T(8,128)S(1)}, u32[]{:S(2)}, u32[]{:S(2)}) %all-to-all-start.1) | async-done | bytes 524320 | tf_op jit(solution)/shard_map/all_to_all | solution.py:456
  53.7 0.0 copy-done.4
  53.7 2.1 %shard_map.60 = f32[16,16,1024]{2,1,0:T(8,128)} custom-call(f32[1024,128]{1,0:T(8,128)S(1)} %bitcast.6, bf16[256,768]{1,0:T(8,128)(2,1)S(1)} %copy-done.4, f32[16,16,1024]{2,1,0:T(8,128)S(1)} %shard_map.59.finest), custom_call_target="tpu_custom_call" | custom-call | flops 1000000000 | bytes 4000000 | tf_op jit(solution)/shard_map/pallas_call | solution.py:458
Async XLA Ops:
  0.0 17.8 %copy-start.3 = (f32[16,16,1024]{2,1,0:T(8,128)S(1)}, f32[16,16,1024]{2,1,0:T(8,128)}, u32[]{:S(2)}) copy-start(f32[16,16,1024]{2,1,0:T(8,128)} %own.1) | copy-start | bytes 3145732
  0.0 17.8 %copy-start.2 = (f32[4,3,9]{2,0,1:T(4,128)S(1)}, f32[4,3,9]{2,0,1:T(4,128)}, u32[]{:S(2)}) copy-start(f32[4,3,9]{2,0,1:T(4,128)} %param.6) | copy-start | bytes 1300
  4.5 13.3 %collective-permute-start = (f32[4,16,1024]{2,1,0:T(8,128)}, f32[4,16,1024]{2,1,0:T(8,128)S(1)}, u32[]{:S(2)}, u32[]{:S(2)}) collective-permute-start(f32[4,16,1024]{2,1,0:T(8,128)} %get-tuple-element.13), channel_id=1, source_target_pairs={{0,16},{16,32},{32,48},{48,64},{64,80},{80,96},{96,112},{112,0},{1... | collective-permute-start | bytes 786440 | tf_op jit(solution)/shard_map/ppermute | solution.py:428
  7.6 10.3 %collective-permute-start.1 = (f32[4,16,1024]{2,1,0:T(8,128)}, f32[4,16,1024]{2,1,0:T(8,128)S(1)}, u32[]{:S(2)}, u32[]{:S(2)}) collective-permute-start(f32[4,16,1024]{2,1,0:T(8,128)} %get-tuple-element.14), channel_id=1, source_target_pairs={{0,112},{16,0},{32,16},{48,32},{64,48},{80,64},{96,80},{112,96},{1... | collective-permute-start | bytes 786440 | tf_op jit(solution)/shard_map/ppermute | solution.py:428
  7.6 24.0 %all-to-all-start = ((f32[128,8,128]{2,1,0:T(8,128)}), f32[128,8,128]{2,1,0:T(8,128)S(1)}, u32[]{:S(2)}, u32[]{:S(2)}) async-start(f32[128,8,128]{2,1,0:T(8,128)} %bitcast.12), calls=%async_computation | async-start | bytes 1048576 | tf_op jit(solution)/shard_map/all_to_all | solution.py:416
  17.8 7.6 %copy-start.1 = (bf16[1632,128]{1,0:T(8,128)(2,1)S(1)}, bf16[1632,128]{1,0:T(8,128)(2,1)}, u32[]{:S(2)}) copy-start(bf16[1632,128]{1,0:T(8,128)(2,1)} %constant.8.clone.refs_1_) | copy-start | bytes 1253380
  19.6 1.0 %copy-start.5 = (f32[16,16,1024]{2,1,0:T(8,128)}, f32[16,16,1024]{2,1,0:T(8,128)S(1)}, u32[]{:S(2)}) copy-start(f32[16,16,1024]{2,1,0:T(8,128)S(1)} %get-tuple-element.17.own) | copy-start | bytes 3145732
  20.5 19.2 %collective-permute-start.3 = (f32[16,4,1024]{2,1,0:T(4,128)}, f32[16,4,1024]{2,1,0:T(4,128)}, u32[]{:S(2)}, u32[]{:S(2)}) collective-permute-start(f32[16,4,1024]{2,1,0:T(4,128)} %get-tuple-element.18), channel_id=1, source_target_pairs={{0,15},{1,0},{2,1},{3,2},{4,3},{5,4},{6,5},{7,6},{8,7},{9,8},{10,9... | collective-permute-start | bytes 786440 | tf_op jit(solution)/shard_map/ppermute | solution.py:428
  25.4 14.4 %collective-permute-start.2 = (f32[16,4,1024]{2,1,0:T(4,128)S(1)}, f32[16,4,1024]{2,1,0:T(4,128)}, u32[]{:S(2)}, u32[]{:S(2)}) collective-permute-start(f32[16,4,1024]{2,1,0:T(4,128)S(1)} %get-tuple-element.15), channel_id=1, source_target_pairs={{0,1},{1,2},{2,3},{3,4},{4,5},{5,6},{6,7},{7,8},{8,9},{9,10},{10,1... | collective-permute-start | bytes 786440 | tf_op jit(solution)/shard_map/ppermute | solution.py:428
  33.9 0.8 %copy-start = (f32[1024,128]{1,0:T(8,128)}, f32[1024,128]{1,0:T(8,128)S(1)}, u32[]{:S(2)}) copy-start(f32[1024,128]{1,0:T(8,128)S(1)} %shard_map.58) | copy-start | bytes 1572868
  34.7 19.0 %all-to-all-start.1 = ((f32[128,8,128]{2,1,0:T(8,128)}), f32[128,8,128]{2,1,0:T(8,128)S(1)}, u32[]{:S(2)}, u32[]{:S(2)}) async-start(f32[128,8,128]{2,1,0:T(8,128)} %bitcast.7), calls=%async_computation.1 | async-start | bytes 1048576 | tf_op jit(solution)/shard_map/all_to_all | solution.py:456
  39.8 1.2 %copy-start.6 = (f32[16,16,1024]{2,1,0:T(8,128)S(1)}, f32[16,16,1024]{2,1,0:T(8,128)}, u32[]{:S(2)}) copy-start(f32[16,16,1024]{2,1,0:T(8,128)} %copy-done.5) | copy-start | bytes 3145732
  41.0 12.7 %copy-start.4 = (bf16[256,768]{1,0:T(8,128)(2,1)S(1)}, bf16[256,768]{1,0:T(8,128)(2,1)}, u32[]{:S(2)}) copy-start(bf16[256,768]{1,0:T(8,128)(2,1)} %constant.7.clone.constants) | copy-start | bytes 1179652

commit v3 on v2

--- a/solution.py
+++ b/solution.py
@@ -12,7 +12,7 @@
 restrict_taps = {-3: -0.0625, -1: 0.5625, 0: 1.0, 1: 0.5625, 3: -0.0625}
 lanes = 128
 block_rows = ((), (0, 1, 2, 3), (4, 5), (6,))
-rows_per_block = 8
+rows_per_block = 7
 
 
 def restrict_1d(level):
@@ -58,6 +58,14 @@
     for fine in range(rows):
         for coarse, weight in prolong_entries(fine).items():
             matrix[fine, margin + coarse] = weight
+    return matrix
+
+
+def prolong_ring(rows):
+    matrix = np.zeros((rows, rows // 2), np.float32)
+    for fine in range(rows):
+        for coarse, weight in prolong_entries(fine).items():
+            matrix[fine, coarse % (rows // 2)] = weight
     return matrix
 
 
@@ -172,30 +180,34 @@
         ],
         axis=0,
     )
-    copies[1].wait()
-    for level in (1, 2, 3):
+    grids = {1: grid}
+    for level in (1, 2):
         cells = grid.shape[0]
-        rim[0:8, :] = grid[cells - 8 :, :]
-        rim[8 : 8 + cells, :] = grid
-        rim[8 + cells : 16 + cells, :] = grid[:8, :]
-        for index, row in enumerate(block_rows[level]):
-            summed = None
-            for tap in range(9):
-                begin = lanes * index + 4 + tap
-                term = taps[2, level, tap] * rim[begin : begin + lanes, :]
-                summed = term if summed is None else summed + term
-            blocks[pl.ds(row, lanes, stride=rows_per_block), :] = summed
-        if level == 3:
-            break
         down = constants[:, 1024 + 128 * level : 1152 + 128 * level]
         grid = dot(side_by_side(grid), jnp.concatenate([down, down], axis=0))
         ready = wrapped(side_by_side(grid), 64, 0)
         grid = jnp.concatenate(
             [both_ways(dot(row_window, ready[begin : begin + 384])) for begin in range(0, cells, 256)], axis=0
         )
-    blocks[pl.ds(7, lanes, stride=rows_per_block), :] = jnp.zeros((lanes, lanes), jnp.float32)
+        grids[level + 1] = grid
+    copies[1].wait()
+    first = 0
+    for level in (1, 2, 3):
+        grid = grids[level]
+        cells = grid.shape[0]
+        rim[first : first + 8, :] = grid[cells - 8 :, :]
+        rim[first + 8 : first + 8 + cells, :] = grid
+        rim[first + 8 + cells : first + 16 + cells, :] = grid[:8, :]
+        for index, row in enumerate(block_rows[level]):
+            summed = None
+            for tap in range(9):
+                begin = first + lanes * index + 4 + tap
+                term = taps[2, level, tap] * rim[begin : begin + lanes, :]
+                summed = term if summed is None else summed + term
+            blocks[pl.ds(row, lanes, stride=rows_per_block), :] = summed
+        first += cells + 16
     for index in range(4):
-        section = pl.ds(256 * index, 256)
+        section = pl.ds(224 * index, 224)
         leaving.append(
             pltpu.make_async_copy(blocks.at[section], blocks_far.at[section], arrived.at[4 + depth // 256 + index])
         )
@@ -232,7 +244,8 @@
     return product[:half] + product[half:]
 
 
-def convolve_kernel(sections, count_x, count_y, received, weights, blocks):
+def convolve_kernel(sections, count_x, count_y, received, weights, blocks_far, blocks, left):
+    columns = {}
     for level in (1, 2, 3):
         slices = len(block_rows[level])
         values = jnp.concatenate(
@@ -245,9 +258,11 @@
             turn = offset % count_x
             turned = jnp.concatenate([stack[:, turn:], stack[:, :turn]], axis=1) if turn else stack
             pieces.append(turned.reshape(2 * slices * lanes, lanes))
-        values = weighted(pieces, weights, start)
+        columns[level] = weighted(pieces, weights, start)
+    for level in (1, 2, 3):
+        slices = len(block_rows[level])
         start, offsets = sections[level, 1]
-        stack = values.reshape(slices * count_x, count_y, lanes)
+        stack = columns[level].reshape(slices * count_x, count_y, lanes)
         pieces = []
         for offset in offsets:
             turn = offset % count_y
@@ -256,26 +271,37 @@
         values = weighted(pieces, weights, start)
         for index, row in enumerate(block_rows[level]):
             blocks[pl.ds(row, lanes, stride=rows_per_block), :] = values[lanes * index : lanes * (index + 1)]
-    blocks[pl.ds(7, lanes, stride=rows_per_block), :] = jnp.zeros((lanes, lanes), jnp.float32)
-
-
-def finish_kernel(received, constants, finest, potential, ready, left):
+    copies = []
+    for index in range(4):
+        section = pl.ds(224 * index, 224)
+        copies.append(pltpu.make_async_copy(blocks.at[section], blocks_far.at[section], left.at[index]))
+        copies[-1].start()
+    for copy in copies:
+        copy.wait()
+
+
+def finish_kernel(received, constants, twice_up, finest, potential, ready, left):
     rows_x, rows_y, depth = finest.shape
     row_window = constants[:, 512:768]
-    running = received[pl.ds(block_rows[3][0], lanes, stride=rows_per_block), :]
-    for level in (2, 1):
-        own = jnp.concatenate(
+    parts = {
+        level: jnp.concatenate(
             [received[pl.ds(row, lanes, stride=rows_per_block), :] for row in block_rows[level]], axis=0
         )
-        up = constants[:, 128 * (2 - level) : 128 * (3 - level)]
-        pairs = wrapped(side_by_side(dot(side_by_side(running), up)), 64, 0)
-        running = own + jnp.concatenate(
-            [
-                both_ways(dot(row_window, pairs[begin : begin + 256]))
-                for begin in range(0, running.shape[0], lanes)
-            ],
-            axis=0,
-        )
+        for level in (1, 2, 3)
+    }
+    high, low = split(parts[3])
+    coarsest = dot(jnp.concatenate([high, low, high], axis=1), twice_up[0 : 3 * lanes, :])
+    middle = dot(side_by_side(parts[2]), constants[:, 128:256])
+    coarsest = both_ways(dot(twice_up[3 * lanes :, :], side_by_side(coarsest)))
+    pairs = wrapped(side_by_side(middle), 64, 0)
+    middle = jnp.concatenate(
+        [
+            both_ways(dot(row_window, pairs[begin : begin + 256]))
+            for begin in range(0, 2 * lanes, lanes)
+        ],
+        axis=0,
+    )
+    running = parts[1] + middle + coarsest
     pairs = wrapped(side_by_side(running), 64, 0)
     copies = []
     for index in range(depth // 256):
@@ -387,9 +413,17 @@
         ),
         jnp.bfloat16,
     )
+    both_ups = padded(np.kron((ups[1] @ ups[2]).T, (ups[1] @ ups[2]).T), lanes, lanes)
+    rounded = both_ups.astype(jnp.bfloat16).astype(np.float32)
+    twice_up = jnp.asarray(
+        np.concatenate(
+            [rounded, rounded, both_ups - rounded, prolong_ring(4 * lanes) @ prolong_ring(2 * lanes)], axis=0
+        ),
+        jnp.bfloat16,
+    )
     sections, section_count = weight_sections(count_x, count_y)
     block_shape = (lanes * rows_per_block, lanes)
-    exchange_shape = (lanes, rows_per_block, lanes)
+    exchange_shape = (lanes * rows_per_block, 1, lanes)
 
     blocks, head, tail = call(
         restrict_kernel,
@@ -404,7 +438,7 @@
             pltpu.VMEM((rows_x, rows_y, depth), jnp.float32),
             pltpu.VMEM(down_constants.shape, jnp.bfloat16),
             pltpu.VMEM((2 * lanes, depth + 2 * lanes), jnp.bfloat16),
-            pltpu.VMEM((depth // 2 + 16, lanes), jnp.float32),
+            pltpu.VMEM((7 * lanes + 48, lanes), jnp.float32),
             pltpu.VMEM(block_shape, jnp.float32),
             pltpu.SemaphoreType.DMA((8 + depth // 256,)),
         ],
@@ -450,6 +484,8 @@
         lambda *refs: convolve_kernel(sections, count_x, count_y, *refs),
         shape_of(*block_shape),
         in_vmem(2),
+        [pltpu.VMEM(block_shape, jnp.float32), pltpu.SemaphoreType.DMA((4,))],
+        far,
         flops=10**9,
         moved=4 * 10**6,
     )(received.reshape(block_shape), weights)
@@ -458,12 +494,12 @@
     return call(
         finish_kernel,
         shape_of(rows_x, rows_y, depth),
-        in_vmem(3),
+        in_vmem(4),
         [pltpu.VMEM((rows_x, rows_y, depth), jnp.float32), pltpu.SemaphoreType.DMA((depth // 256,))],
         far,
         flops=10**9,
         moved=4 * 10**6,
-    )(received.reshape(block_shape), up_constants, finest)
+    )(received.reshape(block_shape), up_constants, twice_up, finest)
 
 
 def solution(mesh):

time: 56.1 us -> 54.5 us (0.971)
  waiting for transfers between devices: 12.9 us -> 11.7 us
  local copies, waits for them, and re-layouts: 2.99 us -> 2.21 us
    all_to_all x2, waiting for transfers between devices: 12.9 us -> 11.7 us  [per_device(): lax.all_to_all(blocks.reshape(exchange_shape), both, 0, 0, tiled=True)]
    unnamed x14, local copies, waits for them, and re-layouts: 2.99 us -> 2.21 us
  transfers between devices with their start and end apart: 6 -> 6, of which waited for: 2 -> 2; matrix products, arithmetic and copies ran while one was open for 0% -> 0% of each run, Pallas kernels for 18% -> 19%
where the time goes in v3:
time: 54.5 us; the launch traced here: 54.2 us
  starting transfers between devices  23.6 us (43%)
  Pallas kernels  16.5 us (30%)
  waiting for transfers between devices  11.7 us (21%)
  local copies, waits for them, and re-layouts  2.21 us (4%)
    all_to_all x2, starting transfers between devices, per_device(): lax.all_to_all(blocks.reshape(exchange_shape), both, 0, 0, tiled=True)  15.8 us
    all_to_all x2, waiting for transfers between devices, per_device(): lax.all_to_all(blocks.reshape(exchange_shape), both, 0, 0, tiled=True)  11.7 us
    ppermute x4, starting transfers between devices, shifted(): lax.ppermute(values, axis, [(i, (i + step) % count) for i in range(count)])  7.85 us
    pallas_call x1, Pallas kernels, per_device(): call(convolve_yz_kernel, shape_of(rows_x, rows_y, depth), [scalars] + in_...  4.49 us
    pallas_call x1, Pallas kernels, per_device(): call(restrict_kernel, (shape_of(*block_shape), shape_of(4, rows_y, depth)...  4.43 us
    pallas_call x1, Pallas kernels, per_device(): call(lambda *refs: convolve_kernel(sections, count_x, count_y, *refs), sh...  2.47 us
    unnamed x14, local copies, waits for them, and re-layouts  2.21 us
    pallas_call x1, Pallas kernels, per_device(): call(finish_kernel, shape_of(rows_x, rows_y, depth), in_vmem(4), [pltpu.V...  1.9 us
  transfers between devices with their start and end apart: 6, of which 2 were waited for; matrix products, arithmetic and copies ran while one was open for 0% of the time, Pallas kernels for 19%

profile of v3, /device:TPU:1, one launch (start us, length us, event | category | flops | bytes accessed | tf_op | source)
XLA Modules:
  0.0 54.2 jit_solution(2637216929401697115)
XLA Ops:
  0.0 0.0 copy-start.2
  0.0 0.0 copy-start.1
  0.0 4.4 %shard_map.64 = (f32[896,128]{1,0:T(8,128)}, f32[4,16,1024]{2,1,0:T(8,128)}, f32[4,16,1024]{2,1,0:T(8,128)}) custom-call(f32[3,4,9]{2,1,0:T(4,128)} %bitcast.11, f32[16,16,1024]{2,1,0:T(8,128)} %own.1, bf16[128,1408]{1,0:T(8,128)(2,1)} %constant.8.clone.constants_far), custom_call_target="tpu_custom_call" | custom-call | flops 1000000000 | bytes 2000000 | tf_op jit(solution)/shard_map/pallas_call | solution.py:428
  4.4 3.0 %collective-permute-start = (f32[4,16,1024]{2,1,0:T(8,128)}, f32[4,16,1024]{2,1,0:T(8,128)S(1)}, u32[]{:S(2)}, u32[]{:S(2)}) collective-permute-start(f32[4,16,1024]{2,1,0:T(8,128)} %get-tuple-element.13), channel_id=1, source_target_pairs={{0,16},{16,32},{32,48},{48,64},{64,80},{80,96},{96,112},{112,0},{1... | collective-permute-start | bytes 786440 | tf_op jit(solution)/shard_map/ppermute | solution.py:462
  7.5 0.0 collective-permute-start.1
  7.5 10.2 %all-to-all-start = ((f32[896,1,128]{2,1,0:T(1,128)}), f32[896,1,128]{2,1,0:T(1,128)S(1)}, u32[]{:S(2)}, u32[]{:S(2)}) async-start(f32[896,1,128]{2,1,0:T(1,128)} %bitcast.15), calls=%async_computation | async-start | bytes 917504 | tf_op jit(solution)/shard_map/all_to_all | solution.py:450
  17.7 0.0 copy-start
  17.7 0.0 collective-permute-done.before
  17.7 0.0 collective-permute-done.1.after
  17.7 0.0 copy-done.2
  17.8 0.0 copy-done.1
  17.8 1.7 %shard_map.65 = (f32[16,16,1024]{2,1,0:T(8,128)S(1)}, f32[16,4,1024]{2,1,0:T(4,128)}, f32[16,4,1024]{2,1,0:T(4,128)S(1)}) custom-call(f32[3,4,9]{2,1,0:T(4,128)S(1)} %bitcast.12, f32[4,16,1024]{2,1,0:T(8,128)S(1)} %collective-permute-done.before, f32[16,16,1024]{2,1,0:T(8,128)S(1)} %copy-done.2, f32[4,16,1024]{2,1,0:T(8,128)S(1)} %collective-permute-done.1.after), custom_call_target="tpu_custom_call" | custom-call | flops 99999997952 | bytes 3000000 | tf_op jit(solution)/shard_map/pallas_call | solution.py:466
  19.5 0.0 copy-start.5
  19.5 1.0 %copy-done.5 = f32[16,16,1024]{2,1,0:T(8,128)} copy-done((f32[16,16,1024]{2,1,0:T(8,128)}, f32[16,16,1024]{2,1,0:T(8,128)S(1)}, u32[]{:S(2)}) %copy-start.5) | copy-done | bytes 1048600
  20.4 4.8 %collective-permute-start.3 = (f32[16,4,1024]{2,1,0:T(4,128)}, f32[16,4,1024]{2,1,0:T(4,128)S(1)}, u32[]{:S(2)}, u32[]{:S(2)}) collective-permute-start(f32[16,4,1024]{2,1,0:T(4,128)} %get-tuple-element.18), channel_id=1, source_target_pairs={{0,15},{1,0},{2,1},{3,2},{4,3},{5,4},{6,5},{7,6},{8,7},{9,8},{10,9... | collective-permute-start | bytes 786440 | tf_op jit(solution)/shard_map/ppermute | solution.py:462
  25.3 0.0 collective-permute-start.2
  25.3 0.0 copy-done
  25.3 1.5 %shard_map.66.refs_1_ = bf16[4992,256]{1,0:T(8,128)(2,1)S(1)} custom-call(f32[3,4,9]{2,1,0:T(4,128)S(1)} %bitcast.13, bf16[1632,128]{1,0:T(8,128)(2,1)S(1)} %copy-done), custom_call_target="tpu_custom_call" | custom-call | flops 20000000 | bytes 3000000 | tf_op jit(solution)/shard_map/pallas_call | solution.py:452
  26.7 4.2 %all-to-all-done = f32[896,1,128]{2,1,0:T(1,128)S(1)} async-done(((f32[896,1,128]{2,1,0:T(1,128)}), f32[896,1,128]{2,1,0:T(1,128)S(1)}, u32[]{:S(2)}, u32[]{:S(2)}) %all-to-all-start) | async-done | bytes 458784 | tf_op jit(solution)/shard_map/all_to_all | solution.py:450
  31.0 2.5 %shard_map.67 = f32[896,128]{1,0:T(8,128)} custom-call(f32[896,128]{1,0:T(8,128)S(1)} %bitcast.9, bf16[4992,256]{1,0:T(8,128)(2,1)S(1)} %shard_map.66.refs_1_), custom_call_target="tpu_custom_call" | custom-call | flops 1000000000 | bytes 4000000 | tf_op jit(solution)/shard_map/pallas_call | solution.py:483
  33.4 5.6 %all-to-all-start.1 = ((f32[896,1,128]{2,1,0:T(1,128)}), f32[896,1,128]{2,1,0:T(1,128)S(1)}, u32[]{:S(2)}, u32[]{:S(2)}) async-start(f32[896,1,128]{2,1,0:T(1,128)} %bitcast.5), calls=%async_computation.1 | async-start | bytes 917504 | tf_op jit(solution)/shard_map/all_to_all | solution.py:492
  39.0 0.0 collective-permute-done.3.after
  39.0 0.0 collective-permute-done.2.before
  39.0 0.0 copy-start.6
  39.0 1.2 %copy-done.6 = f32[16,16,1024]{2,1,0:T(8,128)S(1)} copy-done((f32[16,16,1024]{2,1,0:T(8,128)S(1)}, f32[16,16,1024]{2,1,0:T(8,128)}, u32[]{:S(2)}) %copy-start.6) | copy-done | bytes 1048600
  40.3 0.0 copy-start.3
  40.3 0.0 copy-start.4
  40.3 4.5 %shard_map.68.finest = f32[16,16,1024]{2,1,0:T(8,128)S(1)} custom-call(f32[3,4,9]{2,1,0:T(4,128)S(1)} %bitcast.14, f32[16,4,1024]{2,1,0:T(4,128)} %collective-permute-done.2.before, f32[16,16,1024]{2,1,0:T(8,128)S(1)} %copy-done.6, f32[16,4,1024]{2,1,0:T(4,128)S(1)} %collective-permute-done.3.after), custom_call_target="tpu_custom_call" | custom-call | flops 99999997952 | bytes 3000000 | tf_op jit(solution)/shard_map/pallas_call | solution.py:474
  44.8 7.5 %all-to-all-done.1 = f32[896,1,128]{2,1,0:T(1,128)S(1)} async-done(((f32[896,1,128]{2,1,0:T(1,128)}), f32[896,1,128]{2,1,0:T(1,128)S(1)}, u32[]{:S(2)}, u32[]{:S(2)}) %all-to-all-start.1) | async-done | bytes 458784 | tf_op jit(solution)/shard_map/all_to_all | solution.py:492
  52.3 0.0 copy-done.3
  52.3 0.0 copy-done.4
  52.3 1.9 %shard_map.69 = f32[16,16,1024]{2,1,0:T(8,128)} custom-call(f32[896,128]{1,0:T(8,128)S(1)} %bitcast.10, bf16[256,768]{1,0:T(8,128)(2,1)S(1)} %copy-done.3, bf16[896,128]{1,0:T(8,128)(2,1)S(1)} %copy-done.4, f32[16,16,1024]{2,1,0:T(8,128)S(1)} %shard_map.68.finest), custom_call_target="tpu_custom_call" | custom-call | flops 1000000000 | bytes 4000000 | tf_op jit(solution)/shard_map/pallas_call | solution.py:494
Async XLA Ops:
  0.0 17.7 %copy-start.2 = (f32[16,16,1024]{2,1,0:T(8,128)S(1)}, f32[16,16,1024]{2,1,0:T(8,128)}, u32[]{:S(2)}) copy-start(f32[16,16,1024]{2,1,0:T(8,128)} %own.1) | copy-start | bytes 3145732
  0.0 17.8 %copy-start.1 = (f32[4,3,9]{2,0,1:T(4,128)S(1)}, f32[4,3,9]{2,0,1:T(4,128)}, u32[]{:S(2)}) copy-start(f32[4,3,9]{2,0,1:T(4,128)} %param.7) | copy-start | bytes 1300
  4.4 13.3 %collective-permute-start = (f32[4,16,1024]{2,1,0:T(8,128)}, f32[4,16,1024]{2,1,0:T(8,128)S(1)}, u32[]{:S(2)}, u32[]{:S(2)}) collective-permute-start(f32[4,16,1024]{2,1,0:T(8,128)} %get-tuple-element.13), channel_id=1, source_target_pairs={{0,16},{16,32},{32,48},{48,64},{64,80},{80,96},{96,112},{112,0},{1... | collective-permute-start | bytes 786440 | tf_op jit(solution)/shard_map/ppermute | solution.py:462
  7.5 10.3 %collective-permute-start.1 = (f32[4,16,1024]{2,1,0:T(8,128)}, f32[4,16,1024]{2,1,0:T(8,128)S(1)}, u32[]{:S(2)}, u32[]{:S(2)}) collective-permute-start(f32[4,16,1024]{2,1,0:T(8,128)} %get-tuple-element.14), channel_id=1, source_target_pairs={{0,112},{16,0},{32,16},{48,32},{64,48},{80,64},{96,80},{112,96},{1... | collective-permute-start | bytes 786440 | tf_op jit(solution)/shard_map/ppermute | solution.py:462
  7.5 23.5 %all-to-all-start = ((f32[896,1,128]{2,1,0:T(1,128)}), f32[896,1,128]{2,1,0:T(1,128)S(1)}, u32[]{:S(2)}, u32[]{:S(2)}) async-start(f32[896,1,128]{2,1,0:T(1,128)} %bitcast.15), calls=%async_computation | async-start | bytes 917504 | tf_op jit(solution)/shard_map/all_to_all | solution.py:450
  17.7 7.6 %copy-start = (bf16[1632,128]{1,0:T(8,128)(2,1)S(1)}, bf16[1632,128]{1,0:T(8,128)(2,1)}, u32[]{:S(2)}) copy-start(bf16[1632,128]{1,0:T(8,128)(2,1)} %constant.11.clone.refs_1_) | copy-start | bytes 1253380
  19.5 1.0 %copy-start.5 = (f32[16,16,1024]{2,1,0:T(8,128)}, f32[16,16,1024]{2,1,0:T(8,128)S(1)}, u32[]{:S(2)}) copy-start(f32[16,16,1024]{2,1,0:T(8,128)S(1)} %get-tuple-element.17.own) | copy-start | bytes 3145732
  20.4 18.6 %collective-permute-start.3 = (f32[16,4,1024]{2,1,0:T(4,128)}, f32[16,4,1024]{2,1,0:T(4,128)S(1)}, u32[]{:S(2)}, u32[]{:S(2)}) collective-permute-start(f32[16,4,1024]{2,1,0:T(4,128)} %get-tuple-element.18), channel_id=1, source_target_pairs={{0,15},{1,0},{2,1},{3,2},{4,3},{5,4},{6,5},{7,6},{8,7},{9,8},{10,9... | collective-permute-start | bytes 786440 | tf_op jit(solution)/shard_map/ppermute | solution.py:462
  25.3 13.8 %collective-permute-start.2 = (f32[16,4,1024]{2,1,0:T(4,128)S(1)}, f32[16,4,1024]{2,1,0:T(4,128)}, u32[]{:S(2)}, u32[]{:S(2)}) collective-permute-start(f32[16,4,1024]{2,1,0:T(4,128)S(1)} %get-tuple-element.15), channel_id=1, source_target_pairs={{0,1},{1,2},{2,3},{3,4},{4,5},{5,6},{6,7},{7,8},{8,9},{9,10},{10,1... | collective-permute-start | bytes 786440 | tf_op jit(solution)/shard_map/ppermute | solution.py:462
  33.4 18.8 %all-to-all-start.1 = ((f32[896,1,128]{2,1,0:T(1,128)}), f32[896,1,128]{2,1,0:T(1,128)S(1)}, u32[]{:S(2)}, u32[]{:S(2)}) async-start(f32[896,1,128]{2,1,0:T(1,128)} %bitcast.5), calls=%async_computation.1 | async-start | bytes 917504 | tf_op jit(solution)/shard_map/all_to_all | solution.py:492
  39.0 1.2 %copy-start.6 = (f32[16,16,1024]{2,1,0:T(8,128)S(1)}, f32[16,16,1024]{2,1,0:T(8,128)}, u32[]{:S(2)}) copy-start(f32[16,16,1024]{2,1,0:T(8,128)} %copy-done.5) | copy-start | bytes 3145732
  40.3 12.0 %copy-start.3 = (bf16[256,768]{1,0:T(8,128)(2,1)S(1)}, bf16[256,768]{1,0:T(8,128)(2,1)}, u32[]{:S(2)}) copy-start(bf16[256,768]{1,0:T(8,128)(2,1)} %constant.9.clone.constants) | copy-start | bytes 1179652
  40.3 12.0 %copy-start.4 = (bf16[896,128]{1,0:T(8,128)(2,1)S(1)}, bf16[896,128]{1,0:T(8,128)(2,1)}, u32[]{:S(2)}) copy-start(bf16[896,128]{1,0:T(8,128)(2,1)} %constant.10.clone.twice_up) | copy-start | bytes 688132

commit v4 on v3

--- a/solution.py
+++ b/solution.py
@@ -69,21 +69,36 @@
     return matrix
 
 
+def to_level(level):
+    down = up = np.eye(cell_count[1], dtype=np.float32)
+    for step in range(1, level):
+        down, up = restrict_1d(step) @ down, up @ prolong_1d(step)
+    return down, up
+
+
 def tap_tables():
+    count = cell_count[1]
+    cells = [divmod(cell, count) for cell in range(count * count)]
     tables = []
+    for axis in (0, 1):
+        same = np.zeros((lanes, lanes), np.float32)
+        for row, here in enumerate(cells):
+            for column, there in enumerate(cells):
+                same[row, column] = here[1 - axis] == there[1 - axis]
+        tables.append(same)
     for level in (1, 2, 3):
-        count = cell_count[level]
+        down, up = to_level(level)
+        size = cell_count[level]
         for axis in (0, 1):
-            chooser, same, number = (np.zeros((rows, lanes), np.float32) for rows in (lanes, lanes, 16))
-            number[:] = 256.0
-            for cell in range(count * count):
-                place = divmod(cell, count)
-                chooser[cell, place[axis]] = 1.0
-                for other in range(count * count):
-                    same[cell, other] = divmod(other, count)[1 - axis] == place[1 - axis]
-                for source in range(count):
-                    number[source, cell] = source - place[axis] + 4
-            tables += [chooser, same, number]
+            into, out_of = np.zeros((lanes, lanes), np.float32), np.zeros((16, lanes), np.float32)
+            number = np.full((16, lanes), 256.0, np.float32)
+            for cell, place in enumerate(cells):
+                into[cell, :size] = down[:, place[axis]]
+                out_of[:size, cell] = up[place[axis], :]
+            for source in range(size):
+                for wanted in range(size):
+                    number[source, wanted] = source - wanted + 4
+            tables += [into, out_of, number]
     return jnp.asarray(np.concatenate(tables), jnp.bfloat16)
 
 
@@ -143,8 +158,8 @@
         pltpu.make_async_copy(taps_far, taps, arrived.at[1]),
     ]
     leaving = [
-        pltpu.make_async_copy(charges.at[pl.ds(0, 4)], head, arrived.at[2]),
-        pltpu.make_async_copy(charges.at[pl.ds(rows_x - 4, 4)], tail, arrived.at[3]),
+        pltpu.make_async_copy(charges.at[:, pl.ds(0, 4)], head, arrived.at[2]),
+        pltpu.make_async_copy(charges.at[:, pl.ds(rows_y - 4, 4)], tail, arrived.at[3]),
     ]
     chunks = []
     for index in range(depth // 256):
@@ -182,12 +197,13 @@
     )
     grids = {1: grid}
     for level in (1, 2):
-        cells = grid.shape[0]
-        down = constants[:, 1024 + 128 * level : 1152 + 128 * level]
-        grid = dot(side_by_side(grid), jnp.concatenate([down, down], axis=0))
         ready = wrapped(side_by_side(grid), 64, 0)
         grid = jnp.concatenate(
-            [both_ways(dot(row_window, ready[begin : begin + 384])) for begin in range(0, cells, 256)], axis=0
+            [
+                both_ways(dot(row_window, ready[begin : begin + 384]))
+                for begin in range(0, grid.shape[0], 256)
+            ],
+            axis=0,
         )
         grids[level + 1] = grid
     copies[1].wait()
@@ -217,24 +233,44 @@
 
 
 def weight_kernel(sections, taps, tables, weights):
+    tables_at = {
+        (level, axis): 2 * lanes + (2 * (level - 1) + axis) * (lanes + 32) for level, axis in sections
+    }
+    stacks = {}
     for (level, axis), (start, offsets) in sections.items():
-        begin = (2 * (level - 1) + axis) * (2 * lanes + 16)
-        chooser = tables[begin : begin + lanes, 0:16]
-        same = tables[begin + lanes : begin + 2 * lanes, :]
-        base = tables[begin + 2 * lanes : begin + 2 * lanes + 16, :].astype(jnp.float32).astype(jnp.int32)
+        begin = tables_at[level, axis] + lanes + 16
+        base = tables[begin : begin + 16, :].astype(jnp.float32).astype(jnp.int32)
         scale = 0.5**level if axis == 0 else 1.0
         values = [scale * taps[axis, level, tap] for tap in range(9)]
-        for index, offset in enumerate(offsets):
+        stack = []
+        for offset in offsets:
             number = base + brick_cells[level] * offset
             if level == 3 and axis == 0:
                 number = number & 271
             chosen = jnp.zeros(number.shape, jnp.float32)
             for tap in range(9):
                 chosen = jnp.where(number == tap, values[tap], chosen)
-            spread = dot(chooser, side_by_side(chosen)).astype(jnp.bfloat16)
-            rows = pl.ds((start + index) * lanes, lanes)
-            weights[rows, 0:lanes] = spread[:, :lanes] * same
-            weights[rows, lanes : 2 * lanes] = spread[:, lanes:] * same
+            stack.append(chosen)
+        stacks[level, axis] = split(jnp.concatenate(stack, axis=0))
+    for level, axis in sections:
+        begin = tables_at[level, axis] + lanes
+        high, low = stacks[level, axis]
+        out_of = tables[begin : begin + 16, :]
+        stacks[level, axis] = split(dot(high[:, 0:16], out_of) + dot(low[:, 0:16], out_of))
+    for (level, axis), (start, offsets) in sections.items():
+        same = tables[axis * lanes : (axis + 1) * lanes, :].astype(jnp.float32)
+        into = tables[tables_at[level, axis] : tables_at[level, axis] + lanes, 0:16]
+        into = jnp.concatenate([into, into], axis=1)
+        for index in range(0, len(offsets), 2):
+            pair = range(index, min(index + 2, len(offsets)))
+            parts = [
+                jnp.concatenate([half[16 * part : 16 * (part + 1)] for part in pair], axis=1)
+                for half in stacks[level, axis]
+            ]
+            spread = dot(into, jnp.concatenate(parts, axis=0))
+            for place, part in enumerate(pair):
+                rows = pl.ds((start + part) * lanes, lanes)
+                weights[rows, :] = side_by_side(spread[:, place * lanes : (place + 1) * lanes] * same)
 
 
 def weighted(pieces, weights, start):
@@ -282,31 +318,24 @@
 
 def finish_kernel(received, constants, twice_up, finest, potential, ready, left):
     rows_x, rows_y, depth = finest.shape
-    row_window = constants[:, 512:768]
+    row_window = constants[:, 256:512]
     parts = {
         level: jnp.concatenate(
             [received[pl.ds(row, lanes, stride=rows_per_block), :] for row in block_rows[level]], axis=0
         )
         for level in (1, 2, 3)
     }
-    high, low = split(parts[3])
-    coarsest = dot(jnp.concatenate([high, low, high], axis=1), twice_up[0 : 3 * lanes, :])
-    middle = dot(side_by_side(parts[2]), constants[:, 128:256])
-    coarsest = both_ways(dot(twice_up[3 * lanes :, :], side_by_side(coarsest)))
-    pairs = wrapped(side_by_side(middle), 64, 0)
+    coarsest = both_ways(dot(twice_up[...], side_by_side(parts[3])))
+    pairs = wrapped(side_by_side(parts[2]), 64, 0)
     middle = jnp.concatenate(
-        [
-            both_ways(dot(row_window, pairs[begin : begin + 256]))
-            for begin in range(0, 2 * lanes, lanes)
-        ],
-        axis=0,
+        [both_ways(dot(row_window, pairs[begin : begin + 256])) for begin in (0, lanes)], axis=0
     )
     running = parts[1] + middle + coarsest
     pairs = wrapped(side_by_side(running), 64, 0)
     copies = []
     for index in range(depth // 256):
         fine = both_ways(dot(row_window, pairs[lanes * index : lanes * index + 256]))
-        smooth = dot_lanes(constants[:, 256:512], side_by_side(fine))
+        smooth = dot_lanes(constants[:, 0:256], side_by_side(fine))
         section = slice(256 * index, 256 * (index + 1))
         ready[:, :, section] = finest[:, :, section] + smooth.reshape(rows_x, rows_y, 256)
         places = pl.ds(256 * index, 256)
@@ -318,7 +347,21 @@
         copy.wait()
 
 
-def convolve_x_kernel(taps, before, own, after, summed_ref, head, tail):
+def convolve_y_kernel(taps, before, own, after, summed_ref, head, tail):
+    rows_x, rows_y, depth = own.shape
+    for row in range(rows_x):
+        lines = jnp.concatenate([before[row], own[row], after[row]], axis=0)
+        summed = taps[1, 0, 0] * lines[0:rows_y]
+        for tap in range(1, 9):
+            summed = summed + taps[1, 0, tap] * lines[tap : tap + rows_y]
+        summed_ref[row] = summed
+        if row < 4:
+            head[row] = summed
+        if row >= rows_x - 4:
+            tail[row - (rows_x - 4)] = summed
+
+
+def convolve_xz_kernel(taps, before, own, after, result):
     rows_x, rows_y, depth = own.shape
 
     def layer(index):
@@ -330,21 +373,6 @@
         summed = taps[0, 0, 0] * layer(row)
         for tap in range(1, 9):
             summed = summed + taps[0, 0, tap] * layer(row + tap)
-        summed_ref[row] = summed
-        head[row] = summed[:4]
-        tail[row] = summed[rows_y - 4 :]
-
-
-def convolve_yz_kernel(taps, before, own, after, result, rim):
-    rows_x, rows_y, depth = own.shape
-    for row in range(rows_x):
-        rim[row, 4:8, :] = before[row]
-        rim[row, 8 : 8 + rows_y, :] = own[row]
-        rim[row, 8 + rows_y : 12 + rows_y, :] = after[row]
-    for row in range(rows_x):
-        summed = taps[1, 0, 0] * rim[row, 4 : 4 + rows_y, :]
-        for tap in range(1, 9):
-            summed = summed + taps[1, 0, tap] * rim[row, 4 + tap : 4 + tap + rows_y, :]
         total = taps[2, 0, 4] * summed
         for tap in (0, 1, 2, 3, 5, 6, 7, 8):
             total = total + taps[2, 0, tap] * pltpu.roll(summed, (4 - tap) % depth, 1)
@@ -382,45 +410,22 @@
     rows_x, rows_y, depth = charges.shape
     taps = jnp.transpose(kernel_taps, (1, 0, 2))
     both = ("gx", "gy")
-    downs = [restrict_1d(level) for level in range(3)]
-    ups = [prolong_1d(level) for level in range(3)]
+    down, up = restrict_1d(0), prolong_1d(0)
     down_constants = np.concatenate(
         [
-            padded(np.kron(downs[0], downs[0]), lanes, rows_x * rows_y),
+            padded(np.kron(down, down), lanes, rows_x * rows_y),
             restrict_window(lanes, 512, 128),
             restrict_window(lanes, 384, 64),
-            padded(np.kron(downs[1].T, downs[1].T), lanes, lanes),
-            padded(np.kron(downs[2].T, downs[2].T), lanes, lanes),
         ],
         axis=1,
     )
     down_constants = jnp.asarray(down_constants, jnp.bfloat16)
 
-    def twice(matrix, axis):
-        return np.concatenate([matrix, matrix], axis=axis)
-
-    up_1, up_2, up_3 = (
-        padded(matrix, rows, lanes)
-        for matrix, rows in (
-            (np.kron(ups[0], ups[0]), 256),
-            (np.kron(ups[1].T, ups[1].T), lanes),
-            (np.kron(ups[2].T, ups[2].T), lanes),
-        )
+    up_1 = padded(np.kron(up, up), rows_x * rows_y, lanes)
+    up_constants = jnp.asarray(
+        np.concatenate([up_1, up_1, prolong_window(256, 256, 64)], axis=1), jnp.bfloat16
     )
-    up_constants = jnp.asarray(
-        np.concatenate(
-            [twice(up_3, 0), twice(up_2, 0), twice(up_1, 1), prolong_window(256, 256, 64)], axis=1
-        ),
-        jnp.bfloat16,
-    )
-    both_ups = padded(np.kron((ups[1] @ ups[2]).T, (ups[1] @ ups[2]).T), lanes, lanes)
-    rounded = both_ups.astype(jnp.bfloat16).astype(np.float32)
-    twice_up = jnp.asarray(
-        np.concatenate(
-            [rounded, rounded, both_ups - rounded, prolong_ring(4 * lanes) @ prolong_ring(2 * lanes)], axis=0
-        ),
-        jnp.bfloat16,
-    )
+    twice_up = jnp.asarray(prolong_ring(4 * lanes) @ prolong_ring(2 * lanes), jnp.bfloat16)
     sections, section_count = weight_sections(count_x, count_y)
     block_shape = (lanes * rows_per_block, lanes)
     exchange_shape = (lanes * rows_per_block, 1, lanes)
@@ -429,8 +434,8 @@
         restrict_kernel,
         (
             shape_of(*block_shape),
-            shape_of(4, rows_y, depth),
-            shape_of(4, rows_y, depth),
+            shape_of(rows_x, 4, depth),
+            shape_of(rows_x, 4, depth),
         ),
         [far] * 3,
         [
@@ -461,24 +466,23 @@
         count = lax.axis_size(axis)
         return lax.ppermute(values, axis, [(i, (i + step) % count) for i in range(count)])
 
-    before = shifted(tail, "gx", 1)
-    after = shifted(head, "gx", -1)
+    before = shifted(tail, "gy", 1)
+    after = shifted(head, "gy", -1)
     summed, head, tail = call(
-        convolve_x_kernel,
-        (shape_of(rows_x, rows_y, depth), shape_of(rows_x, 4, depth), shape_of(rows_x, 4, depth)),
+        convolve_y_kernel,
+        (shape_of(rows_x, rows_y, depth), shape_of(4, rows_y, depth), shape_of(4, rows_y, depth)),
         [scalars] + in_vmem(3),
         flops=10**11,
         moved=3 * 10**6,
     )(taps, before, charges, after)
     received, _ = lax.optimization_barrier((received, tail))
     finest = call(
-        convolve_yz_kernel,
+        convolve_xz_kernel,
         shape_of(rows_x, rows_y, depth),
         [scalars] + in_vmem(3),
-        [pltpu.VMEM((rows_x, rows_y + 16, depth), jnp.float32)],
         flops=10**11,
         moved=3 * 10**6,
-    )(taps, shifted(tail, "gy", 1), summed, shifted(head, "gy", -1))
+    )(taps, shifted(tail, "gx", 1), summed, shifted(head, "gx", -1))
 
     blocks = call(
         lambda *refs: convolve_kernel(sections, count_x, count_y, *refs),

time: 54.5 us -> 53.1 us (0.974)
  starting transfers between devices: 23.6 us -> 19.7 us
  waiting for transfers between devices: 11.7 us -> 15 us
  Pallas kernels: 16.5 us -> 15.7 us
    all_to_all x2, starting transfers between devices: 15.8 us -> 12.1 us  [per_device(): lax.all_to_all(blocks.reshape(exchange_shape), both, 0, 0, tiled=True)]
    all_to_all x2, waiting for transfers between devices: 11.7 us -> 15 us  [per_device(): lax.all_to_all(blocks.reshape(exchange_shape), both, 0, 0, tiled=True)]
    pallas_call x3, Pallas kernels: 10.6 us -> 10 us  [the longest x1 4.07 us: per_device(): call(restrict_kernel, (shape_of(*block_shape), shape_of(rows_x, 4, depth)...]
where the time goes in v4:
time: 53.1 us; the launch traced here: 52.8 us
  starting transfers between devices  19.7 us (37%)
  Pallas kernels  15.7 us (30%)
  waiting for transfers between devices  15 us (28%)
  local copies, waits for them, and re-layouts  2.21 us (4%)
    all_to_all x2, waiting for transfers between devices, per_device(): lax.all_to_all(blocks.reshape(exchange_shape), both, 0, 0, tiled=True)  15 us
    all_to_all x2, starting transfers between devices, per_device(): lax.all_to_all(blocks.reshape(exchange_shape), both, 0, 0, tiled=True)  12.1 us
    ppermute x4, starting transfers between devices, shifted(): lax.ppermute(values, axis, [(i, (i + step) % count) for i in range(count)])  7.66 us
    pallas_call x1, Pallas kernels, per_device(): call(restrict_kernel, (shape_of(*block_shape), shape_of(rows_x, 4, depth)...  4.07 us
    pallas_call x1, Pallas kernels, per_device(): call(convolve_xz_kernel, shape_of(rows_x, rows_y, depth), [scalars] + in_...  3.27 us
    pallas_call x1, Pallas kernels, per_device(): call(convolve_y_kernel, (shape_of(rows_x, rows_y, depth), shape_of(4, row...  2.7 us
    pallas_call x1, Pallas kernels, per_device(): call(lambda *refs: convolve_kernel(sections, count_x, count_y, *refs), sh...  2.47 us
    unnamed x14, local copies, waits for them, and re-layouts  2.21 us
  transfers between devices with their start and end apart: 6, of which 2 were waited for; matrix products, arithmetic and copies ran while one was open for 0% of the time, Pallas kernels for 19%

profile of v4, /device:TPU:1, one launch (start us, length us, event | category | flops | bytes accessed | tf_op | source)
XLA Modules:
  0.0 52.8 jit_solution(6837498355267725167)
XLA Ops:
  0.0 0.0 copy-start.2
  0.0 0.0 copy-start.1
  0.0 4.1 %shard_map.64 = (f32[896,128]{1,0:T(8,128)}, f32[16,4,1024]{2,1,0:T(4,128)}, f32[16,4,1024]{2,1,0:T(4,128)}) custom-call(f32[3,4,9]{2,1,0:T(4,128)} %bitcast.11, f32[16,16,1024]{2,1,0:T(8,128)} %own.1, bf16[128,1152]{1,0:T(8,128)(2,1)} %constant.8.clone.constants_far), custom_call_target="tpu_custom_call" | custom-call | flops 1000000000 | bytes 2000000 | tf_op jit(solution)/shard_map/pallas_call | solution.py:433
  4.1 2.1 %collective-permute-start = (f32[16,4,1024]{2,1,0:T(4,128)}, f32[16,4,1024]{2,1,0:T(4,128)S(1)}, u32[]{:S(2)}, u32[]{:S(2)}) collective-permute-start(f32[16,4,1024]{2,1,0:T(4,128)} %get-tuple-element.13), channel_id=1, source_target_pairs={{0,1},{1,2},{2,3},{3,4},{4,5},{5,6},{6,7},{7,8},{8,9},{9,10},{10,1... | collective-permute-start | bytes 786440 | tf_op jit(solution)/shard_map/ppermute | solution.py:467
  6.2 3.8 %collective-permute-start.1 = (f32[16,4,1024]{2,1,0:T(4,128)}, f32[16,4,1024]{2,1,0:T(4,128)S(1)}, u32[]{:S(2)}, u32[]{:S(2)}) collective-permute-start(f32[16,4,1024]{2,1,0:T(4,128)} %get-tuple-element.14), channel_id=1, source_target_pairs={{0,15},{1,0},{2,1},{3,2},{4,3},{5,4},{6,5},{7,6},{8,7},{9,8},{10,9... | collective-permute-start | bytes 786440 | tf_op jit(solution)/shard_map/ppermute | solution.py:467
  10.0 7.7 %all-to-all-start = ((f32[896,1,128]{2,1,0:T(1,128)}), f32[896,1,128]{2,1,0:T(1,128)S(1)}, u32[]{:S(2)}, u32[]{:S(2)}) async-start(f32[896,1,128]{2,1,0:T(1,128)} %bitcast.15), calls=%async_computation | async-start | bytes 917504 | tf_op jit(solution)/shard_map/all_to_all | solution.py:455
  17.7 0.0 copy-start
  17.7 0.0 collective-permute-done.before
  17.7 0.0 collective-permute-done.1.after
  17.7 0.0 copy-done.2
  17.7 0.0 copy-done.1
  17.7 2.7 %shard_map.65 = (f32[16,16,1024]{2,1,0:T(8,128)S(1)}, f32[4,16,1024]{2,1,0:T(8,128)}, f32[4,16,1024]{2,1,0:T(8,128)S(1)}) custom-call(f32[3,4,9]{2,1,0:T(4,128)S(1)} %bitcast.12, f32[16,4,1024]{2,1,0:T(4,128)S(1)} %collective-permute-done.before, f32[16,16,1024]{2,1,0:T(8,128)S(1)} %copy-done.2, f32[16,4,1024]{2,1,0:T(4,128)S(1)} %collective-permute-done.1.after), custom_call_target="tpu_custom_call" | custom-call | flops 99999997952 | bytes 3000000 | tf_op jit(solution)/shard_map/pallas_call | solution.py:471
  20.4 0.0 copy-start.5
  20.4 1.0 %copy-done.5 = f32[16,16,1024]{2,1,0:T(8,128)} copy-done((f32[16,16,1024]{2,1,0:T(8,128)}, f32[16,16,1024]{2,1,0:T(8,128)S(1)}, u32[]{:S(2)}) %copy-start.5) | copy-done | bytes 1048600
  21.4 1.1 %collective-permute-start.3 = (f32[4,16,1024]{2,1,0:T(8,128)}, f32[4,16,1024]{2,1,0:T(8,128)S(1)}, u32[]{:S(2)}, u32[]{:S(2)}) collective-permute-start(f32[4,16,1024]{2,1,0:T(8,128)} %get-tuple-element.18), channel_id=1, source_target_pairs={{0,112},{16,0},{32,16},{48,32},{64,48},{80,64},{96,80},{112,96},{1... | collective-permute-start | bytes 786440 | tf_op jit(solution)/shard_map/ppermute | solution.py:467
  22.5 0.7 %collective-permute-start.2 = (f32[4,16,1024]{2,1,0:T(8,128)S(1)}, f32[4,16,1024]{2,1,0:T(8,128)}, u32[]{:S(2)}, u32[]{:S(2)}) collective-permute-start(f32[4,16,1024]{2,1,0:T(8,128)S(1)} %get-tuple-element.15), channel_id=1, source_target_pairs={{0,16},{16,32},{32,48},{48,64},{64,80},{80,96},{96,112},{112,0},{1... | collective-permute-start | bytes 786440 | tf_op jit(solution)/shard_map/ppermute | solution.py:467
  23.2 0.0 copy-done
  23.2 1.5 %shard_map.66.refs_1_ = bf16[4992,256]{1,0:T(8,128)(2,1)S(1)} custom-call(f32[3,4,9]{2,1,0:T(4,128)S(1)} %bitcast.13, bf16[1216,128]{1,0:T(8,128)(2,1)S(1)} %copy-done), custom_call_target="tpu_custom_call" | custom-call | flops 20000000 | bytes 3000000 | tf_op jit(solution)/shard_map/pallas_call | solution.py:457
  24.6 6.3 %all-to-all-done = f32[896,1,128]{2,1,0:T(1,128)S(1)} async-done(((f32[896,1,128]{2,1,0:T(1,128)}), f32[896,1,128]{2,1,0:T(1,128)S(1)}, u32[]{:S(2)}, u32[]{:S(2)}) %all-to-all-start) | async-done | bytes 458784 | tf_op jit(solution)/shard_map/all_to_all | solution.py:455
  30.9 2.5 %shard_map.67 = f32[896,128]{1,0:T(8,128)} custom-call(f32[896,128]{1,0:T(8,128)S(1)} %bitcast.9, bf16[4992,256]{1,0:T(8,128)(2,1)S(1)} %shard_map.66.refs_1_), custom_call_target="tpu_custom_call" | custom-call | flops 1000000000 | bytes 4000000 | tf_op jit(solution)/shard_map/pallas_call | solution.py:487
  33.4 4.4 %all-to-all-start.1 = ((f32[896,1,128]{2,1,0:T(1,128)}), f32[896,1,128]{2,1,0:T(1,128)S(1)}, u32[]{:S(2)}, u32[]{:S(2)}) async-start(f32[896,1,128]{2,1,0:T(1,128)} %bitcast.5), calls=%async_computation.1 | async-start | bytes 917504 | tf_op jit(solution)/shard_map/all_to_all | solution.py:496
  37.8 0.0 collective-permute-done.3.after
  37.8 0.0 collective-permute-done.2.before
  37.8 0.0 copy-start.6
  37.8 1.2 %copy-done.6 = f32[16,16,1024]{2,1,0:T(8,128)S(1)} copy-done((f32[16,16,1024]{2,1,0:T(8,128)S(1)}, f32[16,16,1024]{2,1,0:T(8,128)}, u32[]{:S(2)}) %copy-start.6) | copy-done | bytes 1048600
  39.1 0.0 copy-start.3
  39.1 0.0 copy-start.4
  39.1 3.3 %shard_map.68.finest = f32[16,16,1024]{2,1,0:T(8,128)S(1)} custom-call(f32[3,4,9]{2,1,0:T(4,128)S(1)} %bitcast.14, f32[4,16,1024]{2,1,0:T(8,128)} %collective-permute-done.2.before, f32[16,16,1024]{2,1,0:T(8,128)S(1)} %copy-done.6, f32[4,16,1024]{2,1,0:T(8,128)S(1)} %collective-permute-done.3.after), custom_call_target="tpu_custom_call" | custom-call | flops 99999997952 | bytes 3000000 | tf_op jit(solution)/shard_map/pallas_call | solution.py:479
  42.3 8.7 %all-to-all-done.1 = f32[896,1,128]{2,1,0:T(1,128)S(1)} async-done(((f32[896,1,128]{2,1,0:T(1,128)}), f32[896,1,128]{2,1,0:T(1,128)S(1)}, u32[]{:S(2)}, u32[]{:S(2)}) %all-to-all-start.1) | async-done | bytes 458784 | tf_op jit(solution)/shard_map/all_to_all | solution.py:496
  51.1 0.0 copy-done.3
  51.1 0.0 copy-done.4
  51.1 1.7 %shard_map.69 = f32[16,16,1024]{2,1,0:T(8,128)} custom-call(f32[896,128]{1,0:T(8,128)S(1)} %bitcast.10, bf16[256,512]{1,0:T(8,128)(2,1)S(1)} %copy-done.3, bf16[512,128]{1,0:T(8,128)(2,1)S(1)} %copy-done.4, f32[16,16,1024]{2,1,0:T(8,128)S(1)} %shard_map.68.finest), custom_call_target="tpu_custom_call" | custom-call | flops 1000000000 | bytes 4000000 | tf_op jit(solution)/shard_map/pallas_call | solution.py:498
Async XLA Ops:
  0.0 17.7 %copy-start.2 = (f32[16,16,1024]{2,1,0:T(8,128)S(1)}, f32[16,16,1024]{2,1,0:T(8,128)}, u32[]{:S(2)}) copy-start(f32[16,16,1024]{2,1,0:T(8,128)} %own.1) | copy-start | bytes 3145732
  0.0 17.7 %copy-start.1 = (f32[4,3,9]{2,0,1:T(4,128)S(1)}, f32[4,3,9]{2,0,1:T(4,128)}, u32[]{:S(2)}) copy-start(f32[4,3,9]{2,0,1:T(4,128)} %param.7) | copy-start | bytes 1300
  4.1 13.6 %collective-permute-start = (f32[16,4,1024]{2,1,0:T(4,128)}, f32[16,4,1024]{2,1,0:T(4,128)S(1)}, u32[]{:S(2)}, u32[]{:S(2)}) collective-permute-start(f32[16,4,1024]{2,1,0:T(4,128)} %get-tuple-element.13), channel_id=1, source_target_pairs={{0,1},{1,2},{2,3},{3,4},{4,5},{5,6},{6,7},{7,8},{8,9},{9,10},{10,1... | collective-permute-start | bytes 786440 | tf_op jit(solution)/shard_map/ppermute | solution.py:467
  6.2 11.5 %collective-permute-start.1 = (f32[16,4,1024]{2,1,0:T(4,128)}, f32[16,4,1024]{2,1,0:T(4,128)S(1)}, u32[]{:S(2)}, u32[]{:S(2)}) collective-permute-start(f32[16,4,1024]{2,1,0:T(4,128)} %get-tuple-element.14), channel_id=1, source_target_pairs={{0,15},{1,0},{2,1},{3,2},{4,3},{5,4},{6,5},{7,6},{8,7},{9,8},{10,9... | collective-permute-start | bytes 786440 | tf_op jit(solution)/shard_map/ppermute | solution.py:467
  10.0 20.9 %all-to-all-start = ((f32[896,1,128]{2,1,0:T(1,128)}), f32[896,1,128]{2,1,0:T(1,128)S(1)}, u32[]{:S(2)}, u32[]{:S(2)}) async-start(f32[896,1,128]{2,1,0:T(1,128)} %bitcast.15), calls=%async_computation | async-start | bytes 917504 | tf_op jit(solution)/shard_map/all_to_all | solution.py:455
  17.7 5.5 %copy-start = (bf16[1216,128]{1,0:T(8,128)(2,1)S(1)}, bf16[1216,128]{1,0:T(8,128)(2,1)}, u32[]{:S(2)}) copy-start(bf16[1216,128]{1,0:T(8,128)(2,1)} %constant.11.clone.refs_1_) | copy-start | bytes 933892
  20.4 1.0 %copy-start.5 = (f32[16,16,1024]{2,1,0:T(8,128)}, f32[16,16,1024]{2,1,0:T(8,128)S(1)}, u32[]{:S(2)}) copy-start(f32[16,16,1024]{2,1,0:T(8,128)S(1)} %get-tuple-element.17.own) | copy-start | bytes 3145732
  21.4 16.4 %collective-permute-start.3 = (f32[4,16,1024]{2,1,0:T(8,128)}, f32[4,16,1024]{2,1,0:T(8,128)S(1)}, u32[]{:S(2)}, u32[]{:S(2)}) collective-permute-start(f32[4,16,1024]{2,1,0:T(8,128)} %get-tuple-element.18), channel_id=1, source_target_pairs={{0,112},{16,0},{32,16},{48,32},{64,48},{80,64},{96,80},{112,96},{1... | collective-permute-start | bytes 786440 | tf_op jit(solution)/shard_map/ppermute | solution.py:467
  22.5 15.4 %collective-permute-start.2 = (f32[4,16,1024]{2,1,0:T(8,128)S(1)}, f32[4,16,1024]{2,1,0:T(8,128)}, u32[]{:S(2)}, u32[]{:S(2)}) collective-permute-start(f32[4,16,1024]{2,1,0:T(8,128)S(1)} %get-tuple-element.15), channel_id=1, source_target_pairs={{0,16},{16,32},{32,48},{48,64},{64,80},{80,96},{96,112},{112,0},{1... | collective-permute-start | bytes 786440 | tf_op jit(solution)/shard_map/ppermute | solution.py:467
  33.4 17.7 %all-to-all-start.1 = ((f32[896,1,128]{2,1,0:T(1,128)}), f32[896,1,128]{2,1,0:T(1,128)S(1)}, u32[]{:S(2)}, u32[]{:S(2)}) async-start(f32[896,1,128]{2,1,0:T(1,128)} %bitcast.5), calls=%async_computation.1 | async-start | bytes 917504 | tf_op jit(solution)/shard_map/all_to_all | solution.py:496
  37.8 1.2 %copy-start.6 = (f32[16,16,1024]{2,1,0:T(8,128)S(1)}, f32[16,16,1024]{2,1,0:T(8,128)}, u32[]{:S(2)}) copy-start(f32[16,16,1024]{2,1,0:T(8,128)} %copy-done.5) | copy-start | bytes 3145732
  39.1 12.0 %copy-start.3 = (bf16[256,512]{1,0:T(8,128)(2,1)S(1)}, bf16[256,512]{1,0:T(8,128)(2,1)}, u32[]{:S(2)}) copy-start(bf16[256,512]{1,0:T(8,128)(2,1)} %constant.9.clone.constants) | copy-start | bytes 786436
  39.1 12.0 %copy-start.4 = (bf16[512,128]{1,0:T(8,128)(2,1)S(1)}, bf16[512,128]{1,0:T(8,128)(2,1)}, u32[]{:S(2)}) copy-start(bf16[512,128]{1,0:T(8,128)(2,1)} %constant.10.clone.twice_up) | copy-start | bytes 393220

commit v5 on v4

--- a/solution.py
+++ b/solution.py
@@ -207,25 +207,28 @@
         )
         grids[level + 1] = grid
     copies[1].wait()
-    first = 0
+    firsts, first = {}, 0
     for level in (1, 2, 3):
         grid = grids[level]
         cells = grid.shape[0]
         rim[first : first + 8, :] = grid[cells - 8 :, :]
         rim[first + 8 : first + 8 + cells, :] = grid
         rim[first + 8 + cells : first + 16 + cells, :] = grid[:8, :]
-        for index, row in enumerate(block_rows[level]):
-            summed = None
-            for tap in range(9):
-                begin = first + lanes * index + 4 + tap
-                term = taps[2, level, tap] * rim[begin : begin + lanes, :]
-                summed = term if summed is None else summed + term
-            blocks[pl.ds(row, lanes, stride=rows_per_block), :] = summed
+        firsts[level] = first
         first += cells + 16
-    for index in range(4):
-        section = pl.ds(224 * index, 224)
+    share = lanes // 4
+    for part in range(4):
+        for level in (1, 2, 3):
+            for index, row in enumerate(block_rows[level]):
+                summed = None
+                for tap in range(9):
+                    begin = firsts[level] + lanes * index + share * part + 4 + tap
+                    term = taps[2, level, tap] * rim[begin : begin + share, :]
+                    summed = term if summed is None else summed + term
+                blocks[pl.ds(rows_per_block * share * part + row, share, stride=rows_per_block), :] = summed
+        section = pl.ds(rows_per_block * share * part, rows_per_block * share)
         leaving.append(
-            pltpu.make_async_copy(blocks.at[section], blocks_far.at[section], arrived.at[4 + depth // 256 + index])
+            pltpu.make_async_copy(blocks.at[section], blocks_far.at[section], arrived.at[4 + depth // 256 + part])
         )
         leaving[-1].start()
     for copy in leaving:

time: 53.1 us -> 52.9 us (level)
  no operation moved by 1% of the time
where the time goes in v5:
time: 52.9 us; the launch traced here: 52.6 us
  starting transfers between devices  19.7 us (37%)
  Pallas kernels  15.5 us (29%)
  waiting for transfers between devices  15.1 us (29%)
  local copies, waits for them, and re-layouts  2.21 us (4%)
    all_to_all x2, waiting for transfers between devices, per_device(): lax.all_to_all(blocks.reshape(exchange_shape), both, 0, 0, tiled=True)  15 us
    all_to_all x2, starting transfers between devices, per_device(): lax.all_to_all(blocks.reshape(exchange_shape), both, 0, 0, tiled=True)  12.1 us
    ppermute x4, starting transfers between devices, shifted(): lax.ppermute(values, axis, [(i, (i + step) % count) for i in range(count)])  7.66 us
    pallas_call x1, Pallas kernels, per_device(): call(restrict_kernel, (shape_of(*block_shape), shape_of(rows_x, 4, depth)...  3.94 us
    pallas_call x1, Pallas kernels, per_device(): call(convolve_xz_kernel, shape_of(rows_x, rows_y, depth), [scalars] + in_...  3.27 us
    pallas_call x1, Pallas kernels, per_device(): call(convolve_y_kernel, (shape_of(rows_x, rows_y, depth), shape_of(4, row...  2.7 us
    pallas_call x1, Pallas kernels, per_device(): call(lambda *refs: convolve_kernel(sections, count_x, count_y, *refs), sh...  2.47 us
    unnamed x14, local copies, waits for them, and re-layouts  2.21 us
  transfers between devices with their start and end apart: 6, of which 2 were waited for; matrix products, arithmetic and copies ran while one was open for 0% of the time, Pallas kernels for 19%

profile of v5, /device:TPU:1, one launch (start us, length us, event | category | flops | bytes accessed | tf_op | source)
XLA Modules:
  0.0 52.6 jit_solution(16991455405920907947)
XLA Ops:
  0.0 0.0 copy-start.2
  0.0 0.0 copy-start.1
  0.0 3.9 %shard_map.64 = (f32[896,128]{1,0:T(8,128)}, f32[16,4,1024]{2,1,0:T(4,128)}, f32[16,4,1024]{2,1,0:T(4,128)}) custom-call(f32[3,4,9]{2,1,0:T(4,128)} %bitcast.11, f32[16,16,1024]{2,1,0:T(8,128)} %own.1, bf16[128,1152]{1,0:T(8,128)(2,1)} %constant.8.clone.constants_far), custom_call_target="tpu_custom_call" | custom-call | flops 1000000000 | bytes 2000000 | tf_op jit(solution)/shard_map/pallas_call | solution.py:436
  3.9 2.1 %collective-permute-start = (f32[16,4,1024]{2,1,0:T(4,128)}, f32[16,4,1024]{2,1,0:T(4,128)S(1)}, u32[]{:S(2)}, u32[]{:S(2)}) collective-permute-start(f32[16,4,1024]{2,1,0:T(4,128)} %get-tuple-element.13), channel_id=1, source_target_pairs={{0,1},{1,2},{2,3},{3,4},{4,5},{5,6},{6,7},{7,8},{8,9},{9,10},{10,1... | collective-permute-start | bytes 786440 | tf_op jit(solution)/shard_map/ppermute | solution.py:470
  6.1 3.8 %collective-permute-start.1 = (f32[16,4,1024]{2,1,0:T(4,128)}, f32[16,4,1024]{2,1,0:T(4,128)S(1)}, u32[]{:S(2)}, u32[]{:S(2)}) collective-permute-start(f32[16,4,1024]{2,1,0:T(4,128)} %get-tuple-element.14), channel_id=1, source_target_pairs={{0,15},{1,0},{2,1},{3,2},{4,3},{5,4},{6,5},{7,6},{8,7},{9,8},{10,9... | collective-permute-start | bytes 786440 | tf_op jit(solution)/shard_map/ppermute | solution.py:470
  9.9 7.7 %all-to-all-start = ((f32[896,1,128]{2,1,0:T(1,128)}), f32[896,1,128]{2,1,0:T(1,128)S(1)}, u32[]{:S(2)}, u32[]{:S(2)}) async-start(f32[896,1,128]{2,1,0:T(1,128)} %bitcast.15), calls=%async_computation | async-start | bytes 917504 | tf_op jit(solution)/shard_map/all_to_all | solution.py:458
  17.5 0.0 copy-start
  17.6 0.0 collective-permute-done.before
  17.6 0.0 collective-permute-done.1.after
  17.6 0.0 copy-done.2
  17.6 0.0 copy-done.1
  17.6 2.7 %shard_map.65 = (f32[16,16,1024]{2,1,0:T(8,128)S(1)}, f32[4,16,1024]{2,1,0:T(8,128)}, f32[4,16,1024]{2,1,0:T(8,128)S(1)}) custom-call(f32[3,4,9]{2,1,0:T(4,128)S(1)} %bitcast.12, f32[16,4,1024]{2,1,0:T(4,128)S(1)} %collective-permute-done.before, f32[16,16,1024]{2,1,0:T(8,128)S(1)} %copy-done.2, f32[16,4,1024]{2,1,0:T(4,128)S(1)} %collective-permute-done.1.after), custom_call_target="tpu_custom_call" | custom-call | flops 99999997952 | bytes 3000000 | tf_op jit(solution)/shard_map/pallas_call | solution.py:474
  20.3 0.0 copy-start.5
  20.3 1.0 %copy-done.5 = f32[16,16,1024]{2,1,0:T(8,128)} copy-done((f32[16,16,1024]{2,1,0:T(8,128)}, f32[16,16,1024]{2,1,0:T(8,128)S(1)}, u32[]{:S(2)}) %copy-start.5) | copy-done | bytes 1048600
  21.3 1.1 %collective-permute-start.3 = (f32[4,16,1024]{2,1,0:T(8,128)}, f32[4,16,1024]{2,1,0:T(8,128)S(1)}, u32[]{:S(2)}, u32[]{:S(2)}) collective-permute-start(f32[4,16,1024]{2,1,0:T(8,128)} %get-tuple-element.18), channel_id=1, source_target_pairs={{0,112},{16,0},{32,16},{48,32},{64,48},{80,64},{96,80},{112,96},{1... | collective-permute-start | bytes 786440 | tf_op jit(solution)/shard_map/ppermute | solution.py:470
  22.3 0.7 %collective-permute-start.2 = (f32[4,16,1024]{2,1,0:T(8,128)S(1)}, f32[4,16,1024]{2,1,0:T(8,128)}, u32[]{:S(2)}, u32[]{:S(2)}) collective-permute-start(f32[4,16,1024]{2,1,0:T(8,128)S(1)} %get-tuple-element.15), channel_id=1, source_target_pairs={{0,16},{16,32},{32,48},{48,64},{64,80},{80,96},{96,112},{112,0},{1... | collective-permute-start | bytes 786440 | tf_op jit(solution)/shard_map/ppermute | solution.py:470
  23.0 0.0 copy-done
  23.0 1.4 %shard_map.66.refs_1_ = bf16[4992,256]{1,0:T(8,128)(2,1)S(1)} custom-call(f32[3,4,9]{2,1,0:T(4,128)S(1)} %bitcast.13, bf16[1216,128]{1,0:T(8,128)(2,1)S(1)} %copy-done), custom_call_target="tpu_custom_call" | custom-call | flops 20000000 | bytes 3000000 | tf_op jit(solution)/shard_map/pallas_call | solution.py:460
  24.5 6.3 %all-to-all-done = f32[896,1,128]{2,1,0:T(1,128)S(1)} async-done(((f32[896,1,128]{2,1,0:T(1,128)}), f32[896,1,128]{2,1,0:T(1,128)S(1)}, u32[]{:S(2)}, u32[]{:S(2)}) %all-to-all-start) | async-done | bytes 458784 | tf_op jit(solution)/shard_map/all_to_all | solution.py:458
  30.8 2.5 %shard_map.67 = f32[896,128]{1,0:T(8,128)} custom-call(f32[896,128]{1,0:T(8,128)S(1)} %bitcast.9, bf16[4992,256]{1,0:T(8,128)(2,1)S(1)} %shard_map.66.refs_1_), custom_call_target="tpu_custom_call" | custom-call | flops 1000000000 | bytes 4000000 | tf_op jit(solution)/shard_map/pallas_call | solution.py:490
  33.3 4.4 %all-to-all-start.1 = ((f32[896,1,128]{2,1,0:T(1,128)}), f32[896,1,128]{2,1,0:T(1,128)S(1)}, u32[]{:S(2)}, u32[]{:S(2)}) async-start(f32[896,1,128]{2,1,0:T(1,128)} %bitcast.5), calls=%async_computation.1 | async-start | bytes 917504 | tf_op jit(solution)/shard_map/all_to_all | solution.py:499
  37.7 0.0 collective-permute-done.3.after
  37.7 0.0 collective-permute-done.2.before
  37.7 0.0 copy-start.6
  37.7 1.2 %copy-done.6 = f32[16,16,1024]{2,1,0:T(8,128)S(1)} copy-done((f32[16,16,1024]{2,1,0:T(8,128)S(1)}, f32[16,16,1024]{2,1,0:T(8,128)}, u32[]{:S(2)}) %copy-start.6) | copy-done | bytes 1048600
  38.9 0.0 copy-start.3
  38.9 0.0 copy-start.4
  38.9 3.3 %shard_map.68.finest = f32[16,16,1024]{2,1,0:T(8,128)S(1)} custom-call(f32[3,4,9]{2,1,0:T(4,128)S(1)} %bitcast.14, f32[4,16,1024]{2,1,0:T(8,128)} %collective-permute-done.2.before, f32[16,16,1024]{2,1,0:T(8,128)S(1)} %copy-done.6, f32[4,16,1024]{2,1,0:T(8,128)S(1)} %collective-permute-done.3.after), custom_call_target="tpu_custom_call" | custom-call | flops 99999997952 | bytes 3000000 | tf_op jit(solution)/shard_map/pallas_call | solution.py:482
  42.2 8.7 %all-to-all-done.1 = f32[896,1,128]{2,1,0:T(1,128)S(1)} async-done(((f32[896,1,128]{2,1,0:T(1,128)}), f32[896,1,128]{2,1,0:T(1,128)S(1)}, u32[]{:S(2)}, u32[]{:S(2)}) %all-to-all-start.1) | async-done | bytes 458784 | tf_op jit(solution)/shard_map/all_to_all | solution.py:499
  50.9 0.0 copy-done.3
  50.9 0.0 copy-done.4
  50.9 1.7 %shard_map.69 = f32[16,16,1024]{2,1,0:T(8,128)} custom-call(f32[896,128]{1,0:T(8,128)S(1)} %bitcast.10, bf16[256,512]{1,0:T(8,128)(2,1)S(1)} %copy-done.3, bf16[512,128]{1,0:T(8,128)(2,1)S(1)} %copy-done.4, f32[16,16,1024]{2,1,0:T(8,128)S(1)} %shard_map.68.finest), custom_call_target="tpu_custom_call" | custom-call | flops 1000000000 | bytes 4000000 | tf_op jit(solution)/shard_map/pallas_call | solution.py:501
Async XLA Ops:
  0.0 17.6 %copy-start.2 = (f32[16,16,1024]{2,1,0:T(8,128)S(1)}, f32[16,16,1024]{2,1,0:T(8,128)}, u32[]{:S(2)}) copy-start(f32[16,16,1024]{2,1,0:T(8,128)} %own.1) | copy-start | bytes 3145732
  0.0 17.6 %copy-start.1 = (f32[4,3,9]{2,0,1:T(4,128)S(1)}, f32[4,3,9]{2,0,1:T(4,128)}, u32[]{:S(2)}) copy-start(f32[4,3,9]{2,0,1:T(4,128)} %param.7) | copy-start | bytes 1300
  3.9 13.6 %collective-permute-start = (f32[16,4,1024]{2,1,0:T(4,128)}, f32[16,4,1024]{2,1,0:T(4,128)S(1)}, u32[]{:S(2)}, u32[]{:S(2)}) collective-permute-start(f32[16,4,1024]{2,1,0:T(4,128)} %get-tuple-element.13), channel_id=1, source_target_pairs={{0,1},{1,2},{2,3},{3,4},{4,5},{5,6},{6,7},{7,8},{8,9},{9,10},{10,1... | collective-permute-start | bytes 786440 | tf_op jit(solution)/shard_map/ppermute | solution.py:470
  6.1 11.5 %collective-permute-start.1 = (f32[16,4,1024]{2,1,0:T(4,128)}, f32[16,4,1024]{2,1,0:T(4,128)S(1)}, u32[]{:S(2)}, u32[]{:S(2)}) collective-permute-start(f32[16,4,1024]{2,1,0:T(4,128)} %get-tuple-element.14), channel_id=1, source_target_pairs={{0,15},{1,0},{2,1},{3,2},{4,3},{5,4},{6,5},{7,6},{8,7},{9,8},{10,9... | collective-permute-start | bytes 786440 | tf_op jit(solution)/shard_map/ppermute | solution.py:470
  9.9 20.9 %all-to-all-start = ((f32[896,1,128]{2,1,0:T(1,128)}), f32[896,1,128]{2,1,0:T(1,128)S(1)}, u32[]{:S(2)}, u32[]{:S(2)}) async-start(f32[896,1,128]{2,1,0:T(1,128)} %bitcast.15), calls=%async_computation | async-start | bytes 917504 | tf_op jit(solution)/shard_map/all_to_all | solution.py:458
  17.5 5.5 %copy-start = (bf16[1216,128]{1,0:T(8,128)(2,1)S(1)}, bf16[1216,128]{1,0:T(8,128)(2,1)}, u32[]{:S(2)}) copy-start(bf16[1216,128]{1,0:T(8,128)(2,1)} %constant.11.clone.refs_1_) | copy-start | bytes 933892
  20.3 1.0 %copy-start.5 = (f32[16,16,1024]{2,1,0:T(8,128)}, f32[16,16,1024]{2,1,0:T(8,128)S(1)}, u32[]{:S(2)}) copy-start(f32[16,16,1024]{2,1,0:T(8,128)S(1)} %get-tuple-element.17.own) | copy-start | bytes 3145732
  21.3 16.4 %collective-permute-start.3 = (f32[4,16,1024]{2,1,0:T(8,128)}, f32[4,16,1024]{2,1,0:T(8,128)S(1)}, u32[]{:S(2)}, u32[]{:S(2)}) collective-permute-start(f32[4,16,1024]{2,1,0:T(8,128)} %get-tuple-element.18), channel_id=1, source_target_pairs={{0,112},{16,0},{32,16},{48,32},{64,48},{80,64},{96,80},{112,96},{1... | collective-permute-start | bytes 786440 | tf_op jit(solution)/shard_map/ppermute | solution.py:470
  22.3 15.4 %collective-permute-start.2 = (f32[4,16,1024]{2,1,0:T(8,128)S(1)}, f32[4,16,1024]{2,1,0:T(8,128)}, u32[]{:S(2)}, u32[]{:S(2)}) collective-permute-start(f32[4,16,1024]{2,1,0:T(8,128)S(1)} %get-tuple-element.15), channel_id=1, source_target_pairs={{0,16},{16,32},{32,48},{48,64},{64,80},{80,96},{96,112},{112,0},{1... | collective-permute-start | bytes 786440 | tf_op jit(solution)/shard_map/ppermute | solution.py:470
  33.3 17.7 %all-to-all-start.1 = ((f32[896,1,128]{2,1,0:T(1,128)}), f32[896,1,128]{2,1,0:T(1,128)S(1)}, u32[]{:S(2)}, u32[]{:S(2)}) async-start(f32[896,1,128]{2,1,0:T(1,128)} %bitcast.5), calls=%async_computation.1 | async-start | bytes 917504 | tf_op jit(solution)/shard_map/all_to_all | solution.py:499
  37.7 1.2 %copy-start.6 = (f32[16,16,1024]{2,1,0:T(8,128)S(1)}, f32[16,16,1024]{2,1,0:T(8,128)}, u32[]{:S(2)}) copy-start(f32[16,16,1024]{2,1,0:T(8,128)} %copy-done.5) | copy-start | bytes 3145732
  38.9 12.0 %copy-start.3 = (bf16[256,512]{1,0:T(8,128)(2,1)S(1)}, bf16[256,512]{1,0:T(8,128)(2,1)}, u32[]{:S(2)}) copy-start(bf16[256,512]{1,0:T(8,128)(2,1)} %constant.9.clone.constants) | copy-start | bytes 786436
  38.9 12.0 %copy-start.4 = (bf16[512,128]{1,0:T(8,128)(2,1)S(1)}, bf16[512,128]{1,0:T(8,128)(2,1)}, u32[]{:S(2)}) copy-start(bf16[512,128]{1,0:T(8,128)(2,1)} %constant.10.clone.twice_up) | copy-start | bytes 393220

commit v6 on v5

--- a/solution.py
+++ b/solution.py
@@ -350,27 +350,31 @@
         copy.wait()
 
 
-def convolve_y_kernel(taps, before, own, after, summed_ref, head, tail):
+def along_y(taps, before, own, after, row):
+    rows_y = own.shape[1]
+    lines = jnp.concatenate([before[row], own[row], after[row]], axis=0)
+    summed = taps[1, 0, 0] * lines[0:rows_y]
+    for tap in range(1, 9):
+        summed = summed + taps[1, 0, tap] * lines[tap : tap + rows_y]
+    return summed
+
+
+def edge_kernel(taps, before, own, after, head, tail):
+    rows_x = own.shape[0]
+    for row in range(4):
+        head[row] = along_y(taps, before, own, after, row)
+        tail[row] = along_y(taps, before, own, after, rows_x - 4 + row)
+
+
+def finest_kernel(taps, before_y, own, after_y, before, after, result, summed_y):
     rows_x, rows_y, depth = own.shape
     for row in range(rows_x):
-        lines = jnp.concatenate([before[row], own[row], after[row]], axis=0)
-        summed = taps[1, 0, 0] * lines[0:rows_y]
-        for tap in range(1, 9):
-            summed = summed + taps[1, 0, tap] * lines[tap : tap + rows_y]
-        summed_ref[row] = summed
-        if row < 4:
-            head[row] = summed
-        if row >= rows_x - 4:
-            tail[row - (rows_x - 4)] = summed
-
-
-def convolve_xz_kernel(taps, before, own, after, result):
-    rows_x, rows_y, depth = own.shape
+        summed_y[row] = along_y(taps, before_y, own, after_y, row)
 
     def layer(index):
         if index < 4:
             return before[index]
-        return own[index - 4] if index < 4 + rows_x else after[index - 4 - rows_x]
+        return summed_y[index - 4] if index < 4 + rows_x else after[index - 4 - rows_x]
 
     for row in range(rows_x):
         summed = taps[0, 0, 0] * layer(row)
@@ -471,21 +475,22 @@
 
     before = shifted(tail, "gy", 1)
     after = shifted(head, "gy", -1)
-    summed, head, tail = call(
-        convolve_y_kernel,
-        (shape_of(rows_x, rows_y, depth), shape_of(4, rows_y, depth), shape_of(4, rows_y, depth)),
+    head, tail = call(
+        edge_kernel,
+        (shape_of(4, rows_y, depth), shape_of(4, rows_y, depth)),
         [scalars] + in_vmem(3),
         flops=10**11,
         moved=3 * 10**6,
     )(taps, before, charges, after)
     received, _ = lax.optimization_barrier((received, tail))
     finest = call(
-        convolve_xz_kernel,
+        finest_kernel,
         shape_of(rows_x, rows_y, depth),
-        [scalars] + in_vmem(3),
+        [scalars] + in_vmem(5),
+        [pltpu.VMEM((rows_x, rows_y, depth), jnp.float32)],
         flops=10**11,
         moved=3 * 10**6,
-    )(taps, shifted(tail, "gx", 1), summed, shifted(head, "gx", -1))
+    )(taps, before, charges, after, shifted(tail, "gx", 1), shifted(head, "gx", -1))
 
     blocks = call(
         lambda *refs: convolve_kernel(sections, count_x, count_y, *refs),

time: 52.9 us -> 53 us (level)
  local copies, waits for them, and re-layouts: 2.21 us -> 1.25 us
  Pallas kernels: 15.5 us -> 16.3 us
    unnamed x14 -> x12, local copies, waits for them, and re-layouts: 2.21 us -> 1.25 us
    pallas_call x2, Pallas kernels: 5.97 us -> 6.75 us  [the longest x1 4.61 us: per_device(): call(finest_kernel, shape_of(rows_x, rows_y, depth), [scalars] + in_vmem(...]
  transfers between devices with their start and end apart: 6 -> 6, of which waited for: 2 -> 2; matrix products, arithmetic and copies ran while one was open for 0% -> 0% of each run, Pallas kernels for 19% -> 20%
where the time goes in v6:
time: 53 us; the launch traced here: 52.7 us
  starting transfers between devices  19.6 us (37%)
  Pallas kernels  16.3 us (31%)
  waiting for transfers between devices  15.4 us (29%)
  local copies, waits for them, and re-layouts  1.25 us (2%)
    all_to_all x2, waiting for transfers between devices, per_device(): lax.all_to_all(blocks.reshape(exchange_shape), both, 0, 0, tiled=True)  15.4 us
    all_to_all x2, starting transfers between devices, per_device(): lax.all_to_all(blocks.reshape(exchange_shape), both, 0, 0, tiled=True)  12 us
    ppermute x4, starting transfers between devices, shifted(): lax.ppermute(values, axis, [(i, (i + step) % count) for i in range(count)])  7.66 us
    pallas_call x1, Pallas kernels, per_device(): call(finest_kernel, shape_of(rows_x, rows_y, depth), [scalars] + in_vmem(...  4.61 us
    pallas_call x1, Pallas kernels, per_device(): call(restrict_kernel, (shape_of(*block_shape), shape_of(rows_x, 4, depth)...  3.95 us
    pallas_call x1, Pallas kernels, per_device(): call(lambda *refs: convolve_kernel(sections, count_x, count_y, *refs), sh...  2.45 us
    pallas_call x1, Pallas kernels, per_device(): call(edge_kernel, (shape_of(4, rows_y, depth), shape_of(4, rows_y, depth)...  2.13 us
    pallas_call x1, Pallas kernels, per_device(): call(finish_kernel, shape_of(rows_x, rows_y, depth), in_vmem(4), [pltpu.V...  1.7 us
  transfers between devices with their start and end apart: 6, of which 2 were waited for; matrix products, arithmetic and copies ran while one was open for 0% of the time, Pallas kernels for 20%

profile of v6, /device:TPU:1, one launch (start us, length us, event | category | flops | bytes accessed | tf_op | source)
XLA Modules:
  0.0 52.7 jit_solution(1755065794775748644)
XLA Ops:
  0.0 0.0 copy-start.2
  0.0 0.0 copy-start.1
  0.0 3.9 %shard_map.64 = (f32[896,128]{1,0:T(8,128)}, f32[16,4,1024]{2,1,0:T(4,128)}, f32[16,4,1024]{2,1,0:T(4,128)}) custom-call(f32[3,4,9]{2,1,0:T(4,128)} %bitcast.11, f32[16,16,1024]{2,1,0:T(8,128)} %own.3, bf16[128,1152]{1,0:T(8,128)(2,1)} %constant.8.clone.constants_far), custom_call_target="tpu_custom_call" | custom-call | flops 1000000000 | bytes 2000000 | tf_op jit(solution)/shard_map/pallas_call | solution.py:440
  4.0 2.1 %collective-permute-start = (f32[16,4,1024]{2,1,0:T(4,128)}, f32[16,4,1024]{2,1,0:T(4,128)S(1)}, u32[]{:S(2)}, u32[]{:S(2)}) collective-permute-start(f32[16,4,1024]{2,1,0:T(4,128)} %get-tuple-element.12), channel_id=1, source_target_pairs={{0,1},{1,2},{2,3},{3,4},{4,5},{5,6},{6,7},{7,8},{8,9},{9,10},{10,1... | collective-permute-start | bytes 786440 | tf_op jit(solution)/shard_map/ppermute | solution.py:474
  6.1 3.8 %collective-permute-start.1 = (f32[16,4,1024]{2,1,0:T(4,128)}, f32[16,4,1024]{2,1,0:T(4,128)S(1)}, u32[]{:S(2)}, u32[]{:S(2)}) collective-permute-start(f32[16,4,1024]{2,1,0:T(4,128)} %get-tuple-element.13), channel_id=1, source_target_pairs={{0,15},{1,0},{2,1},{3,2},{4,3},{5,4},{6,5},{7,6},{8,7},{9,8},{10,9... | collective-permute-start | bytes 786440 | tf_op jit(solution)/shard_map/ppermute | solution.py:474
  9.9 7.7 %all-to-all-start = ((f32[896,1,128]{2,1,0:T(1,128)}), f32[896,1,128]{2,1,0:T(1,128)S(1)}, u32[]{:S(2)}, u32[]{:S(2)}) async-start(f32[896,1,128]{2,1,0:T(1,128)} %bitcast.15), calls=%async_computation | async-start | bytes 917504 | tf_op jit(solution)/shard_map/all_to_all | solution.py:462
  17.6 0.0 copy-start
  17.6 0.0 collective-permute-done.before.before_y
  17.6 0.0 collective-permute-done.1.after.after_y
  17.6 0.0 copy-done.2
  17.6 0.0 copy-done.1
  17.6 2.1 %shard_map.65 = (f32[4,16,1024]{2,1,0:T(8,128)}, f32[4,16,1024]{2,1,0:T(8,128)}) custom-call(f32[3,4,9]{2,1,0:T(4,128)S(1)} %bitcast.12, f32[16,4,1024]{2,1,0:T(4,128)S(1)} %collective-permute-done.before.before_y, f32[16,16,1024]{2,1,0:T(8,128)S(1)} %copy-done.2, f32[16,4,1024]{2,1,0:T(4,128)S(1)} %collective-permute-done.1.after.after_y), custom_call_target="tpu_custom_call" | custom-call | flops 99999997952 | bytes 3000000 | tf_op jit(solution)/shard_map/pallas_call | solution.py:478
  19.7 1.1 %collective-permute-start.3 = (f32[4,16,1024]{2,1,0:T(8,128)}, f32[4,16,1024]{2,1,0:T(8,128)}, u32[]{:S(2)}, u32[]{:S(2)}) collective-permute-start(f32[4,16,1024]{2,1,0:T(8,128)} %get-tuple-element.16), channel_id=1, source_target_pairs={{0,112},{16,0},{32,16},{48,32},{64,48},{80,64},{96,80},{112,96},{1... | collective-permute-start | bytes 786440 | tf_op jit(solution)/shard_map/ppermute | solution.py:474
  20.8 0.7 %collective-permute-start.2 = (f32[4,16,1024]{2,1,0:T(8,128)}, f32[4,16,1024]{2,1,0:T(8,128)}, u32[]{:S(2)}, u32[]{:S(2)}) collective-permute-start(f32[4,16,1024]{2,1,0:T(8,128)} %get-tuple-element.14), channel_id=1, source_target_pairs={{0,16},{16,32},{32,48},{48,64},{64,80},{80,96},{96,112},{112,0},{1... | collective-permute-start | bytes 786440 | tf_op jit(solution)/shard_map/ppermute | solution.py:474
  21.5 0.0 copy-done
  21.5 1.5 %shard_map.66.refs_1_ = bf16[4992,256]{1,0:T(8,128)(2,1)S(1)} custom-call(f32[3,4,9]{2,1,0:T(4,128)S(1)} %bitcast.13, bf16[1216,128]{1,0:T(8,128)(2,1)S(1)} %copy-done), custom_call_target="tpu_custom_call" | custom-call | flops 20000000 | bytes 3000000 | tf_op jit(solution)/shard_map/pallas_call | solution.py:464
  23.0 7.8 %all-to-all-done = f32[896,1,128]{2,1,0:T(1,128)S(1)} async-done(((f32[896,1,128]{2,1,0:T(1,128)}), f32[896,1,128]{2,1,0:T(1,128)S(1)}, u32[]{:S(2)}, u32[]{:S(2)}) %all-to-all-start) | async-done | bytes 458784 | tf_op jit(solution)/shard_map/all_to_all | solution.py:462
  30.8 2.4 %shard_map.67 = f32[896,128]{1,0:T(8,128)} custom-call(f32[896,128]{1,0:T(8,128)S(1)} %bitcast.9, bf16[4992,256]{1,0:T(8,128)(2,1)S(1)} %shard_map.66.refs_1_), custom_call_target="tpu_custom_call" | custom-call | flops 1000000000 | bytes 4000000 | tf_op jit(solution)/shard_map/pallas_call | solution.py:495
  33.3 0.0 copy-start.4
  33.3 0.0 copy-start.5
  33.3 4.3 %all-to-all-start.1 = ((f32[896,1,128]{2,1,0:T(1,128)}), f32[896,1,128]{2,1,0:T(1,128)S(1)}, u32[]{:S(2)}, u32[]{:S(2)}) async-start(f32[896,1,128]{2,1,0:T(1,128)} %bitcast.5), calls=%async_computation.1 | async-start | bytes 917504 | tf_op jit(solution)/shard_map/all_to_all | solution.py:504
  37.6 0.0 collective-permute-done.3.after
  37.6 0.0 collective-permute-done.2.before
  37.6 0.0 copy-start.3
  37.6 1.2 %copy-done.3 = f32[16,16,1024]{2,1,0:T(8,128)S(1)} copy-done((f32[16,16,1024]{2,1,0:T(8,128)S(1)}, f32[16,16,1024]{2,1,0:T(8,128)}, u32[]{:S(2)}) %copy-start.3) | copy-done | bytes 1048600
  38.9 4.6 %shard_map.68.finest = f32[16,16,1024]{2,1,0:T(8,128)S(1)} custom-call(f32[3,4,9]{2,1,0:T(4,128)S(1)} %bitcast.14, f32[16,4,1024]{2,1,0:T(4,128)S(1)} %collective-permute-done.before.before_y, f32[16,16,1024]{2,1,0:T(8,128)S(1)} %copy-done.3, f32[16,4,1024]{2,1,0:T(4,128)S(1)} %collective-permute-done.1.after.after_y, ...), custom_call_target="tpu_custom_call" | custom-call | flops 99999997952 | bytes 3000000 | tf_op jit(solution)/shard_map/pallas_call | solution.py:486
  43.5 7.5 %all-to-all-done.1 = f32[896,1,128]{2,1,0:T(1,128)S(1)} async-done(((f32[896,1,128]{2,1,0:T(1,128)}), f32[896,1,128]{2,1,0:T(1,128)S(1)}, u32[]{:S(2)}, u32[]{:S(2)}) %all-to-all-start.1) | async-done | bytes 458784 | tf_op jit(solution)/shard_map/all_to_all | solution.py:504
  51.0 0.0 copy-done.4
  51.0 0.0 copy-done.5
  51.0 1.7 %shard_map.69 = f32[16,16,1024]{2,1,0:T(8,128)} custom-call(f32[896,128]{1,0:T(8,128)S(1)} %bitcast.10, bf16[256,512]{1,0:T(8,128)(2,1)S(1)} %copy-done.4, bf16[512,128]{1,0:T(8,128)(2,1)S(1)} %copy-done.5, f32[16,16,1024]{2,1,0:T(8,128)S(1)} %shard_map.68.finest), custom_call_target="tpu_custom_call" | custom-call | flops 1000000000 | bytes 4000000 | tf_op jit(solution)/shard_map/pallas_call | solution.py:506
Async XLA Ops:
  0.0 17.6 %copy-start.2 = (f32[16,16,1024]{2,1,0:T(8,128)S(1)}, f32[16,16,1024]{2,1,0:T(8,128)}, u32[]{:S(2)}) copy-start(f32[16,16,1024]{2,1,0:T(8,128)} %own.3) | copy-start | bytes 3145732
  0.0 17.6 %copy-start.1 = (f32[4,3,9]{2,0,1:T(4,128)S(1)}, f32[4,3,9]{2,0,1:T(4,128)}, u32[]{:S(2)}) copy-start(f32[4,3,9]{2,0,1:T(4,128)} %param.7) | copy-start | bytes 1300
  4.0 13.6 %collective-permute-start = (f32[16,4,1024]{2,1,0:T(4,128)}, f32[16,4,1024]{2,1,0:T(4,128)S(1)}, u32[]{:S(2)}, u32[]{:S(2)}) collective-permute-start(f32[16,4,1024]{2,1,0:T(4,128)} %get-tuple-element.12), channel_id=1, source_target_pairs={{0,1},{1,2},{2,3},{3,4},{4,5},{5,6},{6,7},{7,8},{8,9},{9,10},{10,1... | collective-permute-start | bytes 786440 | tf_op jit(solution)/shard_map/ppermute | solution.py:474
  6.1 11.5 %collective-permute-start.1 = (f32[16,4,1024]{2,1,0:T(4,128)}, f32[16,4,1024]{2,1,0:T(4,128)S(1)}, u32[]{:S(2)}, u32[]{:S(2)}) collective-permute-start(f32[16,4,1024]{2,1,0:T(4,128)} %get-tuple-element.13), channel_id=1, source_target_pairs={{0,15},{1,0},{2,1},{3,2},{4,3},{5,4},{6,5},{7,6},{8,7},{9,8},{10,9... | collective-permute-start | bytes 786440 | tf_op jit(solution)/shard_map/ppermute | solution.py:474
  9.9 20.9 %all-to-all-start = ((f32[896,1,128]{2,1,0:T(1,128)}), f32[896,1,128]{2,1,0:T(1,128)S(1)}, u32[]{:S(2)}, u32[]{:S(2)}) async-start(f32[896,1,128]{2,1,0:T(1,128)} %bitcast.15), calls=%async_computation | async-start | bytes 917504 | tf_op jit(solution)/shard_map/all_to_all | solution.py:462
  17.6 3.9 %copy-start = (bf16[1216,128]{1,0:T(8,128)(2,1)S(1)}, bf16[1216,128]{1,0:T(8,128)(2,1)}, u32[]{:S(2)}) copy-start(bf16[1216,128]{1,0:T(8,128)(2,1)} %constant.11.clone.refs_1_) | copy-start | bytes 933892
  19.7 17.9 %collective-permute-start.3 = (f32[4,16,1024]{2,1,0:T(8,128)}, f32[4,16,1024]{2,1,0:T(8,128)}, u32[]{:S(2)}, u32[]{:S(2)}) collective-permute-start(f32[4,16,1024]{2,1,0:T(8,128)} %get-tuple-element.16), channel_id=1, source_target_pairs={{0,112},{16,0},{32,16},{48,32},{64,48},{80,64},{96,80},{112,96},{1... | collective-permute-start | bytes 786440 | tf_op jit(solution)/shard_map/ppermute | solution.py:474
  20.8 16.8 %collective-permute-start.2 = (f32[4,16,1024]{2,1,0:T(8,128)}, f32[4,16,1024]{2,1,0:T(8,128)}, u32[]{:S(2)}, u32[]{:S(2)}) collective-permute-start(f32[4,16,1024]{2,1,0:T(8,128)} %get-tuple-element.14), channel_id=1, source_target_pairs={{0,16},{16,32},{32,48},{48,64},{64,80},{80,96},{96,112},{112,0},{1... | collective-permute-start | bytes 786440 | tf_op jit(solution)/shard_map/ppermute | solution.py:474
  33.3 17.7 %copy-start.4 = (bf16[256,512]{1,0:T(8,128)(2,1)S(1)}, bf16[256,512]{1,0:T(8,128)(2,1)}, u32[]{:S(2)}) copy-start(bf16[256,512]{1,0:T(8,128)(2,1)} %constant.9.clone.constants) | copy-start | bytes 786436
  33.3 17.7 %copy-start.5 = (bf16[512,128]{1,0:T(8,128)(2,1)S(1)}, bf16[512,128]{1,0:T(8,128)(2,1)}, u32[]{:S(2)}) copy-start(bf16[512,128]{1,0:T(8,128)(2,1)} %constant.10.clone.twice_up) | copy-start | bytes 393220
  33.3 17.7 %all-to-all-start.1 = ((f32[896,1,128]{2,1,0:T(1,128)}), f32[896,1,128]{2,1,0:T(1,128)S(1)}, u32[]{:S(2)}, u32[]{:S(2)}) async-start(f32[896,1,128]{2,1,0:T(1,128)} %bitcast.5), calls=%async_computation.1 | async-start | bytes 917504 | tf_op jit(solution)/shard_map/all_to_all | solution.py:504
  37.6 1.2 %copy-start.3 = (f32[16,16,1024]{2,1,0:T(8,128)S(1)}, f32[16,16,1024]{2,1,0:T(8,128)}, u32[]{:S(2)}) copy-start(f32[16,16,1024]{2,1,0:T(8,128)} %own.3) | copy-start | bytes 3145732

commit v7 on v6

--- a/solution.py
+++ b/solution.py
@@ -154,8 +154,15 @@
     rows_x, rows_y, depth = charges.shape
     columns = rows_x * rows_y
     copies = [
-        pltpu.make_async_copy(constants_far, constants, arrived.at[0]),
+        pltpu.make_async_copy(
+            constants_far.at[:, pl.ds(0, columns)], constants.at[:, pl.ds(0, columns)], arrived.at[0]
+        ),
         pltpu.make_async_copy(taps_far, taps, arrived.at[1]),
+        pltpu.make_async_copy(
+            constants_far.at[:, pl.ds(columns, 896)],
+            constants.at[:, pl.ds(columns, 896)],
+            arrived.at[8 + depth // 256],
+        ),
     ]
     leaving = [
         pltpu.make_async_copy(charges.at[:, pl.ds(0, 4)], head, arrived.at[2]),
@@ -173,6 +180,7 @@
     for chunk in chunks:
         chunk.start()
     copies[1].start()
+    copies[2].start()
     copies[0].wait()
     for index, chunk in enumerate(chunks):
         chunk.wait()
@@ -186,6 +194,7 @@
         copy.start()
     patch[:, 0:lanes] = patch[:, depth : depth + lanes]
     patch[:, depth + lanes : depth + 2 * lanes] = patch[:, lanes : 2 * lanes]
+    copies[2].wait()
     lane_window = constants[:, 256:768]
     row_window = constants[:, 768:1152]
     grid = jnp.concatenate(
@@ -452,7 +461,7 @@
             pltpu.VMEM((2 * lanes, depth + 2 * lanes), jnp.bfloat16),
             pltpu.VMEM((7 * lanes + 48, lanes), jnp.float32),
             pltpu.VMEM(block_shape, jnp.float32),
-            pltpu.SemaphoreType.DMA((8 + depth // 256,)),
+            pltpu.SemaphoreType.DMA((9 + depth // 256,)),
         ],
         (far,) * 3,
         limit=60,

time: 53 us -> 53 us (level)
  no operation moved by 1% of the time
where the time goes in v7:
time: 53 us; the launch traced here: 52.7 us
  starting transfers between devices  19.7 us (37%)
  Pallas kernels  16.3 us (31%)
  waiting for transfers between devices  15.4 us (29%)
  local copies, waits for them, and re-layouts  1.25 us (2%)
    all_to_all x2, waiting for transfers between devices, per_device(): lax.all_to_all(blocks.reshape(exchange_shape), both, 0, 0, tiled=True)  15.4 us
    all_to_all x2, starting transfers between devices, per_device(): lax.all_to_all(blocks.reshape(exchange_shape), both, 0, 0, tiled=True)  12 us
    ppermute x4, starting transfers between devices, shifted(): lax.ppermute(values, axis, [(i, (i + step) % count) for i in range(count)])  7.66 us
    pallas_call x1, Pallas kernels, per_device(): call(finest_kernel, shape_of(rows_x, rows_y, depth), [scalars] + in_vmem(...  4.61 us
    pallas_call x1, Pallas kernels, per_device(): call(restrict_kernel, (shape_of(*block_shape), shape_of(rows_x, 4, depth)...  3.93 us
    pallas_call x1, Pallas kernels, per_device(): call(lambda *refs: convolve_kernel(sections, count_x, count_y, *refs), sh...  2.45 us
    pallas_call x1, Pallas kernels, per_device(): call(edge_kernel, (shape_of(4, rows_y, depth), shape_of(4, rows_y, depth)...  2.13 us
    pallas_call x1, Pallas kernels, per_device(): call(finish_kernel, shape_of(rows_x, rows_y, depth), in_vmem(4), [pltpu.V...  1.7 us
  transfers between devices with their start and end apart: 6, of which 2 were waited for; matrix products, arithmetic and copies ran while one was open for 0% of the time, Pallas kernels for 20%

profile of v7, /device:TPU:1, one launch (start us, length us, event | category | flops | bytes accessed | tf_op | source)
XLA Modules:
  0.0 52.7 jit_solution(7305507254858401516)
XLA Ops:
  0.0 0.0 copy-start.2
  0.0 0.0 copy-start.1
  0.0 3.9 %shard_map.64 = (f32[896,128]{1,0:T(8,128)}, f32[16,4,1024]{2,1,0:T(4,128)}, f32[16,4,1024]{2,1,0:T(4,128)}) custom-call(f32[3,4,9]{2,1,0:T(4,128)} %bitcast.11, f32[16,16,1024]{2,1,0:T(8,128)} %own.3, bf16[128,1152]{1,0:T(8,128)(2,1)} %constant.8.clone.constants_far), custom_call_target="tpu_custom_call" | custom-call | flops 1000000000 | bytes 2000000 | tf_op jit(solution)/shard_map/pallas_call | solution.py:449
  3.9 2.1 %collective-permute-start = (f32[16,4,1024]{2,1,0:T(4,128)}, f32[16,4,1024]{2,1,0:T(4,128)S(1)}, u32[]{:S(2)}, u32[]{:S(2)}) collective-permute-start(f32[16,4,1024]{2,1,0:T(4,128)} %get-tuple-element.12), channel_id=1, source_target_pairs={{0,1},{1,2},{2,3},{3,4},{4,5},{5,6},{6,7},{7,8},{8,9},{9,10},{10,1... | collective-permute-start | bytes 786440 | tf_op jit(solution)/shard_map/ppermute | solution.py:483
  6.1 3.8 %collective-permute-start.1 = (f32[16,4,1024]{2,1,0:T(4,128)}, f32[16,4,1024]{2,1,0:T(4,128)S(1)}, u32[]{:S(2)}, u32[]{:S(2)}) collective-permute-start(f32[16,4,1024]{2,1,0:T(4,128)} %get-tuple-element.13), channel_id=1, source_target_pairs={{0,15},{1,0},{2,1},{3,2},{4,3},{5,4},{6,5},{7,6},{8,7},{9,8},{10,9... | collective-permute-start | bytes 786440 | tf_op jit(solution)/shard_map/ppermute | solution.py:483
  9.9 7.7 %all-to-all-start = ((f32[896,1,128]{2,1,0:T(1,128)}), f32[896,1,128]{2,1,0:T(1,128)S(1)}, u32[]{:S(2)}, u32[]{:S(2)}) async-start(f32[896,1,128]{2,1,0:T(1,128)} %bitcast.15), calls=%async_computation | async-start | bytes 917504 | tf_op jit(solution)/shard_map/all_to_all | solution.py:471
  17.5 0.0 copy-start
  17.6 0.0 collective-permute-done.before.before_y
  17.6 0.0 collective-permute-done.1.after.after_y
  17.6 0.0 copy-done.2
  17.6 0.0 copy-done.1
  17.6 2.1 %shard_map.65 = (f32[4,16,1024]{2,1,0:T(8,128)}, f32[4,16,1024]{2,1,0:T(8,128)}) custom-call(f32[3,4,9]{2,1,0:T(4,128)S(1)} %bitcast.12, f32[16,4,1024]{2,1,0:T(4,128)S(1)} %collective-permute-done.before.before_y, f32[16,16,1024]{2,1,0:T(8,128)S(1)} %copy-done.2, f32[16,4,1024]{2,1,0:T(4,128)S(1)} %collective-permute-done.1.after.after_y), custom_call_target="tpu_custom_call" | custom-call | flops 99999997952 | bytes 3000000 | tf_op jit(solution)/shard_map/pallas_call | solution.py:487
  19.7 1.1 %collective-permute-start.3 = (f32[4,16,1024]{2,1,0:T(8,128)}, f32[4,16,1024]{2,1,0:T(8,128)}, u32[]{:S(2)}, u32[]{:S(2)}) collective-permute-start(f32[4,16,1024]{2,1,0:T(8,128)} %get-tuple-element.16), channel_id=1, source_target_pairs={{0,112},{16,0},{32,16},{48,32},{64,48},{80,64},{96,80},{112,96},{1... | collective-permute-start | bytes 786440 | tf_op jit(solution)/shard_map/ppermute | solution.py:483
  20.8 0.7 %collective-permute-start.2 = (f32[4,16,1024]{2,1,0:T(8,128)}, f32[4,16,1024]{2,1,0:T(8,128)}, u32[]{:S(2)}, u32[]{:S(2)}) collective-permute-start(f32[4,16,1024]{2,1,0:T(8,128)} %get-tuple-element.14), channel_id=1, source_target_pairs={{0,16},{16,32},{32,48},{48,64},{64,80},{80,96},{96,112},{112,0},{1... | collective-permute-start | bytes 786440 | tf_op jit(solution)/shard_map/ppermute | solution.py:483
  21.5 0.0 copy-done
  21.5 1.5 %shard_map.66.refs_1_ = bf16[4992,256]{1,0:T(8,128)(2,1)S(1)} custom-call(f32[3,4,9]{2,1,0:T(4,128)S(1)} %bitcast.13, bf16[1216,128]{1,0:T(8,128)(2,1)S(1)} %copy-done), custom_call_target="tpu_custom_call" | custom-call | flops 20000000 | bytes 3000000 | tf_op jit(solution)/shard_map/pallas_call | solution.py:473
  23.0 7.8 %all-to-all-done = f32[896,1,128]{2,1,0:T(1,128)S(1)} async-done(((f32[896,1,128]{2,1,0:T(1,128)}), f32[896,1,128]{2,1,0:T(1,128)S(1)}, u32[]{:S(2)}, u32[]{:S(2)}) %all-to-all-start) | async-done | bytes 458784 | tf_op jit(solution)/shard_map/all_to_all | solution.py:471
  30.8 2.4 %shard_map.67 = f32[896,128]{1,0:T(8,128)} custom-call(f32[896,128]{1,0:T(8,128)S(1)} %bitcast.9, bf16[4992,256]{1,0:T(8,128)(2,1)S(1)} %shard_map.66.refs_1_), custom_call_target="tpu_custom_call" | custom-call | flops 1000000000 | bytes 4000000 | tf_op jit(solution)/shard_map/pallas_call | solution.py:504
  33.3 0.0 copy-start.4
  33.3 0.0 copy-start.5
  33.3 4.3 %all-to-all-start.1 = ((f32[896,1,128]{2,1,0:T(1,128)}), f32[896,1,128]{2,1,0:T(1,128)S(1)}, u32[]{:S(2)}, u32[]{:S(2)}) async-start(f32[896,1,128]{2,1,0:T(1,128)} %bitcast.5), calls=%async_computation.1 | async-start | bytes 917504 | tf_op jit(solution)/shard_map/all_to_all | solution.py:513
  37.6 0.0 collective-permute-done.3.after
  37.6 0.0 collective-permute-done.2.before
  37.6 0.0 copy-start.3
  37.6 1.2 %copy-done.3 = f32[16,16,1024]{2,1,0:T(8,128)S(1)} copy-done((f32[16,16,1024]{2,1,0:T(8,128)S(1)}, f32[16,16,1024]{2,1,0:T(8,128)}, u32[]{:S(2)}) %copy-start.3) | copy-done | bytes 1048600
  38.8 4.6 %shard_map.68.finest = f32[16,16,1024]{2,1,0:T(8,128)S(1)} custom-call(f32[3,4,9]{2,1,0:T(4,128)S(1)} %bitcast.14, f32[16,4,1024]{2,1,0:T(4,128)S(1)} %collective-permute-done.before.before_y, f32[16,16,1024]{2,1,0:T(8,128)S(1)} %copy-done.3, f32[16,4,1024]{2,1,0:T(4,128)S(1)} %collective-permute-done.1.after.after_y, ...), custom_call_target="tpu_custom_call" | custom-call | flops 99999997952 | bytes 3000000 | tf_op jit(solution)/shard_map/pallas_call | solution.py:495
  43.5 7.5 %all-to-all-done.1 = f32[896,1,128]{2,1,0:T(1,128)S(1)} async-done(((f32[896,1,128]{2,1,0:T(1,128)}), f32[896,1,128]{2,1,0:T(1,128)S(1)}, u32[]{:S(2)}, u32[]{:S(2)}) %all-to-all-start.1) | async-done | bytes 458784 | tf_op jit(solution)/shard_map/all_to_all | solution.py:513
  51.0 0.0 copy-done.4
  51.0 0.0 copy-done.5
  51.0 1.7 %shard_map.69 = f32[16,16,1024]{2,1,0:T(8,128)} custom-call(f32[896,128]{1,0:T(8,128)S(1)} %bitcast.10, bf16[256,512]{1,0:T(8,128)(2,1)S(1)} %copy-done.4, bf16[512,128]{1,0:T(8,128)(2,1)S(1)} %copy-done.5, f32[16,16,1024]{2,1,0:T(8,128)S(1)} %shard_map.68.finest), custom_call_target="tpu_custom_call" | custom-call | flops 1000000000 | bytes 4000000 | tf_op jit(solution)/shard_map/pallas_call | solution.py:515
Async XLA Ops:
  0.0 17.6 %copy-start.2 = (f32[16,16,1024]{2,1,0:T(8,128)S(1)}, f32[16,16,1024]{2,1,0:T(8,128)}, u32[]{:S(2)}) copy-start(f32[16,16,1024]{2,1,0:T(8,128)} %own.3) | copy-start | bytes 3145732
  0.0 17.6 %copy-start.1 = (f32[4,3,9]{2,0,1:T(4,128)S(1)}, f32[4,3,9]{2,0,1:T(4,128)}, u32[]{:S(2)}) copy-start(f32[4,3,9]{2,0,1:T(4,128)} %param.7) | copy-start | bytes 1300
  3.9 13.6 %collective-permute-start = (f32[16,4,1024]{2,1,0:T(4,128)}, f32[16,4,1024]{2,1,0:T(4,128)S(1)}, u32[]{:S(2)}, u32[]{:S(2)}) collective-permute-start(f32[16,4,1024]{2,1,0:T(4,128)} %get-tuple-element.12), channel_id=1, source_target_pairs={{0,1},{1,2},{2,3},{3,4},{4,5},{5,6},{6,7},{7,8},{8,9},{9,10},{10,1... | collective-permute-start | bytes 786440 | tf_op jit(solution)/shard_map/ppermute | solution.py:483
  6.1 11.5 %collective-permute-start.1 = (f32[16,4,1024]{2,1,0:T(4,128)}, f32[16,4,1024]{2,1,0:T(4,128)S(1)}, u32[]{:S(2)}, u32[]{:S(2)}) collective-permute-start(f32[16,4,1024]{2,1,0:T(4,128)} %get-tuple-element.13), channel_id=1, source_target_pairs={{0,15},{1,0},{2,1},{3,2},{4,3},{5,4},{6,5},{7,6},{8,7},{9,8},{10,9... | collective-permute-start | bytes 786440 | tf_op jit(solution)/shard_map/ppermute | solution.py:483
  9.9 21.0 %all-to-all-start = ((f32[896,1,128]{2,1,0:T(1,128)}), f32[896,1,128]{2,1,0:T(1,128)S(1)}, u32[]{:S(2)}, u32[]{:S(2)}) async-start(f32[896,1,128]{2,1,0:T(1,128)} %bitcast.15), calls=%async_computation | async-start | bytes 917504 | tf_op jit(solution)/shard_map/all_to_all | solution.py:471
  17.5 3.9 %copy-start = (bf16[1216,128]{1,0:T(8,128)(2,1)S(1)}, bf16[1216,128]{1,0:T(8,128)(2,1)}, u32[]{:S(2)}) copy-start(bf16[1216,128]{1,0:T(8,128)(2,1)} %constant.11.clone.refs_1_) | copy-start | bytes 933892
  19.7 17.9 %collective-permute-start.3 = (f32[4,16,1024]{2,1,0:T(8,128)}, f32[4,16,1024]{2,1,0:T(8,128)}, u32[]{:S(2)}, u32[]{:S(2)}) collective-permute-start(f32[4,16,1024]{2,1,0:T(8,128)} %get-tuple-element.16), channel_id=1, source_target_pairs={{0,112},{16,0},{32,16},{48,32},{64,48},{80,64},{96,80},{112,96},{1... | collective-permute-start | bytes 786440 | tf_op jit(solution)/shard_map/ppermute | solution.py:483
  20.8 16.8 %collective-permute-start.2 = (f32[4,16,1024]{2,1,0:T(8,128)}, f32[4,16,1024]{2,1,0:T(8,128)}, u32[]{:S(2)}, u32[]{:S(2)}) collective-permute-start(f32[4,16,1024]{2,1,0:T(8,128)} %get-tuple-element.14), channel_id=1, source_target_pairs={{0,16},{16,32},{32,48},{48,64},{64,80},{80,96},{96,112},{112,0},{1... | collective-permute-start | bytes 786440 | tf_op jit(solution)/shard_map/ppermute | solution.py:483
  33.3 17.7 %copy-start.4 = (bf16[256,512]{1,0:T(8,128)(2,1)S(1)}, bf16[256,512]{1,0:T(8,128)(2,1)}, u32[]{:S(2)}) copy-start(bf16[256,512]{1,0:T(8,128)(2,1)} %constant.9.clone.constants) | copy-start | bytes 786436
  33.3 17.7 %copy-start.5 = (bf16[512,128]{1,0:T(8,128)(2,1)S(1)}, bf16[512,128]{1,0:T(8,128)(2,1)}, u32[]{:S(2)}) copy-start(bf16[512,128]{1,0:T(8,128)(2,1)} %constant.10.clone.twice_up) | copy-start | bytes 393220
  33.3 17.7 %all-to-all-start.1 = ((f32[896,1,128]{2,1,0:T(1,128)}), f32[896,1,128]{2,1,0:T(1,128)S(1)}, u32[]{:S(2)}, u32[]{:S(2)}) async-start(f32[896,1,128]{2,1,0:T(1,128)} %bitcast.5), calls=%async_computation.1 | async-start | bytes 917504 | tf_op jit(solution)/shard_map/all_to_all | solution.py:513
  37.6 1.2 %copy-start.3 = (f32[16,16,1024]{2,1,0:T(8,128)S(1)}, f32[16,16,1024]{2,1,0:T(8,128)}, u32[]{:S(2)}) copy-start(f32[16,16,1024]{2,1,0:T(8,128)} %own.3) | copy-start | bytes 3145732

commit v8 on v6

--- a/solution.py
+++ b/solution.py
@@ -335,10 +335,13 @@
     )
     running = parts[1] + middle + coarsest
     pairs = wrapped(side_by_side(running), 64, 0)
+    fines = [
+        side_by_side(both_ways(dot(row_window, pairs[lanes * index : lanes * index + 256])))
+        for index in range(depth // 256)
+    ]
     copies = []
-    for index in range(depth // 256):
-        fine = both_ways(dot(row_window, pairs[lanes * index : lanes * index + 256]))
-        smooth = dot_lanes(constants[:, 0:256], side_by_side(fine))
+    for index, fine in enumerate(fines):
+        smooth = dot_lanes(constants[:, 0:256], fine)
         section = slice(256 * index, 256 * (index + 1))
         ready[:, :, section] = finest[:, :, section] + smooth.reshape(rows_x, rows_y, 256)
         places = pl.ds(256 * index, 256)

time: 53 us -> 53 us (level)
  no operation moved by 1% of the time
where the time goes in v8:
time: 53 us; the launch traced here: 52.7 us
  starting transfers between devices  19.6 us (37%)
  Pallas kernels  16.3 us (31%)
  waiting for transfers between devices  15.4 us (29%)
  local copies, waits for them, and re-layouts  1.25 us (2%)
    all_to_all x2, waiting for transfers between devices, per_device(): lax.all_to_all(blocks.reshape(exchange_shape), both, 0, 0, tiled=True)  15.4 us
    all_to_all x2, starting transfers between devices, per_device(): lax.all_to_all(blocks.reshape(exchange_shape), both, 0, 0, tiled=True)  12 us
    ppermute x4, starting transfers between devices, shifted(): lax.ppermute(values, axis, [(i, (i + step) % count) for i in range(count)])  7.66 us
    pallas_call x1, Pallas kernels, per_device(): call(finest_kernel, shape_of(rows_x, rows_y, depth), [scalars] + in_vmem(...  4.61 us
    pallas_call x1, Pallas kernels, per_device(): call(restrict_kernel, (shape_of(*block_shape), shape_of(rows_x, 4, depth)...  3.95 us
    pallas_call x1, Pallas kernels, per_device(): call(lambda *refs: convolve_kernel(sections, count_x, count_y, *refs), sh...  2.45 us
    pallas_call x1, Pallas kernels, per_device(): call(edge_kernel, (shape_of(4, rows_y, depth), shape_of(4, rows_y, depth)...  2.13 us
    pallas_call x1, Pallas kernels, per_device(): call(finish_kernel, shape_of(rows_x, rows_y, depth), in_vmem(4), [pltpu.V...  1.71 us
  transfers between devices with their start and end apart: 6, of which 2 were waited for; matrix products, arithmetic and copies ran while one was open for 0% of the time, Pallas kernels for 20%

profile of v8, /device:TPU:1, one launch (start us, length us, event | category | flops | bytes accessed | tf_op | source)
XLA Modules:
  0.0 52.7 jit_solution(12115750429316805837)
XLA Ops:
  0.0 0.0 copy-start.2
  0.0 0.0 copy-start.1
  0.0 3.9 %shard_map.64 = (f32[896,128]{1,0:T(8,128)}, f32[16,4,1024]{2,1,0:T(4,128)}, f32[16,4,1024]{2,1,0:T(4,128)}) custom-call(f32[3,4,9]{2,1,0:T(4,128)} %bitcast.11, f32[16,16,1024]{2,1,0:T(8,128)} %own.3, bf16[128,1152]{1,0:T(8,128)(2,1)} %constant.8.clone.constants_far), custom_call_target="tpu_custom_call" | custom-call | flops 1000000000 | bytes 2000000 | tf_op jit(solution)/shard_map/pallas_call | solution.py:443
  4.0 2.1 %collective-permute-start = (f32[16,4,1024]{2,1,0:T(4,128)}, f32[16,4,1024]{2,1,0:T(4,128)S(1)}, u32[]{:S(2)}, u32[]{:S(2)}) collective-permute-start(f32[16,4,1024]{2,1,0:T(4,128)} %get-tuple-element.12), channel_id=1, source_target_pairs={{0,1},{1,2},{2,3},{3,4},{4,5},{5,6},{6,7},{7,8},{8,9},{9,10},{10,1... | collective-permute-start | bytes 786440 | tf_op jit(solution)/shard_map/ppermute | solution.py:477
  6.1 3.8 %collective-permute-start.1 = (f32[16,4,1024]{2,1,0:T(4,128)}, f32[16,4,1024]{2,1,0:T(4,128)S(1)}, u32[]{:S(2)}, u32[]{:S(2)}) collective-permute-start(f32[16,4,1024]{2,1,0:T(4,128)} %get-tuple-element.13), channel_id=1, source_target_pairs={{0,15},{1,0},{2,1},{3,2},{4,3},{5,4},{6,5},{7,6},{8,7},{9,8},{10,9... | collective-permute-start | bytes 786440 | tf_op jit(solution)/shard_map/ppermute | solution.py:477
  9.9 7.7 %all-to-all-start = ((f32[896,1,128]{2,1,0:T(1,128)}), f32[896,1,128]{2,1,0:T(1,128)S(1)}, u32[]{:S(2)}, u32[]{:S(2)}) async-start(f32[896,1,128]{2,1,0:T(1,128)} %bitcast.15), calls=%async_computation | async-start | bytes 917504 | tf_op jit(solution)/shard_map/all_to_all | solution.py:465
  17.6 0.0 copy-start
  17.6 0.0 collective-permute-done.before.before_y
  17.6 0.0 collective-permute-done.1.after.after_y
  17.6 0.0 copy-done.2
  17.6 0.0 copy-done.1
  17.6 2.1 %shard_map.65 = (f32[4,16,1024]{2,1,0:T(8,128)}, f32[4,16,1024]{2,1,0:T(8,128)}) custom-call(f32[3,4,9]{2,1,0:T(4,128)S(1)} %bitcast.12, f32[16,4,1024]{2,1,0:T(4,128)S(1)} %collective-permute-done.before.before_y, f32[16,16,1024]{2,1,0:T(8,128)S(1)} %copy-done.2, f32[16,4,1024]{2,1,0:T(4,128)S(1)} %collective-permute-done.1.after.after_y), custom_call_target="tpu_custom_call" | custom-call | flops 99999997952 | bytes 3000000 | tf_op jit(solution)/shard_map/pallas_call | solution.py:481
  19.7 1.1 %collective-permute-start.3 = (f32[4,16,1024]{2,1,0:T(8,128)}, f32[4,16,1024]{2,1,0:T(8,128)}, u32[]{:S(2)}, u32[]{:S(2)}) collective-permute-start(f32[4,16,1024]{2,1,0:T(8,128)} %get-tuple-element.16), channel_id=1, source_target_pairs={{0,112},{16,0},{32,16},{48,32},{64,48},{80,64},{96,80},{112,96},{1... | collective-permute-start | bytes 786440 | tf_op jit(solution)/shard_map/ppermute | solution.py:477
  20.8 0.7 %collective-permute-start.2 = (f32[4,16,1024]{2,1,0:T(8,128)}, f32[4,16,1024]{2,1,0:T(8,128)}, u32[]{:S(2)}, u32[]{:S(2)}) collective-permute-start(f32[4,16,1024]{2,1,0:T(8,128)} %get-tuple-element.14), channel_id=1, source_target_pairs={{0,16},{16,32},{32,48},{48,64},{64,80},{80,96},{96,112},{112,0},{1... | collective-permute-start | bytes 786440 | tf_op jit(solution)/shard_map/ppermute | solution.py:477
  21.5 0.0 copy-done
  21.5 1.5 %shard_map.66.refs_1_ = bf16[4992,256]{1,0:T(8,128)(2,1)S(1)} custom-call(f32[3,4,9]{2,1,0:T(4,128)S(1)} %bitcast.13, bf16[1216,128]{1,0:T(8,128)(2,1)S(1)} %copy-done), custom_call_target="tpu_custom_call" | custom-call | flops 20000000 | bytes 3000000 | tf_op jit(solution)/shard_map/pallas_call | solution.py:467
  23.0 7.8 %all-to-all-done = f32[896,1,128]{2,1,0:T(1,128)S(1)} async-done(((f32[896,1,128]{2,1,0:T(1,128)}), f32[896,1,128]{2,1,0:T(1,128)S(1)}, u32[]{:S(2)}, u32[]{:S(2)}) %all-to-all-start) | async-done | bytes 458784 | tf_op jit(solution)/shard_map/all_to_all | solution.py:465
  30.8 2.4 %shard_map.67 = f32[896,128]{1,0:T(8,128)} custom-call(f32[896,128]{1,0:T(8,128)S(1)} %bitcast.9, bf16[4992,256]{1,0:T(8,128)(2,1)S(1)} %shard_map.66.refs_1_), custom_call_target="tpu_custom_call" | custom-call | flops 1000000000 | bytes 4000000 | tf_op jit(solution)/shard_map/pallas_call | solution.py:498
  33.3 0.0 copy-start.4
  33.3 0.0 copy-start.5
  33.3 4.3 %all-to-all-start.1 = ((f32[896,1,128]{2,1,0:T(1,128)}), f32[896,1,128]{2,1,0:T(1,128)S(1)}, u32[]{:S(2)}, u32[]{:S(2)}) async-start(f32[896,1,128]{2,1,0:T(1,128)} %bitcast.5), calls=%async_computation.1 | async-start | bytes 917504 | tf_op jit(solution)/shard_map/all_to_all | solution.py:507
  37.6 0.0 collective-permute-done.3.after
  37.6 0.0 collective-permute-done.2.before
  37.6 0.0 copy-start.3
  37.6 1.2 %copy-done.3 = f32[16,16,1024]{2,1,0:T(8,128)S(1)} copy-done((f32[16,16,1024]{2,1,0:T(8,128)S(1)}, f32[16,16,1024]{2,1,0:T(8,128)}, u32[]{:S(2)}) %copy-start.3) | copy-done | bytes 1048600
  38.9 4.6 %shard_map.68.finest = f32[16,16,1024]{2,1,0:T(8,128)S(1)} custom-call(f32[3,4,9]{2,1,0:T(4,128)S(1)} %bitcast.14, f32[16,4,1024]{2,1,0:T(4,128)S(1)} %collective-permute-done.before.before_y, f32[16,16,1024]{2,1,0:T(8,128)S(1)} %copy-done.3, f32[16,4,1024]{2,1,0:T(4,128)S(1)} %collective-permute-done.1.after.after_y, ...), custom_call_target="tpu_custom_call" | custom-call | flops 99999997952 | bytes 3000000 | tf_op jit(solution)/shard_map/pallas_call | solution.py:489
  43.5 7.5 %all-to-all-done.1 = f32[896,1,128]{2,1,0:T(1,128)S(1)} async-done(((f32[896,1,128]{2,1,0:T(1,128)}), f32[896,1,128]{2,1,0:T(1,128)S(1)}, u32[]{:S(2)}, u32[]{:S(2)}) %all-to-all-start.1) | async-done | bytes 458784 | tf_op jit(solution)/shard_map/all_to_all | solution.py:507
  51.0 0.0 copy-done.4
  51.0 0.0 copy-done.5
  51.0 1.7 %shard_map.69 = f32[16,16,1024]{2,1,0:T(8,128)} custom-call(f32[896,128]{1,0:T(8,128)S(1)} %bitcast.10, bf16[256,512]{1,0:T(8,128)(2,1)S(1)} %copy-done.4, bf16[512,128]{1,0:T(8,128)(2,1)S(1)} %copy-done.5, f32[16,16,1024]{2,1,0:T(8,128)S(1)} %shard_map.68.finest), custom_call_target="tpu_custom_call" | custom-call | flops 1000000000 | bytes 4000000 | tf_op jit(solution)/shard_map/pallas_call | solution.py:509
Async XLA Ops:
  0.0 17.6 %copy-start.2 = (f32[16,16,1024]{2,1,0:T(8,128)S(1)}, f32[16,16,1024]{2,1,0:T(8,128)}, u32[]{:S(2)}) copy-start(f32[16,16,1024]{2,1,0:T(8,128)} %own.3) | copy-start | bytes 3145732
  0.0 17.6 %copy-start.1 = (f32[4,3,9]{2,0,1:T(4,128)S(1)}, f32[4,3,9]{2,0,1:T(4,128)}, u32[]{:S(2)}) copy-start(f32[4,3,9]{2,0,1:T(4,128)} %param.7) | copy-start | bytes 1300
  4.0 13.6 %collective-permute-start = (f32[16,4,1024]{2,1,0:T(4,128)}, f32[16,4,1024]{2,1,0:T(4,128)S(1)}, u32[]{:S(2)}, u32[]{:S(2)}) collective-permute-start(f32[16,4,1024]{2,1,0:T(4,128)} %get-tuple-element.12), channel_id=1, source_target_pairs={{0,1},{1,2},{2,3},{3,4},{4,5},{5,6},{6,7},{7,8},{8,9},{9,10},{10,1... | collective-permute-start | bytes 786440 | tf_op jit(solution)/shard_map/ppermute | solution.py:477
  6.1 11.5 %collective-permute-start.1 = (f32[16,4,1024]{2,1,0:T(4,128)}, f32[16,4,1024]{2,1,0:T(4,128)S(1)}, u32[]{:S(2)}, u32[]{:S(2)}) collective-permute-start(f32[16,4,1024]{2,1,0:T(4,128)} %get-tuple-element.13), channel_id=1, source_target_pairs={{0,15},{1,0},{2,1},{3,2},{4,3},{5,4},{6,5},{7,6},{8,7},{9,8},{10,9... | collective-permute-start | bytes 786440 | tf_op jit(solution)/shard_map/ppermute | solution.py:477
  9.9 20.9 %all-to-all-start = ((f32[896,1,128]{2,1,0:T(1,128)}), f32[896,1,128]{2,1,0:T(1,128)S(1)}, u32[]{:S(2)}, u32[]{:S(2)}) async-start(f32[896,1,128]{2,1,0:T(1,128)} %bitcast.15), calls=%async_computation | async-start | bytes 917504 | tf_op jit(solution)/shard_map/all_to_all | solution.py:465
  17.6 3.9 %copy-start = (bf16[1216,128]{1,0:T(8,128)(2,1)S(1)}, bf16[1216,128]{1,0:T(8,128)(2,1)}, u32[]{:S(2)}) copy-start(bf16[1216,128]{1,0:T(8,128)(2,1)} %constant.11.clone.refs_1_) | copy-start | bytes 933892
  19.7 17.9 %collective-permute-start.3 = (f32[4,16,1024]{2,1,0:T(8,128)}, f32[4,16,1024]{2,1,0:T(8,128)}, u32[]{:S(2)}, u32[]{:S(2)}) collective-permute-start(f32[4,16,1024]{2,1,0:T(8,128)} %get-tuple-element.16), channel_id=1, source_target_pairs={{0,112},{16,0},{32,16},{48,32},{64,48},{80,64},{96,80},{112,96},{1... | collective-permute-start | bytes 786440 | tf_op jit(solution)/shard_map/ppermute | solution.py:477
  20.8 16.8 %collective-permute-start.2 = (f32[4,16,1024]{2,1,0:T(8,128)}, f32[4,16,1024]{2,1,0:T(8,128)}, u32[]{:S(2)}, u32[]{:S(2)}) collective-permute-start(f32[4,16,1024]{2,1,0:T(8,128)} %get-tuple-element.14), channel_id=1, source_target_pairs={{0,16},{16,32},{32,48},{48,64},{64,80},{80,96},{96,112},{112,0},{1... | collective-permute-start | bytes 786440 | tf_op jit(solution)/shard_map/ppermute | solution.py:477
  33.3 17.7 %copy-start.4 = (bf16[256,512]{1,0:T(8,128)(2,1)S(1)}, bf16[256,512]{1,0:T(8,128)(2,1)}, u32[]{:S(2)}) copy-start(bf16[256,512]{1,0:T(8,128)(2,1)} %constant.9.clone.constants) | copy-start | bytes 786436
  33.3 17.7 %copy-start.5 = (bf16[512,128]{1,0:T(8,128)(2,1)S(1)}, bf16[512,128]{1,0:T(8,128)(2,1)}, u32[]{:S(2)}) copy-start(bf16[512,128]{1,0:T(8,128)(2,1)} %constant.10.clone.twice_up) | copy-start | bytes 393220
  33.3 17.7 %all-to-all-start.1 = ((f32[896,1,128]{2,1,0:T(1,128)}), f32[896,1,128]{2,1,0:T(1,128)S(1)}, u32[]{:S(2)}, u32[]{:S(2)}) async-start(f32[896,1,128]{2,1,0:T(1,128)} %bitcast.5), calls=%async_computation.1 | async-start | bytes 917504 | tf_op jit(solution)/shard_map/all_to_all | solution.py:507
  37.6 1.2 %copy-start.3 = (f32[16,16,1024]{2,1,0:T(8,128)S(1)}, f32[16,16,1024]{2,1,0:T(8,128)}, u32[]{:S(2)}) copy-start(f32[16,16,1024]{2,1,0:T(8,128)} %own.3) | copy-start | bytes 3145732
